TPU v7x, 32 devices: a whole 2x2x4 slice. The times are simulated.
32 devices in a mesh: dp: 8 (over y, x, core), head: 4 (over z).
Axes of the slice: x: 2, y: 2, z: 4, core: 2. Of those that a mesh axis runs over, the one named last changes fastest.
Arguments:
- char_ids: int32 [16, 1024, 16], P('dp', 'head'), may hold values from 0 to 255
- char_counts: int32 [16, 1024], P('dp', 'head'), may hold values from 1 to 16
- language: int32 [16], P('dp'), may hold values from 0 to 3
- words_in: bfloat16 [16, 1024, 512], P('dp', 'head'), may hold values from -6 to 6
- out_cotangent: bfloat16 [16, 1024, 512], P('dp', 'head'), may hold values from -6 to 6
- char_table: float32 [1024, 256], P('dp', 'head'), may hold values from -0.6 to 0.6
- char_in: float32 [256, 2560], P('dp', 'head'), may hold values from -1.06066017 to 1.06066017
- char_down: float32 [1024, 256], P('dp', 'head'), may hold values from -0.1875 to 0.1875
- word_in: float32 [512, 4096], P('dp', 'head'), may hold values from -1.5 to 1.5
- word_down: float32 [2048, 512], P('dp', 'head'), may hold values from -0.125 to 0.125
- norm_gains: float32 [1536], replicated, may hold values from 0.4 to 3
- old_table_first: float32 [1024, 256], P('dp', 'head'), may hold values from -0.0029296875 to 0.0029296875
- old_table_second: float32 [1024, 256], P('dp', 'head'), may hold values from 2.311117e-07 to 9.244468e-07
- old_char_in_first: float32 [256, 2560], P('dp', 'head'), may hold values from -0.0029296875 to 0.0029296875
- old_char_in_second: float32 [256, 2560], P('dp', 'head'), may hold values from 2.311117e-07 to 9.244468e-07
- old_char_down_first: float32 [1024, 256], P('dp', 'head'), may hold values from -0.0029296875 to 0.0029296875
- old_char_down_second: float32 [1024, 256], P('dp', 'head'), may hold values from 2.311117e-07 to 9.244468e-07
- old_word_in_first: float32 [512, 4096], P('dp', 'head'), may hold values from -0.0029296875 to 0.0029296875
- old_word_in_second: float32 [512, 4096], P('dp', 'head'), may hold values from 2.311117e-07 to 9.244468e-07
- old_word_down_first: float32 [2048, 512], P('dp', 'head'), may hold values from -0.0029296875 to 0.0029296875
- old_word_down_second: float32 [2048, 512], P('dp', 'head'), may hold values from 2.311117e-07 to 9.244468e-07
- old_gains_first: float32 [1536], replicated, may hold values from -0.01171875 to 0.01171875
- old_gains_second: float32 [1536], replicated, may hold values from 3.6977872e-06 to 1.4791149e-05
Outputs:
- output: bfloat16 [16, 1024, 512], P('dp', 'head')
- input_grad: float32 [16, 1024, 512], P('dp', 'head')
- grad_norm: float32 [], replicated
- table_grad: float32 [1024, 256], P('dp', 'head')
- table_first: float32 [1024, 256], P('dp', 'head')
- table_second: float32 [1024, 256], P('dp', 'head')
- table_new: float32 [1024, 256], P('dp', 'head')
- table_copy: bfloat16 [1024, 256], P('dp', 'head')
- char_in_grad: float32 [256, 2560], P('dp', 'head')
- char_in_first: float32 [256, 2560], P('dp', 'head')
- char_in_second: float32 [256, 2560], P('dp', 'head')
- char_in_new: float32 [256, 2560], P('dp', 'head')
- char_in_copy: bfloat16 [256, 2560], P('dp', 'head')
- char_down_grad: float32 [1024, 256], P('dp', 'head')
- char_down_first: float32 [1024, 256], P('dp', 'head')
- char_down_second: float32 [1024, 256], P('dp', 'head')
- char_down_new: float32 [1024, 256], P('dp', 'head')
- char_down_copy: bfloat16 [1024, 256], P('dp', 'head')
- word_in_grad: float32 [512, 4096], P('dp', 'head')
- word_in_first: float32 [512, 4096], P('dp', 'head')
- word_in_second: float32 [512, 4096], P('dp', 'head')
- word_in_new: float32 [512, 4096], P('dp', 'head')
- word_in_copy: bfloat16 [512, 4096], P('dp', 'head')
- word_down_grad: float32 [2048, 512], P('dp', 'head')
- word_down_first: float32 [2048, 512], P('dp', 'head')
- word_down_second: float32 [2048, 512], P('dp', 'head')
- word_down_new: float32 [2048, 512], P('dp', 'head')
- word_down_copy: bfloat16 [2048, 512], P('dp', 'head')
- gains_grad: float32 [1536], replicated
- gains_first: float32 [1536], replicated
- gains_second: float32 [1536], replicated
- gains_new: float32 [1536], replicated
- gains_copy: bfloat16 [1536], replicated
Inputs may be any that keep to these rules, and one draw needn't show every extreme that they name: `char_counts`: the number of real characters of each word; slots at and past it are padding.
All inputs are finite; a program needn't handle non-finite values.
Results may differ from a plain program's by a relative error of at most 0.015.
The roundings to bfloat16 on the way count: a program that leaves them out, or rounds other values in their place, can miss the bound.
Values may be sent and summed in bfloat16 or wider, within the bound.
A program may use at most 320 MiB of HBM per device.

v0:
```python
import jax
import jax.numpy as jnp
from jax import lax
from jax.sharding import PartitionSpec as P

D = 512
HEADS = 8
CD = 256
CHEADS = 4
CFF = 1024
CV = 256
STEP = 5


EPS = 1e-05
CLIP = 1.0
MATRIX_RATE = 0.03
GAIN_RATE = 0.25
MATRIX_DECAY = 0.1
BETA_ONE = 0.5
BETA_TWO = 0.5
ADAM_EPS = 1e-08
NEG_FILL = -1e30
SQRT_HALF = 0.7071067811865476
INV_ROOT_TWO_PI = 0.3989422804014327


def matmul(left_side, right_side):
    return jnp.dot(left_side, right_side, preferred_element_type=jnp.float32)


def matmul_tn(left_side, right_side):
    return lax.dot_general(
        left_side, right_side, (((0,), (0,)), ((), ())), preferred_element_type=jnp.float32
    )


def matmul_nt(left_side, right_side):
    return lax.dot_general(
        left_side, right_side, (((1,), (1,)), ((), ())), preferred_element_type=jnp.float32
    )


def gelu_value(upper_in):
    return upper_in * 0.5 * (1.0 + lax.erf(upper_in * SQRT_HALF))


def gelu_slope(upper_in):
    return (
        0.5 * (1.0 + lax.erf(upper_in * SQRT_HALF))
        + upper_in * jnp.exp(-0.5 * upper_in * upper_in) * INV_ROOT_TWO_PI
    )


def rms_forward(values, gain_vec):
    inverse = lax.rsqrt(jnp.mean(values * values, axis=-1, keepdims=True) + EPS)
    normed = values * inverse
    return (normed * gain_vec, normed, inverse)


def rms_backward(grad_in, gain_vec, normed, inverse):
    grad_gain = jnp.sum(grad_in * normed, axis=0)
    scaled = grad_in * gain_vec
    grad_values = inverse * (scaled - normed * jnp.mean(scaled * normed, axis=-1, keepdims=True))
    return (grad_values, grad_gain)


def causal_mask(length):
    row_pos = lax.broadcasted_iota(jnp.int32, (length, length), 0)
    col_pos = lax.broadcasted_iota(jnp.int32, (length, length), 1)
    return (row_pos >= col_pos)[None, None]


def score_block(queries, key_rows, allowed):
    factor = queries.shape[-1] ** (-0.5)
    scores = (
        jnp.einsum("bqhd,bkhd->bhqk", queries, key_rows, preferred_element_type=jnp.float32)
        * factor
    )
    return (jnp.where(allowed, scores, NEG_FILL), factor)


def attend_forward(queries, key_rows, value_rows, allowed):
    scores, factor = score_block(queries, key_rows, allowed)
    highest = jnp.max(scores, axis=-1, keepdims=True)
    powers = jnp.exp(scores - highest)
    totals = jnp.sum(powers, axis=-1, keepdims=True)
    weights_low = (powers / totals).astype(jnp.bfloat16)
    mixed = jnp.einsum(
        "bhqk,bkhd->bqhd", weights_low, value_rows, preferred_element_type=jnp.float32
    )
    return (mixed.astype(jnp.bfloat16), highest + jnp.log(totals))


def attend_backward(queries, key_rows, value_rows, allowed, log_total, grad_mixed):
    scores, factor = score_block(queries, key_rows, allowed)
    weights_soft = jnp.exp(scores - log_total)
    grad_weights = jnp.einsum(
        "bqhd,bkhd->bhqk", grad_mixed, value_rows, preferred_element_type=jnp.float32
    )
    grad_values = jnp.einsum(
        "bhqk,bqhd->bkhd",
        weights_soft.astype(jnp.bfloat16),
        grad_mixed,
        preferred_element_type=jnp.float32,
    )
    grad_scores = weights_soft * (
        grad_weights - jnp.sum(grad_weights * weights_soft, axis=-1, keepdims=True)
    )
    grad_raw = (grad_scores * factor).astype(jnp.bfloat16)
    grad_queries = jnp.einsum(
        "bhqk,bkhd->bqhd", grad_raw, key_rows, preferred_element_type=jnp.float32
    )
    grad_keys = jnp.einsum("bhqk,bqhd->bkhd", grad_raw, queries, preferred_element_type=jnp.float32)
    return jnp.stack([grad_queries, grad_keys, grad_values], axis=2)


def char_forward(
    char_ids, char_counts, language, table_low, char_in_low, char_down_low, gain_one, gain_two
):
    seq_count, local_words, char_count = char_ids.shape
    word_total = seq_count * local_words
    row_total = word_total * char_count
    table_rows = table_low.shape[0]
    head_size = CD // CHEADS
    index = (char_ids + CV * language[:, None, None]).reshape(row_total, 1)
    one_hot = (index == lax.broadcasted_iota(jnp.int32, (1, table_rows), 1)).astype(jnp.bfloat16)
    embedded = matmul(one_hot, table_low)
    scaled_one, normed_one, inverse_one = rms_forward(embedded, gain_one)
    act_one = scaled_one.astype(jnp.bfloat16)
    char_triple = matmul(act_one, char_in_low[:, : 3 * CD]).astype(jnp.bfloat16)
    char_triple = char_triple.reshape(word_total, char_count, 3, CHEADS, head_size)
    counts_flat = char_counts.reshape(word_total, 1)
    key_mask = lax.broadcasted_iota(jnp.int32, (1, char_count), 1) < counts_flat
    char_mixed, char_lse = attend_forward(
        char_triple[:, :, 0], char_triple[:, :, 1], char_triple[:, :, 2], key_mask[:, None, None, :]
    )
    mixed_flat = char_mixed.reshape(row_total, CD)
    char_first = embedded + matmul(mixed_flat, char_in_low[:, 3 * CD : 4 * CD])
    scaled_two, normed_two, inverse_two = rms_forward(char_first, gain_two)
    act_two = scaled_two.astype(jnp.bfloat16)
    char_upper = matmul(act_two, char_in_low[:, 4 * CD : 4 * CD + CFF])
    char_hidden = gelu_value(char_upper).astype(jnp.bfloat16)
    char_second = char_first + matmul(char_hidden, char_down_low)
    kept_rows = jnp.where(
        key_mask[:, :, None], char_second.reshape(word_total, char_count, CD), 0.0
    )
    pooled = (jnp.sum(kept_rows, axis=1) / counts_flat.astype(jnp.float32)).astype(jnp.bfloat16)
    return {
        "one_hot": one_hot,
        "act_one": act_one,
        "char_triple": char_triple,
        "key_mask": key_mask,
        "char_lse": char_lse,
        "mixed_flat": mixed_flat,
        "normed_one": normed_one,
        "inverse_one": inverse_one,
        "normed_two": normed_two,
        "inverse_two": inverse_two,
        "act_two": act_two,
        "char_upper": char_upper,
        "char_hidden": char_hidden,
        "pooled": pooled,
    }


def char_backward(state, grad_pooled, char_counts, char_in_low, char_down_low, gain_one, gain_two):
    word_total = grad_pooled.shape[0]
    char_count = state["key_mask"].shape[1]
    row_total = word_total * char_count
    head_size = CD // CHEADS
    counts_flat = char_counts.reshape(word_total, 1).astype(jnp.float32)
    spread = jnp.where(state["key_mask"][:, :, None], (grad_pooled / counts_flat)[:, None, :], 0.0)
    grad_second = spread.reshape(row_total, CD)
    grad_branch = grad_second.astype(jnp.bfloat16)
    grad_down = matmul_tn(state["char_hidden"], grad_branch)
    grad_hidden = matmul_nt(grad_branch, char_down_low)
    grad_upper = (grad_hidden * gelu_slope(state["char_upper"])).astype(jnp.bfloat16)
    grad_up = matmul_tn(state["act_two"], grad_upper)
    grad_act_two = matmul_nt(grad_upper, char_in_low[:, 4 * CD : 4 * CD + CFF])
    back_two, grad_gain_two = rms_backward(
        grad_act_two, gain_two, state["normed_two"], state["inverse_two"]
    )
    grad_first = grad_second + back_two
    grad_attn_in = grad_first.astype(jnp.bfloat16)
    grad_out_proj = matmul_tn(state["mixed_flat"], grad_attn_in)
    grad_mixed = matmul_nt(grad_attn_in, char_in_low[:, 3 * CD : 4 * CD]).astype(jnp.bfloat16)
    grad_mixed = grad_mixed.reshape(word_total, char_count, CHEADS, head_size)
    triple = state["char_triple"]
    grad_triple = attend_backward(
        triple[:, :, 0],
        triple[:, :, 1],
        triple[:, :, 2],
        state["key_mask"][:, None, None, :],
        state["char_lse"],
        grad_mixed,
    )
    grad_triple = grad_triple.astype(jnp.bfloat16).reshape(row_total, 3 * CD)
    grad_triple_proj = matmul_tn(state["act_one"], grad_triple)
    grad_act_one = matmul_nt(grad_triple, char_in_low[:, : 3 * CD])
    back_one, grad_gain_one = rms_backward(
        grad_act_one, gain_one, state["normed_one"], state["inverse_one"]
    )
    grad_embedded = (grad_first + back_one).astype(jnp.bfloat16)
    grad_table = matmul_tn(state["one_hot"], grad_embedded)
    return (
        grad_table,
        grad_triple_proj,
        grad_out_proj,
        grad_up,
        grad_down,
        grad_gain_one,
        grad_gain_two,
    )


def adam_step(weight, grad, first_old, second_old, clip_factor, rate, decay):
    clipped = grad * clip_factor
    first_new = BETA_ONE * first_old + (1.0 - BETA_ONE) * clipped
    second_new = BETA_TWO * second_old + (1.0 - BETA_TWO) * clipped * clipped
    first_hat = first_new / (1.0 - BETA_ONE**STEP)
    second_hat = second_new / (1.0 - BETA_TWO**STEP)
    weight_new = weight - rate * (first_hat / (jnp.sqrt(second_hat) + ADAM_EPS) + decay * weight)
    return (grad, first_new, second_new, weight_new, weight_new.astype(jnp.bfloat16))


def body(
    char_ids,
    char_counts,
    language,
    words_in,
    out_cotangent,
    char_table,
    char_in,
    char_down,
    word_in,
    word_down,
    norm_gains,
    old_table_first,
    old_table_second,
    old_char_in_first,
    old_char_in_second,
    old_char_down_first,
    old_char_down_second,
    old_word_in_first,
    old_word_in_second,
    old_word_down_first,
    old_word_down_second,
    old_gains_first,
    old_gains_second,
):
    by_cols = (
        lax.all_gather(char_table.astype(jnp.bfloat16), "head", axis=1, tiled=True),
        lax.all_gather(char_in.astype(jnp.bfloat16), "head", axis=1, tiled=True),
        lax.all_gather(char_down.astype(jnp.bfloat16), "head", axis=1, tiled=True),
        lax.all_gather(word_in.astype(jnp.bfloat16), "head", axis=1, tiled=True),
        lax.all_gather(word_down.astype(jnp.bfloat16), "head", axis=1, tiled=True),
    )
    table_low, char_in_low, char_down_low, word_in_low, word_down_low = (
        lax.all_gather(by_cols[0], "dp", axis=0, tiled=True),
        lax.all_gather(by_cols[1], "dp", axis=0, tiled=True),
        lax.all_gather(by_cols[2], "dp", axis=0, tiled=True),
        lax.all_gather(by_cols[3], "dp", axis=0, tiled=True),
        lax.all_gather(by_cols[4], "dp", axis=0, tiled=True),
    )
    gain_one = norm_gains[:CD]
    gain_two = norm_gains[CD : 2 * CD]
    gain_three = norm_gains[2 * CD : 2 * CD + D]
    gain_four = norm_gains[2 * CD + D :]
    seq_count, local_words = (words_in.shape[0], words_in.shape[1])
    word_total = seq_count * local_words
    head_size = D // HEADS
    char_state = char_forward(
        char_ids, char_counts, language, table_low, char_in_low, char_down_low, gain_one, gain_two
    )
    word_vector = matmul(char_state["pooled"], char_in_low[:, 4 * CD + CFF :])
    word_start = words_in.reshape(word_total, D).astype(jnp.float32) + word_vector
    scaled_three, normed_three, inverse_three = rms_forward(word_start, gain_three)
    act_three = scaled_three.astype(jnp.bfloat16)
    word_triple = matmul(act_three, word_in_low[:, : 3 * D]).astype(jnp.bfloat16)
    word_triple = word_triple.reshape(seq_count, local_words, 3, HEADS, head_size)
    block = lax.all_to_all(word_triple, "head", split_axis=3, concat_axis=1, tiled=True)
    mixed, log_total = attend_forward(
        block[:, :, 0], block[:, :, 1], block[:, :, 2], causal_mask(block.shape[1])
    )
    returned = lax.all_to_all(mixed, "head", split_axis=1, concat_axis=2, tiled=True)
    mixed_flat = returned.reshape(word_total, D)
    word_after = word_start + matmul(mixed_flat, word_in_low[:, 3 * D : 4 * D])
    scaled_four, normed_four, inverse_four = rms_forward(word_after, gain_four)
    act_four = scaled_four.astype(jnp.bfloat16)
    word_upper = matmul(act_four, word_in_low[:, 4 * D :])
    word_hidden = gelu_value(word_upper).astype(jnp.bfloat16)
    result = word_after + matmul(word_hidden, word_down_low)
    output = result.astype(jnp.bfloat16).reshape(seq_count, local_words, D)
    grad_result = out_cotangent.reshape(word_total, D).astype(jnp.float32)
    grad_down_in = grad_result.astype(jnp.bfloat16)
    grad_wdown = matmul_tn(word_hidden, grad_down_in)
    grad_hidden = matmul_nt(grad_down_in, word_down_low)
    grad_upper = (grad_hidden * gelu_slope(word_upper)).astype(jnp.bfloat16)
    grad_wup = matmul_tn(act_four, grad_upper)
    grad_act_four = matmul_nt(grad_upper, word_in_low[:, 4 * D :])
    back_four, grad_gain_four = rms_backward(grad_act_four, gain_four, normed_four, inverse_four)
    grad_after = grad_result + back_four
    grad_out_in = grad_after.astype(jnp.bfloat16)
    grad_wout = matmul_tn(mixed_flat, grad_out_in)
    grad_mixed = matmul_nt(grad_out_in, word_in_low[:, 3 * D : 4 * D]).astype(jnp.bfloat16)
    grad_mixed = grad_mixed.reshape(seq_count, local_words, HEADS, head_size)
    head_grads = lax.all_to_all(grad_mixed, "head", split_axis=2, concat_axis=1, tiled=True)
    triple_heads = attend_backward(
        block[:, :, 0],
        block[:, :, 1],
        block[:, :, 2],
        causal_mask(block.shape[1]),
        log_total,
        head_grads,
    )
    triple_grads = lax.all_to_all(
        triple_heads.astype(jnp.bfloat16), "head", split_axis=1, concat_axis=3, tiled=True
    )
    triple_grads = triple_grads.reshape(word_total, 3 * D)
    grad_wtriple = matmul_tn(act_three, triple_grads)
    grad_act_three = matmul_nt(triple_grads, word_in_low[:, : 3 * D])
    back_three, grad_gain_three = rms_backward(
        grad_act_three, gain_three, normed_three, inverse_three
    )
    grad_start = grad_after + back_three
    input_grad = grad_start.reshape(seq_count, local_words, D)
    grad_vector = grad_start.astype(jnp.bfloat16)
    grad_pool = matmul_tn(char_state["pooled"], grad_vector)
    grad_pooled = matmul_nt(grad_vector, char_in_low[:, 4 * CD + CFF :])
    fresh_in = lax.optimization_barrier((grad_pooled, table_low, char_in_low, char_down_low))
    recent = char_forward(
        char_ids, char_counts, language, fresh_in[1], fresh_in[2], fresh_in[3], gain_one, gain_two
    )
    char_grads = char_backward(
        recent, grad_pooled, char_counts, char_in_low, char_down_low, gain_one, gain_two
    )
    grad_table, grad_ctriple, grad_cout, grad_cup, grad_cdown, grad_gain_one, grad_gain_two = (
        char_grads
    )
    grad_cin = jnp.concatenate([grad_ctriple, grad_cout, grad_cup, grad_pool], axis=1)
    grad_win = jnp.concatenate([grad_wtriple, grad_wout, grad_wup], axis=1)
    gain_grads = jnp.concatenate([grad_gain_one, grad_gain_two, grad_gain_three, grad_gain_four])
    owned_parts = (char_table, char_in, char_down, word_in, word_down)
    summed = lax.psum(
        (grad_table, grad_cin, grad_cdown, grad_win, grad_wdown, gain_grads), ("dp", "head")
    )
    square = jnp.sum(summed[0] * summed[0])
    for grad_part in summed[1:]:
        square = square + jnp.sum(grad_part * grad_part)
    row_index = lax.axis_index("dp")
    col_index = lax.axis_index("head")
    reduced = [
        lax.dynamic_slice(
            full_grad,
            (row_index * shard_part.shape[0], col_index * shard_part.shape[1]),
            shard_part.shape,
        )
        for full_grad, shard_part in zip(summed[:5], owned_parts)
    ]
    gains_sum = summed[5]
    grad_norm = jnp.sqrt(square)
    clip_factor = jnp.minimum(1.0, CLIP / grad_norm)
    table_out = adam_step(
        char_table,
        reduced[0],
        old_table_first,
        old_table_second,
        clip_factor,
        MATRIX_RATE,
        MATRIX_DECAY,
    )
    cin_out = adam_step(
        char_in,
        reduced[1],
        old_char_in_first,
        old_char_in_second,
        clip_factor,
        MATRIX_RATE,
        MATRIX_DECAY,
    )
    cdown_out = adam_step(
        char_down,
        reduced[2],
        old_char_down_first,
        old_char_down_second,
        clip_factor,
        MATRIX_RATE,
        MATRIX_DECAY,
    )
    win_out = adam_step(
        word_in,
        reduced[3],
        old_word_in_first,
        old_word_in_second,
        clip_factor,
        MATRIX_RATE,
        MATRIX_DECAY,
    )
    wdown_out = adam_step(
        word_down,
        reduced[4],
        old_word_down_first,
        old_word_down_second,
        clip_factor,
        MATRIX_RATE,
        MATRIX_DECAY,
    )
    gains_out = adam_step(
        norm_gains, gains_sum, old_gains_first, old_gains_second, clip_factor, GAIN_RATE, 0.0
    )
    return (
        (output, input_grad, grad_norm)
        + table_out
        + cin_out
        + cdown_out
        + win_out
        + wdown_out
        + gains_out
    )


def solution(mesh):
    return jax.shard_map(
        body,
        mesh=mesh,
        in_specs=(
            P("dp", "head", None),
            P("dp", "head"),
            P("dp"),
            P("dp", "head", None),
            P("dp", "head", None),
            P("dp", "head"),
            P("dp", "head"),
            P("dp", "head"),
            P("dp", "head"),
            P("dp", "head"),
            P(),
            P("dp", "head"),
            P("dp", "head"),
            P("dp", "head"),
            P("dp", "head"),
            P("dp", "head"),
            P("dp", "head"),
            P("dp", "head"),
            P("dp", "head"),
            P("dp", "head"),
            P("dp", "head"),
            P(),
            P(),
        ),
        out_specs=(
            P("dp", "head", None),
            P("dp", "head", None),
            P(),
            P("dp", "head"),
            P("dp", "head"),
            P("dp", "head"),
            P("dp", "head"),
            P("dp", "head"),
            P("dp", "head"),
            P("dp", "head"),
            P("dp", "head"),
            P("dp", "head"),
            P("dp", "head"),
            P("dp", "head"),
            P("dp", "head"),
            P("dp", "head"),
            P("dp", "head"),
            P("dp", "head"),
            P("dp", "head"),
            P("dp", "head"),
            P("dp", "head"),
            P("dp", "head"),
            P("dp", "head"),
            P("dp", "head"),
            P("dp", "head"),
            P("dp", "head"),
            P("dp", "head"),
            P("dp", "head"),
            P(),
            P(),
            P(),
            P(),
            P(),
        ),
        check_vma=False,
    )
```

profile of v0, /device:TPU:0, one launch (start us, length us, event | category | flops | bytes accessed | tf_op | source)
XLA Modules:
  0.0 1357.1 jit_solution(17441313958146858325)
XLA Ops:
  8.2 16.0 %all_gather.32 = bf16[32,2560]{1,0:T(8,128)(2,1)} all-gather(bf16[32,640]{1,0:T(8,128)(2,1)S(1)} %convert_element_type.172), channel_id=1, replica_groups=mesh['dp'=8,'head'=4] {'head'}, dimensions={1}, use_global_device_ids=true | all-gather | bytes 204800 | tf_op jit(solution)/shard_map/all_gather | solution.py:254
  25.2 16.7 %all_gather.36 = bf16[64,4096]{1,0:T(8,128)(2,1)} all-gather(bf16[64,1024]{1,0:T(8,128)(2,1)S(1)} %convert_element_type.183), channel_id=1, replica_groups=mesh['dp'=8,'head'=4] {'head'}, dimensions={1}, use_global_device_ids=true | all-gather | bytes 655360 | tf_op jit(solution)/shard_map/all_gather | solution.py:256
  46.9 13.1 all_gather.34
  60.1 13.1 all_gather.30
  74.4 12.5 all_gather.35
  113.9 35.9 %reshape.278 = bf16[512,16,3,4,64]{4,3,2,1,0:T(4,128)(2,1)} reshape(bf16[8192,768]{1,0:T(8,128)(2,1)} %convolution_convert_fusion.1) | data formatting | bytes 25165824 | tf_op jit(solution)/shard_map/reshape | solution.py:132
  149.8 21.9 %fusion.192 = (bf16[512,16,1,4,64]{4,3,2,1,0:T(4,128)(2,1)}, bf16[512,16,1,4,64]{4,3,2,1,0:T(4,128)(2,1)}, bf16[512,16,1,4,64]{4,3,2,1,0:T(4,128)(2,1)}) fusion(bf16[512,16,3,4,64]{4,3,2,1,0:T(4,128)(2,1)} %reshape.278), kind=kLoop, calls=%fused_computation.268 | loop fusion | bytes 25165824 | tf_op jit(solution)/shard_map/slice | solution.py:136
  171.7 11.5 fusion.34
  183.2 10.2 copy.200
  194.8 12.4 copy.201
  207.2 13.5 convert_bitcast_fusion.4
  229.0 12.8 reshape.279
  247.9 10.4 multiply_convert_fusion.6.clone.4
  258.3 9.6 select_reduce_fusion
  285.0 45.2 %all_gather.38 = bf16[256,512]{1,0:T(8,128)(2,1)} all-gather(bf16[256,128]{1,0:T(8,128)(2,1)S(1)} %convert_element_type.190), channel_id=1, replica_groups=mesh['dp'=8,'head'=4] {'head'}, dimensions={1}, use_global_device_ids=true | all-gather | bytes 327680 | tf_op jit(solution)/shard_map/all_gather | solution.py:257
  351.2 15.5 %all_to_all.66 = bf16[4,2,32768]{2,1,0:T(2,128)(2,1)S(1)} all-to-all(bf16[4,2,32768]{2,1,0:T(2,128)(2,1)S(1)} %reshape.293), channel_id=1, replica_groups=mesh['dp'=8,'head'=4] {'head'}, dimensions={0} | all-to-all | bytes 1048576 | tf_op jit(solution)/shard_map/all_to_all | solution.py:286
  393.0 12.5 all-to-all-done.2
  428.3 24.9 %fusion.110 = bf16[2,1024,1,2,64]{1,4,3,0,2:T(8,128)(2,1)} fusion(f32[2,2,1024,1024]{2,3,1,0:T(8,128)} %fusion.123, f32[2,2,1024,1024]{2,3,1,0:T(8,128)} %copy-done.4, f32[2,2,1024]{2,1,0:T(2,128)S(1)} %log_add_fusion.1, pred[1024,1024]{0,1:T(8,128)(4,1)} %iota_compare_fusion.4, bf16[2,1024,3,2,64]{1,4,3,0,2:T(8,128)(2,1)} %copy-done.19), kind=kOutput, calls=%fused_computation.148 | convolution fusion | flops 583275520 | bytes 70287360 | tf_op jit(solution)/shard_map/bhqk,bkhd->bqhd/dot_general | solution.py:111
  453.2 25.0 %fusion.107 = bf16[2,1024,1,2,64]{1,4,3,0,2:T(8,128)(2,1)} fusion(f32[2,2,1024,1024]{2,3,1,0:T(8,128)} %fusion.123, f32[2,2,1024,1024]{2,3,1,0:T(8,128)} %copy-done.4, f32[2,2,1024]{2,1,0:T(2,128)S(1)} %log_add_fusion.1, pred[1024,1024]{0,1:T(8,128)(4,1)} %iota_compare_fusion.4, bf16[2,1024,3,2,64]{1,4,3,0,2:T(8,128)(2,1)} %copy-done.19), kind=kOutput, calls=%fused_computation.147 | convolution fusion | flops 583275520 | bytes 70287360 | tf_op jit(solution)/shard_map/bhqk,bqhd->bkhd/dot_general | solution.py:114
  510.2 22.5 %all-to-all-done.3 = bf16[4,2,98304]{2,1,0:T(2,128)(2,1)} async-done(((bf16[4,2,98304]{2,1,0:T(2,128)(2,1)}), bf16[4,2,98304]{2,1,0:T(2,128)(2,1)}, u32[]{:S(2)}, u32[]{:S(2)}) %all-to-all-start.3) | async-done | bytes 1572896 | tf_op jit(solution)/shard_map/all_to_all | solution.py:317
  557.0 10.1 multiply_reduce_fusion.7
  584.6 35.9 %reshape.288 = bf16[512,16,3,4,64]{4,3,2,1,0:T(4,128)(2,1)} reshape(bf16[8192,768]{1,0:T(8,128)(2,1)} %convolution_convert_fusion) | data formatting | bytes 25165824 | tf_op jit(solution)/shard_map/reshape | solution.py:132
  620.5 21.9 %fusion.191 = (bf16[512,16,1,4,64]{4,3,2,1,0:T(4,128)(2,1)}, bf16[512,16,1,4,64]{4,3,2,1,0:T(4,128)(2,1)}, bf16[512,16,1,4,64]{4,3,2,1,0:T(4,128)(2,1)}) fusion(bf16[512,16,3,4,64]{4,3,2,1,0:T(4,128)(2,1)} %reshape.288), kind=kLoop, calls=%fused_computation.267 | loop fusion | bytes 25165824 | tf_op jit(solution)/shard_map/slice | solution.py:136
  642.4 11.9 fusion.58
  654.3 10.3 copy.220
  667.9 12.0 copy.221
  679.8 13.5 convert_bitcast_fusion.3
  701.6 13.1 reshape.289
  723.9 13.2 fusion.121
  737.1 16.9 %fusion.12 = f32[1024,256]{0,1:T(8,128)} fusion(bf16[8192,256]{1,0:T(8,128)(2,1)} %fusion.36, f32[8192,1024]{1,0:T(8,128)} %fusion.121), kind=kOutput, calls=%fused_computation.18 | convolution fusion | flops 4336910336 | bytes 38797312 | tf_op jit(solution)/shard_map/dot_general | solution.py:33
  754.0 18.3 %fusion.8 = bf16[8192,1024]{1,0:T(8,128)(2,1)} fusion(f32[8192,1024]{1,0:T(8,128)} %fusion.121, bf16[8192,256]{1,0:T(8,128)(2,1)S(1)} %copy-done.16, bf16[1024,256]{0,1:T(8,128)(2,1)S(1)} %copy-done.27), kind=kOutput, calls=%fused_computation.9 | convolution fusion | flops 4378853376 | bytes 55050240 | tf_op jit(solution)/shard_map/dot_general | solution.py:39
  772.3 9.8 fusion.178
  782.2 12.2 multiply_reduce_fusion.1
  807.3 12.9 reshape.290
  820.1 11.5 fusion.60
  831.7 11.3 copy.227
  847.1 15.1 %copy.229 = bf16[512,4,16,16]{2,3,1,0:T(8,128)(2,1)} copy(bf16[512,4,16,16]{0,3,2,1:T(8,128)(2,1)} %multiply_convert_fusion.15) | data formatting | bytes 2097152 | tf_op jit(solution)/shard_map/convert_element_type | solution.py:110
  871.8 13.6 %convert_bitcast_fusion.1 = bf16[512,16,1,4,64]{4,1,3,0,2:T(8,128)(2,1)} fusion(bf16[512,4,16,16]{2,3,1,0:T(8,128)(2,1)} %copy.229, bf16[512,16,1,4,64]{4,3,2,1,0:T(4,128)(2,1)} %get-tuple-element.180), kind=kOutput, calls=%fused_computation.61 | convolution fusion | flops 69206016 | bytes 9437184 | tf_op jit(solution)/shard_map/bhqk,bqhd->bkhd/dot_general | solution.py:114
  885.4 12.4 copy.231
  897.8 13.6 %convert_bitcast_fusion = bf16[512,16,1,4,64]{4,1,3,0,2:T(8,128)(2,1)} fusion(bf16[512,4,16,16]{2,3,1,0:T(8,128)(2,1)} %copy.231, bf16[512,16,4,64]{3,2,1,0:T(4,128)(2,1)} %reshape.290), kind=kOutput, calls=%fused_computation.60 | convolution fusion | flops 69206016 | bytes 9437184 | tf_op jit(solution)/shard_map/bhqk,bqhd->bkhd/dot_general | solution.py:101
  911.4 22.4 %pad_maximum_fusion = bf16[512,16,3,4,64]{4,1,3,0,2:T(8,128)(2,1)} fusion(bf16[512,16,1,4,64]{4,1,3,0,2:T(8,128)(2,1)} %convert_bitcast_fusion, bf16[512,16,1,4,64]{4,1,3,0,2:T(8,128)(2,1)} %convert_bitcast_fusion.1, bf16[512,16,1,4,64]{4,1,3,0,2:T(8,128)(2,1)} %convert_bitcast_fusion.2), kind=kLoop, calls=%fused_computation.17 | loop fusion | flops 12582912 | bytes 25165824 | tf_op jit(solution)/shard_map/stack | solution.py:115
  933.8 19.1 %copy.232 = bf16[512,16,3,4,64]{4,3,2,1,0:T(4,128)(2,1)} copy(bf16[512,16,3,4,64]{4,1,3,0,2:T(8,128)(2,1)} %pad_maximum_fusion) | data formatting | bytes 25165824 | tf_op jit(solution)/shard_map/stack | solution.py:115
  952.9 35.6 %convert_element_type.211 = bf16[8192,768]{1,0:T(8,128)(2,1)} reshape(bf16[512,16,3,4,64]{4,3,2,1,0:T(4,128)(2,1)} %copy.232) | data formatting | bytes 25165824 | tf_op jit(solution)/shard_map/convert_element_type | solution.py:198
  988.6 11.5 fusion.177
  1000.1 12.3 multiply_reduce_fusion.2
  1012.5 16.5 %fusion.9 = f32[1024,256]{0,1:T(8,128)} fusion(s32[8192]{0:T(1024)S(1)} %copy-done.64, f32[8192,256]{1,0:T(8,128)S(1)} %bitcast.161, f32[8192,256]{1,0:T(8,128)} %get-tuple-element.213, f32[8192,256]{1,0:T(8,128)S(1)} %bitcast.159, f32[8192]{0:T(1024)S(1)} %broadcast_multiply_fusion, f32[8192]{0:T(1024)S(1)} %copy-done.51, f32[256]{0:T(256)S(1)} %copy-done.67), kind=kOutput, calls=%fused_computation.14 | convolution fusion | flops 4318035968 | bytes 26313728 | tf_op jit(solution)/shard_map/dot_general | solution.py:33
  1040.0 39.9 %psum.47 = f32[1536]{0:T(1024)S(1)} all-reduce(f32[1536]{0:T(1024)S(1)} %pad_maximum_fusion.4), channel_id=1, replica_groups=mesh['dp'=8,'head'=4] {'dp','head'}, use_global_device_ids=true, to_apply=%region_33.34 | all-reduce | flops 1536 | bytes 12288 | tf_op jit(solution)/shard_map/psum | solution.py:345
  1080.5 242.5 %all-reduce.3.cloned.1.call-done = (f32[1024,256]{0,1:T(8,128)}, f32[256,2560]{1,0:T(8,128)}, f32[1024,256]{0,1:T(8,128)}, f32[512,4096]{1,0:T(8,128)}, f32[2048,512]{1,0:T(8,128)}) async-done(((f32[1024,256]{0,1:T(8,128)}, f32[256,2560]{1,0:T(8,128)}, f32[1024,256]{0,1:T(8,128)}, f32[512,4096]{1,0:T(8,128)}, f32[2048,512]{1,0:T(8,128)}), (f32[1024,256]{0,1:T(8,128)}, f32[256,2560]{1,0:T(8,128)}, ...) | async-done | bytes 17301520 | tf_op jit(solution)/shard_map/psum | solution.py:345
  (273 shorter events, 292.5 us)
Async XLA Ops:
  7.2 98.1 %all-gather.4.cloned.1.call-start = ((), (), s32[]{:S(2)}) async-start(), calls=%async_computation.4 | async-start | bytes 1474560 | tf_op jit(solution)/shard_map/all_gather | solution.py:261
  24.2 244.6 %all-gather.6.cloned.1.call-start = ((), (), s32[]{:S(2)}) async-start(), calls=%async_computation.5 | async-start | bytes 4718592 | tf_op jit(solution)/shard_map/all_gather | solution.py:263
  42.6 62.6 %copy-start.65 = (f32[256]{0:T(256)}, f32[256]{0:T(256)S(1)}, u32[]{:S(2)}) copy-start(f32[256]{0:T(256)S(1)} %get-tuple-element.189) | copy-start | bytes 3076
  42.6 205.2 %copy-start.60 = (f32[256]{0:T(256)}, f32[256]{0:T(256)S(1)}, u32[]{:S(2)}) copy-start(f32[256]{0:T(256)S(1)} %get-tuple-element.188) | copy-start | bytes 3076
  73.3 120.1 %copy-start.52 = (pred[512,16]{0,1:T(8,128)(4,1)}, pred[512,16]{0,1:T(8,128)(4,1)S(1)}, u32[]{:S(2)}) copy-start(pred[512,16]{0,1:T(8,128)(4,1)S(1)} %copy.197) | copy-start | bytes 24580
  74.4 30.8 %copy-start.62 = (s32[8192]{0:T(1024)}, s32[8192]{0:T(1024)S(1)}, u32[]{:S(2)}) copy-start(s32[8192]{0:T(1024)S(1)} %eq.8) | copy-start | bytes 98308
  87.0 171.4 %copy-start.26 = (bf16[1024,256]{0,1:T(8,128)(2,1)}, bf16[1024,256]{0,1:T(8,128)(2,1)S(1)}, u32[]{:S(2)}) copy-start(bf16[1024,256]{0,1:T(8,128)(2,1)S(1)} %all_gather.35) | copy-start | bytes 1572868
  229.0 12.8 copy-start.21
  269.7 15.3 %copy-start.43 = (f32[256,128]{1,0:T(8,128)S(1)}, f32[256,128]{1,0:T(8,128)}, u32[]{:S(2)}) copy-start(f32[256,128]{1,0:T(8,128)} %param.32) | copy-start | bytes 393220
  281.2 50.3 %all-to-all-start = ((bf16[2,256,3,8,64]{1,0,4,2,3:T(2,128)(2,1)}), bf16[2,256,3,8,64]{1,0,4,2,3:T(2,128)(2,1)S(1)}, u32[]{:S(2)}, u32[]{:S(2)}) async-start(bf16[2,256,3,8,64]{1,0,4,2,3:T(2,128)(2,1)} %copy.204), calls=%async_computation | async-start | bytes 3145728 | tf_op jit(solution)/shard_map/all_to_all | solution.py:282
  285.0 91.2 %all-gather.8.cloned.1.call-start = ((), (), s32[]{:S(2)}) async-start(), calls=%async_computation.6 | async-start | bytes 2359296 | tf_op jit(solution)/shard_map/all_gather | solution.py:264
  349.5 19.6 %copy-start.8 = (f32[512,512]{1,0:T(8,128)S(1)}, f32[512,512]{1,0:T(8,128)}, u32[]{:S(2)}) copy-start(f32[512,512]{1,0:T(8,128)} %copy-done.7) | copy-start | bytes 3145732
  349.5 21.3 %copy-start.59 = (f32[512]{0:T(512)S(1)}, f32[512]{0:T(512)}, u32[]{:S(2)}) copy-start(f32[512]{0:T(512)} %get-tuple-element.186) | copy-start | bytes 6148
  370.8 136.1 %copy-start.9 = (f32[512,512]{1,0:T(8,128)}, f32[512,512]{1,0:T(8,128)S(1)}, u32[]{:S(2)}) copy-start(f32[512,512]{1,0:T(8,128)S(1)} %get-tuple-element.201) | copy-start | bytes 3145732
  388.4 17.1 %all-to-all-start.2 = ((bf16[2,256,8,64]{1,0,3,2:T(2,128)(2,1)}), bf16[2,256,8,64]{1,0,3,2:T(2,128)(2,1)}, u32[]{:S(2)}, u32[]{:S(2)}) async-start(bf16[2,256,8,64]{1,0,3,2:T(2,128)(2,1)} %reshape.285), calls=%async_computation.2 | async-start | bytes 1048576 | tf_op jit(solution)/shard_map/all_to_all | solution.py:308
  494.4 38.3 %all-to-all-start.3 = ((bf16[4,2,98304]{2,1,0:T(2,128)(2,1)}), bf16[4,2,98304]{2,1,0:T(2,128)(2,1)}, u32[]{:S(2)}, u32[]{:S(2)}) async-start(bf16[4,2,98304]{2,1,0:T(2,128)(2,1)} %reshape.295), calls=%async_computation.3 | async-start | bytes 3145728 | tf_op jit(solution)/shard_map/all_to_all | solution.py:317
  498.8 824.2 %all-reduce.3.cloned.1.call-start = ((), (), s32[]{:S(2)}) async-start(), calls=%async_computation.7 | async-start | bytes 34603008 | tf_op jit(solution)/shard_map/psum | solution.py:345
  554.6 12.5 copy-start.35
  654.3 10.3 copy-start.53
  664.6 15.3 %copy-start.2 = (f32[512,4,16,16]{0,3,2,1:T(8,128)}, f32[512,4,16,16]{0,3,2,1:T(8,128)S(1)}, u32[]{:S(2)}) copy-start(f32[512,4,16,16]{0,3,2,1:T(8,128)S(1)} %copy.220) | copy-start | bytes 6291460
  701.6 13.1 copy-start.23
  737.1 16.9 %copy-start.16 = (bf16[8192,256]{1,0:T(8,128)(2,1)S(1)}, bf16[8192,256]{1,0:T(8,128)(2,1)}, u32[]{:S(2)}) copy-start(bf16[8192,256]{1,0:T(8,128)(2,1)} %fusion.36) | copy-start | bytes 12582916
  737.1 16.9 %copy-start.27 = (bf16[1024,256]{0,1:T(8,128)(2,1)S(1)}, bf16[1024,256]{0,1:T(8,128)(2,1)}, u32[]{:S(2)}) copy-start(bf16[1024,256]{0,1:T(8,128)(2,1)} %copy-done.26) | copy-start | bytes 1572868
  782.2 12.3 copy-start.25
  831.7 11.3 copy-start.3
  831.7 11.3 copy-start.42
  831.7 11.3 copy-start.54
  871.8 13.6 %copy-start.17 = (bf16[512,4,16,16]{0,3,2,1:T(8,128)(2,1)S(1)}, bf16[512,4,16,16]{0,3,2,1:T(8,128)(2,1)}, u32[]{:S(2)}) copy-start(bf16[512,4,16,16]{0,3,2,1:T(8,128)(2,1)} %get-tuple-element.184) | copy-start | bytes 3145732
  952.9 35.6 %copy-start.51 = (f32[8192]{0:T(1024)S(1)}, f32[8192]{0:T(1024)}, u32[]{:S(2)}) copy-start(f32[8192]{0:T(1024)} %copy-done.50) | copy-start | bytes 98308
  952.9 35.7 %copy-start.67 = (f32[256]{0:T(256)S(1)}, f32[256]{0:T(256)}, u32[]{:S(2)}) copy-start(f32[256]{0:T(256)} %copy-done.65) | copy-start | bytes 3076
  988.6 23.8 %slice-start = ((s8[8388608]{0:T(1024)(128)(4,1)}), s8[4194304]{0:T(1024)(128)(4,1)S(1)}, s32[]{:S(2)}) async-start(s8[8388608]{0:T(1024)(128)(4,1)} %bitcast.158), calls=%async_computation.8 | async-start | bytes 8388608
  988.6 23.8 %slice-start.2 = ((s8[8388608]{0:T(1024)(128)(4,1)}), s8[4194304]{0:T(1024)(128)(4,1)S(1)}, s32[]{:S(2)}) async-start(s8[8388608]{0:T(1024)(128)(4,1)} %bitcast.160), calls=%async_computation.10 | async-start | bytes 8388608
  1000.1 12.3 slice-start.1
  1000.1 12.3 slice-start.3
  1000.1 12.3 copy-start.64
  1012.5 16.6 %copy-start.5 = (f32[512,2048]{1,0:T(8,128)S(1)}, f32[512,2048]{1,0:T(8,128)}, u32[]{:S(2)}) copy-start(f32[512,2048]{1,0:T(8,128)} %fusion.176) | copy-start | bytes 12582916
  1012.5 16.6 %copy-start.6 = (f32[512,1536]{1,0:T(8,128)S(1)}, f32[512,1536]{1,0:T(8,128)}, u32[]{:S(2)}) copy-start(f32[512,1536]{1,0:T(8,128)} %fusion.175) | copy-start | bytes 9437188
  1012.5 16.6 %copy-start.13 = (f32[512,512]{1,0:T(8,128)S(1)}, f32[512,512]{1,0:T(8,128)}, u32[]{:S(2)}) copy-start(f32[512,512]{1,0:T(8,128)} %fusion.140) | copy-start | bytes 3145732
  1323.0 10.3 copy-start.20
  1323.0 11.5 copy-start.33
  1323.0 11.5 copy-start.34
  1323.0 16.4 %copy-start.56 = (f32[128,64]{0,1:T(8,128)S(1)}, f32[128,64]{0,1:T(8,128)}, u32[]{:S(2)}) copy-start(f32[128,64]{0,1:T(8,128)} %param.28) | copy-start | bytes 98308
  1323.0 17.8 %copy-start.57 = (f32[128,64]{0,1:T(8,128)S(1)}, f32[128,64]{0,1:T(8,128)}, u32[]{:S(2)}) copy-start(f32[128,64]{0,1:T(8,128)} %param.30) | copy-start | bytes 98308
  1323.0 20.7 %copy-start.37 = (f32[64,1024]{1,0:T(8,128)S(1)}, f32[64,1024]{1,0:T(8,128)}, u32[]{:S(2)}) copy-start(f32[64,1024]{1,0:T(8,128)} %param.31) | copy-start | bytes 786436
  1323.0 20.7 %copy-start.48 = (f32[64,1024]{1,0:T(8,128)S(1)}, f32[64,1024]{1,0:T(8,128)}, u32[]{:S(2)}) copy-start(f32[64,1024]{1,0:T(8,128)} %param.41) | copy-start | bytes 786436
  1327.0 18.7 %copy-start.44 = (f32[256,128]{1,0:T(8,128)S(1)}, f32[256,128]{1,0:T(8,128)}, u32[]{:S(2)}) copy-start(f32[256,128]{1,0:T(8,128)} %param.32) | copy-start | bytes 393220
  1327.0 18.7 %copy-start.55 = (f32[256,128]{1,0:T(8,128)S(1)}, f32[256,128]{1,0:T(8,128)}, u32[]{:S(2)}) copy-start(f32[256,128]{1,0:T(8,128)} %param.43) | copy-start | bytes 393220
  1327.1 20.5 %copy-start.47 = (f32[32,640]{1,0:T(8,128)S(1)}, f32[32,640]{1,0:T(8,128)}, u32[]{:S(2)}) copy-start(f32[32,640]{1,0:T(8,128)} %param.29) | copy-start | bytes 245764
  (35 other events, 182.2 us)
Sparse Core Ops, SparseCore 0:
  24.3 25.7 all-gather.3
  52.0 38.8 all-gather.5
  330.4 26.5 all-gather.7
  1034.6 288.3 all-reduce.2
where the time goes:
time: 1370 us; the launch traced here: 1360 us
  matrix products  404 us (29%)
  local copies, waits for them, and re-layouts  379 us (28%)
  waiting for transfers between devices  278 us (20%)
  blocking collectives  182 us (13%)
  other arithmetic  82 us (6%)
  between operations  20 us (1%)
    psum x1, waiting for transfers between devices, body(): lax.psum((grad_table, grad_cin, grad_cdown, grad_win, grad_wdown, gain_gr...  242 us
    dot_general x14, matrix products, matmul(): return jnp.dot(left_side, right_side, preferred_element_type=jnp.float32)  96 us
    dot_general x10, matrix products, matmul_tn(): lax.dot_general(left_side, right_side, (((0,), (0,)), ((), ())), preferre...  72.5 us
    reshape x2, local copies, waits for them, and re-layouts, char_forward(): char_triple.reshape(word_total, char_count, 3, CHEADS, head_size)  71.8 us
    dot_general x9, matrix products, matmul_nt(): lax.dot_general(left_side, right_side, (((1,), (1,)), ((), ())), preferre...  58.3 us
    all_gather x1, blocking collectives, body(): lax.all_gather(word_down.astype(jnp.bfloat16), 'head', axis=1, tiled=True)  45.2 us
    slice x2, local copies, waits for them, and re-layouts, char_forward(): char_triple[:, :, 2]  43.7 us
    psum x1, blocking collectives, body(): lax.psum((grad_table, grad_cin, grad_cdown, grad_win, grad_wdown, gain_gr...  39.9 us
  transfers between devices with their start and end apart: 7, of which 3 were waited for; matrix products, arithmetic and copies ran while one was open for 16% of the time, Pallas kernels for 0%

commit v1 on v0

--- a/solution.py
+++ b/solution.py
@@ -1,6 +1,8 @@
 import jax
 import jax.numpy as jnp
 from jax import lax
+from jax.experimental import pallas as pl
+from jax.experimental.pallas import tpu as pltpu
 from jax.sharding import PartitionSpec as P
 
 D = 512
@@ -115,103 +117,365 @@
     return jnp.stack([grad_queries, grad_keys, grad_values], axis=2)
 
 
-def char_forward(
-    char_ids, char_counts, language, table_low, char_in_low, char_down_low, gain_one, gain_two
+ROWS = 256
+SLOTS = 16
+GROUP = 128
+VMEM_BYTES = 56 * 1024 * 1024
+ERFC_P = 0.39
+ERFC = (0.235325887, 0.091384224, 0.649569841, -0.635413203, 0.886672317, -0.227539068)
+
+
+def dot_nn(left_side, right_side):
+    return lax.dot_general(
+        left_side, right_side, (((1,), (0,)), ((), ())), preferred_element_type=jnp.float32
+    )
+
+
+def dot_tn(left_side, right_side):
+    return lax.dot_general(
+        left_side, right_side, (((0,), (0,)), ((), ())), preferred_element_type=jnp.float32
+    )
+
+
+def dot_nt(left_side, right_side):
+    return lax.dot_general(
+        left_side, right_side, (((1,), (1,)), ((), ())), preferred_element_type=jnp.float32
+    )
+
+
+def gelu_pair(upper):
+    size = jnp.abs(upper)
+    t = 1.0 / (1.0 + (ERFC_P * SQRT_HALF) * size)
+    poly = ERFC[5]
+    for c in ERFC[4::-1]:
+        poly = poly * t + c
+    bell = jnp.exp(upper * upper * -0.5)
+    half = 0.5 * (poly * t * bell)
+    phi = jnp.where(upper > 0, 1.0 - half, half)
+    return upper * phi, phi + upper * (bell * INV_ROOT_TWO_PI)
+
+
+def iota(shape, dim):
+    return lax.broadcasted_iota(jnp.int32, shape, dim)
+
+
+def split_two(values):
+    high = values.astype(jnp.bfloat16)
+    return high, (values - high.astype(jnp.float32)).astype(jnp.bfloat16)
+
+
+def pack_kernel(count_row_ref, count_col_ref, ids_ref, ids_back_ref, out_ref, tiles_ref):
+    row = count_row_ref[0]
+    col = count_col_ref[0]
+    n = row.shape[1]
+    sub, lane = iota((n, n), 0), iota((n, n), 1)
+    ahead = (row > col) | ((row == col) & (lane < sub))
+    rank_col = jnp.sum(ahead.astype(jnp.float32), axis=1, keepdims=True).astype(jnp.int32)
+    ahead = (col > row) | ((col == row) & (sub < lane))
+    rank_row = jnp.sum(ahead.astype(jnp.float32), axis=0, keepdims=True).astype(jnp.int32)
+    clash = (rank_col < rank_row) & (col + row > SLOTS)
+    alone = jnp.max(jnp.where(clash, rank_col + rank_row, 0).astype(jnp.float32))
+    alone = jnp.maximum(alone.astype(jnp.int32) - n + 2, 0)
+    partner = n - 1 + alone - rank_row
+    second = (rank_row >= alone) & (rank_row > partner)
+    bins = jnp.where(second, partner, rank_row)
+    here = sub == bins
+    first_map = (here & jnp.logical_not(second)).astype(jnp.float32).astype(jnp.bfloat16)
+    second_map = (here & second).astype(jnp.float32).astype(jnp.bfloat16)
+    pos = lax.rem(iota((n, GROUP), 1), SLOTS)
+    word = iota((n, GROUP), 0) + 1
+    wide = jnp.broadcast_to(col, (n, GROUP))
+    in_first, in_second = pos < wide, pos >= SLOTS - wide
+
+    def kept(mask, values):
+        return jnp.where(mask, values, 0).astype(jnp.float32).astype(jnp.bfloat16)
+
+    groups = n * SLOTS // GROUP
+    per = GROUP // SLOTS
+    own = iota((groups, per, GROUP), 1) == lax.div(iota((groups, per, GROUP), 2), SLOTS)
+    ids, back = ids_ref[0], ids_back_ref[0]
+    zero = jnp.zeros_like(wide)
+    for k, (one, two) in enumerate(
+        ((ids + 1, back + 1), (word, word), (zero, SLOTS - wide), (wide, zero + SLOTS))
+    ):
+        full = dot_nn(first_map, kept(in_first, one)) + dot_nn(second_map, kept(in_second, two))
+        full = jnp.where(own, full.reshape(groups, per, GROUP), 0.0)
+        out_ref[0, k] = jnp.sum(full, axis=1).astype(jnp.int32)
+    used = alone + lax.div(n - alone + 1, 2)
+    tiles_ref[pl.program_id(0)] = lax.div(used * SLOTS + ROWS - 1, ROWS)
+
+
+def pack_rows(char_ids, char_counts):
+    seqs, words, slots = char_ids.shape
+    ids = jnp.tile(char_ids, (1, 1, GROUP // slots))
+    back = jnp.tile(char_ids[:, :, ::-1], (1, 1, GROUP // slots))
+    groups = words * slots // GROUP
+    return pl.pallas_call(
+        pack_kernel,
+        grid=(seqs,),
+        in_specs=[
+            pl.BlockSpec((1, 1, words), lambda s: (s, 0, 0)),
+            pl.BlockSpec((1, words, 1), lambda s: (s, 0, 0)),
+            pl.BlockSpec((1, words, GROUP), lambda s: (s, 0, 0)),
+            pl.BlockSpec((1, words, GROUP), lambda s: (s, 0, 0)),
+        ],
+        out_specs=[
+            pl.BlockSpec((1, 4, groups, GROUP), lambda s: (s, 0, 0, 0)),
+            pl.BlockSpec(memory_space=pltpu.SMEM),
+        ],
+        out_shape=[
+            jax.ShapeDtypeStruct((seqs, 4, groups, GROUP), jnp.int32),
+            jax.ShapeDtypeStruct((seqs,), jnp.int32),
+        ],
+        name="pack",
+    )(char_counts[:, None, :], char_counts[:, :, None], ids, back)
+
+
+def tile_maps(pack_ref, step, words):
+    per = ROWS // GROUP
+    id_rows = pack_ref[0, pl.ds(step * per, per), :]
+    word_rows = pack_ref[1, pl.ds(step * per, per), :]
+    letters = iota((CV, GROUP), 0) + 1
+    spots = iota((words, GROUP), 0) + 1
+    one_hot = [
+        (letters == id_rows[g : g + 1]).astype(jnp.float32).astype(jnp.bfloat16) for g in range(per)
+    ]
+    word_map = [
+        (spots == word_rows[g : g + 1]).astype(jnp.float32).astype(jnp.bfloat16) for g in range(per)
+    ]
+    return jnp.concatenate(one_hot, axis=1), jnp.concatenate(word_map, axis=1)
+
+
+def column_rms(values):
+    inverse = lax.rsqrt(jnp.mean(values * values, axis=0, keepdims=True) + EPS)
+    return values * inverse, inverse
+
+
+def own_block():
+    per = GROUP // SLOTS
+    shape = (per, SLOTS, GROUP)
+    return iota(shape, 0) == lax.div(iota(shape, 2), SLOTS)
+
+
+def to_compact(block, own):
+    per = GROUP // SLOTS
+    return jnp.sum(jnp.where(own, block.reshape(per, SLOTS, GROUP), 0.0), axis=0)
+
+
+def from_compact(compact, own):
+    per = GROUP // SLOTS
+    wide = jnp.broadcast_to(compact[None], (per, SLOTS, GROUP))
+    return jnp.where(own, wide, 0.0).astype(jnp.bfloat16).reshape(GROUP, GROUP)
+
+
+def char_fwd_kernel(tiles_ref, *refs):
+    @pl.when(pl.program_id(0) < tiles_ref[0])
+    def _():
+        char_fwd_tile(*refs)
+
+
+def char_fwd_tile(
+    pack_ref, table_ref, qkv_ref, out_ref, up_ref, down_ref, g1_ref, g2_ref,
+    pooled_ref, keep_qkv, keep_probs, keep_mixed, keep_first, keep_hidden, keep_slope,
 ):
-    seq_count, local_words, char_count = char_ids.shape
-    word_total = seq_count * local_words
-    row_total = word_total * char_count
-    table_rows = table_low.shape[0]
-    head_size = CD // CHEADS
-    index = (char_ids + CV * language[:, None, None]).reshape(row_total, 1)
-    one_hot = (index == lax.broadcasted_iota(jnp.int32, (1, table_rows), 1)).astype(jnp.bfloat16)
-    embedded = matmul(one_hot, table_low)
-    scaled_one, normed_one, inverse_one = rms_forward(embedded, gain_one)
-    act_one = scaled_one.astype(jnp.bfloat16)
-    char_triple = matmul(act_one, char_in_low[:, : 3 * CD]).astype(jnp.bfloat16)
-    char_triple = char_triple.reshape(word_total, char_count, 3, CHEADS, head_size)
-    counts_flat = char_counts.reshape(word_total, 1)
-    key_mask = lax.broadcasted_iota(jnp.int32, (1, char_count), 1) < counts_flat
-    char_mixed, char_lse = attend_forward(
-        char_triple[:, :, 0], char_triple[:, :, 1], char_triple[:, :, 2], key_mask[:, None, None, :]
-    )
-    mixed_flat = char_mixed.reshape(row_total, CD)
-    char_first = embedded + matmul(mixed_flat, char_in_low[:, 3 * CD : 4 * CD])
-    scaled_two, normed_two, inverse_two = rms_forward(char_first, gain_two)
-    act_two = scaled_two.astype(jnp.bfloat16)
-    char_upper = matmul(act_two, char_in_low[:, 4 * CD : 4 * CD + CFF])
-    char_hidden = gelu_value(char_upper).astype(jnp.bfloat16)
-    char_second = char_first + matmul(char_hidden, char_down_low)
-    kept_rows = jnp.where(
-        key_mask[:, :, None], char_second.reshape(word_total, char_count, CD), 0.0
-    )
-    pooled = (jnp.sum(kept_rows, axis=1) / counts_flat.astype(jnp.float32)).astype(jnp.bfloat16)
-    return {
-        "one_hot": one_hot,
-        "act_one": act_one,
-        "char_triple": char_triple,
-        "key_mask": key_mask,
-        "char_lse": char_lse,
-        "mixed_flat": mixed_flat,
-        "normed_one": normed_one,
-        "inverse_one": inverse_one,
-        "normed_two": normed_two,
-        "inverse_two": inverse_two,
-        "act_two": act_two,
-        "char_upper": char_upper,
-        "char_hidden": char_hidden,
-        "pooled": pooled,
-    }
-
-
-def char_backward(state, grad_pooled, char_counts, char_in_low, char_down_low, gain_one, gain_two):
-    word_total = grad_pooled.shape[0]
-    char_count = state["key_mask"].shape[1]
-    row_total = word_total * char_count
-    head_size = CD // CHEADS
-    counts_flat = char_counts.reshape(word_total, 1).astype(jnp.float32)
-    spread = jnp.where(state["key_mask"][:, :, None], (grad_pooled / counts_flat)[:, None, :], 0.0)
-    grad_second = spread.reshape(row_total, CD)
+    step = pl.program_id(0)
+    words = pooled_ref.shape[0]
+    per = ROWS // GROUP
+    head = CD // CHEADS
+
+    @pl.when(step == 0)
+    def _():
+        pooled_ref[...] = jnp.zeros_like(pooled_ref)
+
+    one_hot, word_map = tile_maps(pack_ref, step, words)
+    embedded = dot_nn(table_ref[...], one_hot)
+    act_one = (column_rms(embedded)[0] * g1_ref[...]).astype(jnp.bfloat16)
+    triple = dot_nn(qkv_ref[...], act_one).astype(jnp.bfloat16)
+    keep_qkv[...] = triple
+    low_rows = pack_ref[2, pl.ds(step * per, per), :]
+    high_rows = pack_ref[3, pl.ds(step * per, per), :]
+    own = own_block()
+    key_pos = iota((SLOTS, GROUP), 0)
+    mixed = []
+    for g in range(per):
+        valid = (key_pos >= low_rows[g : g + 1]) & (key_pos < high_rows[g : g + 1])
+        lanes = slice(g * GROUP, (g + 1) * GROUP)
+        parts = []
+        for h in range(CHEADS):
+            q = triple[h * head : (h + 1) * head, lanes]
+            k = triple[CD + h * head : CD + (h + 1) * head, lanes]
+            v = triple[2 * CD + h * head : 2 * CD + (h + 1) * head, lanes]
+            scores = jnp.where(valid, to_compact(dot_tn(k, q), own) * head**-0.5, NEG_FILL)
+            powers = jnp.exp(scores - jnp.max(scores, axis=0, keepdims=True))
+            powers = jnp.where(valid, powers, 0.0)
+            total = jnp.sum(powers, axis=0, keepdims=True)
+            probs = powers / jnp.where(total > 0, total, 1.0)
+            keep_probs[h * SLOTS : (h + 1) * SLOTS, lanes] = probs
+            parts.append(dot_nn(v, from_compact(probs, own)).astype(jnp.bfloat16))
+        mixed.append(jnp.concatenate(parts, axis=0))
+    mixed = jnp.concatenate(mixed, axis=1)
+    keep_mixed[...] = mixed
+    first = embedded + dot_nn(out_ref[...], mixed)
+    keep_first[...] = first
+    act_two = (column_rms(first)[0] * g2_ref[...]).astype(jnp.bfloat16)
+    branch = None
+    for c in range(CFF // CD):
+        rows = slice(c * CD, (c + 1) * CD)
+        hidden, slope = gelu_pair(dot_nn(up_ref[rows, :], act_two))
+        hidden = hidden.astype(jnp.bfloat16)
+        keep_hidden[rows, :] = hidden
+        keep_slope[rows, :] = slope.astype(jnp.bfloat16)
+        part = dot_nn(down_ref[:, rows], hidden)
+        branch = part if branch is None else branch + part
+    high, low = split_two(first + branch)
+    pooled_ref[...] += dot_nt(word_map, high) + dot_nt(word_map, low)
+
+
+KEPT = (
+    (3 * CD, jnp.bfloat16),
+    (CHEADS * SLOTS, jnp.float32),
+    (CD, jnp.bfloat16),
+    (CD, jnp.float32),
+    (CFF, jnp.bfloat16),
+    (CFF, jnp.bfloat16),
+)
+
+
+def whole(array):
+    zeros = (0,) * array.ndim
+    return pl.BlockSpec(array.shape, lambda *_: zeros)
+
+
+def kept_place(step, tiles):
+    return 0, jnp.minimum(step, tiles[0] - 1)
+
+
+def char_fwd(tiles, pack, weights, words):
+    rows = words * SLOTS
+    operands = (pack,) + weights
+    return pl.pallas_call(
+        char_fwd_kernel,
+        grid_spec=pltpu.PrefetchScalarGridSpec(
+            num_scalar_prefetch=1,
+            grid=(rows // ROWS,),
+            in_specs=[whole(a) for a in operands],
+            out_specs=[pl.BlockSpec((words, CD), lambda t, n: (0, 0))]
+            + [pl.BlockSpec((depth, ROWS), kept_place) for depth, _ in KEPT],
+        ),
+        out_shape=[jax.ShapeDtypeStruct((words, CD), jnp.float32)]
+        + [jax.ShapeDtypeStruct((depth, rows), dtype) for depth, dtype in KEPT],
+        compiler_params=pltpu.CompilerParams(vmem_limit_bytes=VMEM_BYTES),
+        name="char_fwd",
+    )(tiles, *operands)
+
+
+def fold_lanes(values):
+    total = values[:, :GROUP]
+    for g in range(1, values.shape[1] // GROUP):
+        total = total + values[:, g * GROUP : (g + 1) * GROUP]
+    return total
+
+
+def column_rms_back(grad_in, gain, normed, inverse):
+    scaled = grad_in * gain
+    return inverse * (scaled - normed * jnp.mean(scaled * normed, axis=0, keepdims=True))
+
+
+def char_bwd_kernel(tiles_ref, *refs):
+    @pl.when(pl.program_id(0) < tiles_ref[0])
+    def _():
+        char_bwd_tile(*refs)
+
+
+def char_bwd_tile(
+    pack_ref, spread_ref, table_ref, qkv_ref, out_ref, up_ref, down_ref, g1_ref, g2_ref,
+    keep_qkv, keep_probs, keep_mixed, keep_first, keep_hidden, keep_slope,
+    d_table, d_qkv, d_out, d_up, d_down, d_g1, d_g2,
+):
+    step = pl.program_id(0)
+    words = spread_ref.shape[1]
+    per = ROWS // GROUP
+    head = CD // CHEADS
+
+    @pl.when(step == 0)
+    def _():
+        for ref in (d_table, d_qkv, d_out, d_up, d_down, d_g1, d_g2):
+            ref[...] = jnp.zeros_like(ref)
+
+    one_hot, word_map = tile_maps(pack_ref, step, words)
+    halves = dot_nn(spread_ref[...], word_map)
+    grad_second = halves[:CD] + halves[CD:]
     grad_branch = grad_second.astype(jnp.bfloat16)
-    grad_down = matmul_tn(state["char_hidden"], grad_branch)
-    grad_hidden = matmul_nt(grad_branch, char_down_low)
-    grad_upper = (grad_hidden * gelu_slope(state["char_upper"])).astype(jnp.bfloat16)
-    grad_up = matmul_tn(state["act_two"], grad_upper)
-    grad_act_two = matmul_nt(grad_upper, char_in_low[:, 4 * CD : 4 * CD + CFF])
-    back_two, grad_gain_two = rms_backward(
-        grad_act_two, gain_two, state["normed_two"], state["inverse_two"]
-    )
-    grad_first = grad_second + back_two
-    grad_attn_in = grad_first.astype(jnp.bfloat16)
-    grad_out_proj = matmul_tn(state["mixed_flat"], grad_attn_in)
-    grad_mixed = matmul_nt(grad_attn_in, char_in_low[:, 3 * CD : 4 * CD]).astype(jnp.bfloat16)
-    grad_mixed = grad_mixed.reshape(word_total, char_count, CHEADS, head_size)
-    triple = state["char_triple"]
-    grad_triple = attend_backward(
-        triple[:, :, 0],
-        triple[:, :, 1],
-        triple[:, :, 2],
-        state["key_mask"][:, None, None, :],
-        state["char_lse"],
-        grad_mixed,
-    )
-    grad_triple = grad_triple.astype(jnp.bfloat16).reshape(row_total, 3 * CD)
-    grad_triple_proj = matmul_tn(state["act_one"], grad_triple)
-    grad_act_one = matmul_nt(grad_triple, char_in_low[:, : 3 * CD])
-    back_one, grad_gain_one = rms_backward(
-        grad_act_one, gain_one, state["normed_one"], state["inverse_one"]
-    )
+    first = keep_first[...]
+    normed_two, inverse_two = column_rms(first)
+    act_two = (normed_two * g2_ref[...]).astype(jnp.bfloat16)
+    grad_act_two = None
+    for c in range(CFF // CD):
+        rows = slice(c * CD, (c + 1) * CD)
+        d_down[rows, :] += dot_nt(keep_hidden[rows, :], grad_branch)
+        grad_upper = dot_nn(down_ref[rows, :], grad_branch) * keep_slope[rows, :].astype(
+            jnp.float32
+        )
+        grad_upper = grad_upper.astype(jnp.bfloat16)
+        d_up[:, rows] += dot_nt(act_two, grad_upper)
+        part = dot_nn(up_ref[:, rows], grad_upper)
+        grad_act_two = part if grad_act_two is None else grad_act_two + part
+    d_g2[...] += fold_lanes(grad_act_two * normed_two)
+    grad_first = grad_second + column_rms_back(
+        grad_act_two, g2_ref[...], normed_two, inverse_two
+    )
+    grad_attn = grad_first.astype(jnp.bfloat16)
+    d_out[...] += dot_nt(keep_mixed[...], grad_attn)
+    grad_mixed = dot_nn(out_ref[...], grad_attn).astype(jnp.bfloat16)
+    own = own_block()
+    triple = keep_qkv[...]
+    columns = []
+    for g in range(per):
+        lanes = slice(g * GROUP, (g + 1) * GROUP)
+        gq, gk, gv = [], [], []
+        for h in range(CHEADS):
+            q = triple[h * head : (h + 1) * head, lanes]
+            k = triple[CD + h * head : CD + (h + 1) * head, lanes]
+            v = triple[2 * CD + h * head : 2 * CD + (h + 1) * head, lanes]
+            grad_o = grad_mixed[h * head : (h + 1) * head, lanes]
+            probs = keep_probs[h * SLOTS : (h + 1) * SLOTS, lanes]
+            grad_probs = to_compact(dot_tn(v, grad_o), own)
+            grad_scores = probs * (
+                grad_probs - jnp.sum(probs * grad_probs, axis=0, keepdims=True)
+            )
+            grad_raw = from_compact(grad_scores * head**-0.5, own)
+            gq.append(dot_nn(k, grad_raw).astype(jnp.bfloat16))
+            gk.append(dot_nt(q, grad_raw).astype(jnp.bfloat16))
+            gv.append(dot_nt(grad_o, from_compact(probs, own)).astype(jnp.bfloat16))
+        columns.append(jnp.concatenate(gq + gk + gv, axis=0))
+    grad_triple = jnp.concatenate(columns, axis=1)
+    embedded = dot_nn(table_ref[...], one_hot)
+    normed_one, inverse_one = column_rms(embedded)
+    act_one = (normed_one * g1_ref[...]).astype(jnp.bfloat16)
+    d_qkv[...] += dot_nt(act_one, grad_triple)
+    grad_act_one = dot_nn(qkv_ref[...], grad_triple)
+    d_g1[...] += fold_lanes(grad_act_one * normed_one)
+    back_one = column_rms_back(grad_act_one, g1_ref[...], normed_one, inverse_one)
     grad_embedded = (grad_first + back_one).astype(jnp.bfloat16)
-    grad_table = matmul_tn(state["one_hot"], grad_embedded)
-    return (
-        grad_table,
-        grad_triple_proj,
-        grad_out_proj,
-        grad_up,
-        grad_down,
-        grad_gain_one,
-        grad_gain_two,
-    )
+    d_table[...] += dot_nt(one_hot, grad_embedded)
+
+
+def char_bwd(tiles, pack, spread, weights, kept):
+    operands = (pack, spread) + weights
+    shapes = ((CV, CD), (CD, 3 * CD), (CD, CD), (CD, CFF), (CFF, CD), (CD, GROUP), (CD, GROUP))
+    return pl.pallas_call(
+        char_bwd_kernel,
+        grid_spec=pltpu.PrefetchScalarGridSpec(
+            num_scalar_prefetch=1,
+            grid=(kept[0].shape[1] // ROWS,),
+            in_specs=[whole(a) for a in operands]
+            + [pl.BlockSpec((depth, ROWS), kept_place) for depth, _ in KEPT],
+            out_specs=[pl.BlockSpec(s, lambda t, n: (0, 0)) for s in shapes],
+        ),
+        out_shape=[jax.ShapeDtypeStruct(s, jnp.float32) for s in shapes],
+        compiler_params=pltpu.CompilerParams(vmem_limit_bytes=VMEM_BYTES),
+        name="char_bwd",
+    )(tiles, *operands, *kept)
 
 
 def adam_step(weight, grad, first_old, second_old, clip_factor, rate, decay):
@@ -270,10 +534,31 @@
     seq_count, local_words = (words_in.shape[0], words_in.shape[1])
     word_total = seq_count * local_words
     head_size = D // HEADS
-    char_state = char_forward(
-        char_ids, char_counts, language, table_low, char_in_low, char_down_low, gain_one, gain_two
-    )
-    word_vector = matmul(char_state["pooled"], char_in_low[:, 4 * CD + CFF :])
+    packed, tiles = pack_rows(char_ids, char_counts)
+    tables = table_low.reshape(-1, CV, CD)
+    lanes = lambda g: jnp.broadcast_to(g[:, None], (g.shape[0], ROWS))
+    gains = (lanes(gain_one), lanes(gain_two))
+    table_t = [
+        lax.dynamic_index_in_dim(tables, language[i], 0, keepdims=False).T
+        for i in range(seq_count)
+    ]
+    char_parts = (
+        char_in_low[:, : 3 * CD],
+        char_in_low[:, 3 * CD : 4 * CD],
+        char_in_low[:, 4 * CD : 4 * CD + CFF],
+        char_down_low,
+    )
+    flipped = tuple(part.T for part in char_parts)
+    kept, pooled = [], []
+    for i in range(seq_count):
+        first_out, *saved = char_fwd(
+            tiles[i : i + 1], packed[i], (table_t[i],) + flipped + gains, local_words
+        )
+        pooled.append(first_out)
+        kept.append(saved)
+    counts = char_counts.reshape(word_total, 1).astype(jnp.float32)
+    pooled = (jnp.concatenate(pooled, axis=0) / counts).astype(jnp.bfloat16)
+    word_vector = matmul(pooled, char_in_low[:, 4 * CD + CFF :])
     word_start = words_in.reshape(word_total, D).astype(jnp.float32) + word_vector
     scaled_three, normed_three, inverse_three = rms_forward(word_start, gain_three)
     act_three = scaled_three.astype(jnp.bfloat16)
@@ -326,18 +611,30 @@
     grad_start = grad_after + back_three
     input_grad = grad_start.reshape(seq_count, local_words, D)
     grad_vector = grad_start.astype(jnp.bfloat16)
-    grad_pool = matmul_tn(char_state["pooled"], grad_vector)
+    grad_pool = matmul_tn(pooled, grad_vector)
     grad_pooled = matmul_nt(grad_vector, char_in_low[:, 4 * CD + CFF :])
-    fresh_in = lax.optimization_barrier((grad_pooled, table_low, char_in_low, char_down_low))
-    recent = char_forward(
-        char_ids, char_counts, language, fresh_in[1], fresh_in[2], fresh_in[3], gain_one, gain_two
-    )
-    char_grads = char_backward(
-        recent, grad_pooled, char_counts, char_in_low, char_down_low, gain_one, gain_two
-    )
-    grad_table, grad_ctriple, grad_cout, grad_cup, grad_cdown, grad_gain_one, grad_gain_two = (
-        char_grads
-    )
+    scaled_pooled = (grad_pooled / counts).reshape(seq_count, local_words, CD)
+    char_grads = []
+    grad_table = jnp.zeros((tables.shape[0], CV, CD), jnp.float32)
+    for i in range(seq_count):
+        high, low = split_two(scaled_pooled[i].T)
+        one_table, *rest = char_bwd(
+            tiles[i : i + 1],
+            packed[i],
+            jnp.concatenate([high, low], axis=0),
+            (table_t[i],) + char_parts + gains,
+            kept[i],
+        )
+        char_grads.append(rest)
+        grad_table = grad_table + jnp.where(
+            (jnp.arange(tables.shape[0]) == language[i])[:, None, None], one_table[None], 0.0
+        )
+    grad_table = grad_table.reshape(-1, CD)
+    grad_ctriple, grad_cout, grad_cup, grad_cdown, grad_gain_one, grad_gain_two = (
+        sum(parts[1:], parts[0]) for parts in zip(*char_grads)
+    )
+    grad_gain_one = jnp.sum(grad_gain_one, axis=1)
+    grad_gain_two = jnp.sum(grad_gain_two, axis=1)
     grad_cin = jnp.concatenate([grad_ctriple, grad_cout, grad_cup, grad_pool], axis=1)
     grad_win = jnp.concatenate([grad_wtriple, grad_wout, grad_wup], axis=1)
     gain_grads = jnp.concatenate([grad_gain_one, grad_gain_two, grad_gain_three, grad_gain_four])

time: 1370 us -> 940 us (0.69)
  local copies, waits for them, and re-layouts: 379 us -> 90 us
  matrix products: 404 us -> 117 us
  Pallas kernels: 0 us -> 177 us
  other arithmetic: 82 us -> 47.3 us
    pallas_call x0 -> x5, Pallas kernels: none -> 177 us  [the longest x2 92.9 us: char_bwd(): pl.pallas_call(char_bwd_kernel, grid_spec=pltpu.PrefetchScalarGridSpec(nu...]
    reshape x5 -> x1, local copies, waits for them, and re-layouts: 111 us -> 0.37 us  [body(): tables = table_low.reshape(-1, CV, CD)]
    convert_element_type x5 -> x0, local copies, waits for them, and re-layouts: 87.5 us -> none  [the longest x1 35.6 us: char_backward(): grad_triple = grad_triple.astype(jnp.bfloat16).reshape(row_total, 3 * CD)]
    dot_general x14 -> x5, matrix products: 96 us -> 14.5 us  [matmul(): return jnp.dot(left_side, right_side, preferred_element_type=jnp.float32)]
    dot_general x10 -> x5, matrix products: 72.5 us -> 12.4 us  [matmul_tn(): lax.dot_general(left_side, right_side, (((0,), (0,)), ((), ())), preferre...]
    dot_general x9 -> x5, matrix products: 58.3 us -> 12.3 us  [matmul_nt(): lax.dot_general(left_side, right_side, (((1,), (1,)), ((), ())), preferre...]
    dot_general x4 -> x0, local copies, waits for them, and re-layouts: 40.8 us -> none  [the longest x2 20.5 us: score_block(): jnp.einsum('bqhd,bkhd->bhqk', queries, key_rows, preferred_element_type=j...]
    slice x2 -> x5, local copies, waits for them, and re-layouts: 43.7 us -> 8.02 us  [the longest x1 2.02 us: body(): char_in_low[:, 4 * CD:4 * CD + CFF]]
  transfers between devices with their start and end apart: 7 -> 7, of which waited for: 3 -> 3; matrix products, arithmetic and copies ran while one was open for 16% -> 8% of each run, Pallas kernels for 0% -> 9%
where the time goes in v1:
time: 940 us; the launch traced here: 929 us
  waiting for transfers between devices  279 us (30%)
  blocking collectives  182 us (19%)
  Pallas kernels  177 us (19%)
  matrix products  117 us (12%)
  local copies, waits for them, and re-layouts  90 us (10%)
  other arithmetic  47.3 us (5%)
  between operations  24.2 us (3%)
  starting transfers between devices  12.6 us (1%)
    psum x1, waiting for transfers between devices, body(): lax.psum((grad_table, grad_cin, grad_cdown, grad_win, grad_wdown, gain_gr...  242 us
    pallas_call x2, Pallas kernels, char_bwd(): pl.pallas_call(char_bwd_kernel, grid_spec=pltpu.PrefetchScalarGridSpec(nu...  92.9 us
    pallas_call x2, Pallas kernels, char_fwd(): pl.pallas_call(char_fwd_kernel, grid_spec=pltpu.PrefetchScalarGridSpec(nu...  80.3 us
    all_gather x1, blocking collectives, body(): lax.all_gather(word_down.astype(jnp.bfloat16), 'head', axis=1, tiled=True)  43.3 us
    psum x1, blocking collectives, body(): lax.psum((grad_table, grad_cin, grad_cdown, grad_win, grad_wdown, gain_gr...  39.3 us
    unnamed x149, local copies, waits for them, and re-layouts  27.1 us
    dot_general x1, matrix products, attend_backward(): jnp.einsum('bhqk,bqhd->bkhd', grad_raw, queries, preferred_element_type=j...  25 us
    dot_general x1, matrix products, attend_backward(): jnp.einsum('bhqk,bkhd->bqhd', grad_raw, key_rows, preferred_element_type=...  24.8 us
  transfers between devices with their start and end apart: 7, of which 3 were waited for; matrix products, arithmetic and copies ran while one was open for 8% of the time, Pallas kernels for 9%

profile of v1, /device:TPU:0, one launch (start us, length us, event | category | flops | bytes accessed | tf_op | source)
XLA Modules:
  0.0 929.0 jit_solution(16624621878221494201)
XLA Ops:
  8.2 16.0 %all_gather.32 = bf16[32,2560]{1,0:T(8,128)(2,1)} all-gather(bf16[32,640]{1,0:T(8,128)(2,1)S(1)} %convert_element_type.121), channel_id=1, replica_groups=mesh['dp'=8,'head'=4] {'head'}, dimensions={1}, use_global_device_ids=true | all-gather | bytes 204800 | tf_op jit(solution)/shard_map/all_gather | solution.py:518
  25.2 16.7 %all_gather.36 = bf16[64,4096]{1,0:T(8,128)(2,1)} all-gather(bf16[64,1024]{1,0:T(8,128)(2,1)S(1)} %convert_element_type.127), channel_id=1, replica_groups=mesh['dp'=8,'head'=4] {'head'}, dimensions={1}, use_global_device_ids=true | all-gather | bytes 655360 | tf_op jit(solution)/shard_map/all_gather | solution.py:520
  52.6 13.1 %all_gather.30 = bf16[128,256]{0,1:T(8,128)(2,1)S(1)} all-gather(bf16[128,64]{0,1:T(8,128)(2,1)S(1)} %convert_element_type.120), channel_id=1, replica_groups=mesh['dp'=8,'head'=4] {'head'}, dimensions={1}, use_global_device_ids=true | all-gather | bytes 81920 | tf_op jit(solution)/shard_map/all_gather | solution.py:517
  65.7 10.0 %all_gather.31 = bf16[1024,256]{0,1:T(8,128)(2,1)S(1)} all-gather(bf16[128,256]{0,1:T(8,128)(2,1)S(1)} %all_gather.30), channel_id=1, replica_groups=mesh['dp'=8,'head'=4] {'dp'}, dimensions={0}, use_global_device_ids=true | all-gather | bytes 589824 | tf_op jit(solution)/shard_map/all_gather | solution.py:524
  76.1 13.1 %all_gather.34 = bf16[128,256]{0,1:T(8,128)(2,1)S(1)} all-gather(bf16[128,64]{0,1:T(8,128)(2,1)S(1)} %convert_element_type.122), channel_id=1, replica_groups=mesh['dp'=8,'head'=4] {'head'}, dimensions={1}, use_global_device_ids=true | all-gather | bytes 81920 | tf_op jit(solution)/shard_map/all_gather | solution.py:519
  89.3 10.0 %all_gather.35.refs_6_ = bf16[1024,256]{1,0:T(8,128)(2,1)S(1)} all-gather(bf16[128,256]{1,0:T(8,128)(2,1)S(1)} %copy.193), channel_id=1, replica_groups=mesh['dp'=8,'head'=4] {'dp'}, dimensions={0}, use_global_device_ids=true | all-gather | bytes 589824 | tf_op jit(solution)/shard_map/all_gather | solution.py:526
  101.6 3.4 pack.1
  118.9 38.3 %char_fwd.3 = (f32[256,256]{1,0:T(8,128)}, bf16[768,4096]{1,0:T(8,128)(2,1)}, f32[64,4096]{1,0:T(8,128)}, bf16[256,4096]{1,0:T(8,128)(2,1)}, f32[256,4096]{1,0:T...) custom-call(s32[1]{0:T(128)} %get-tuple-element.286.tiles_ref, ...), custom_call_target="tpu_custom_call" | custom-call | tf_op jit(solution)/shard_map/char_fwd/pallas_call | solution.py:356
  158.3 42.0 %char_fwd.2 = (f32[256,256]{1,0:T(8,128)}, bf16[768,4096]{1,0:T(8,128)(2,1)}, f32[64,4096]{1,0:T(8,128)}, bf16[256,4096]{1,0:T(8,128)(2,1)}, f32[256,4096]{1,0:T...) custom-call(s32[1]{0:T(128)} %get-tuple-element.285.tiles_ref, ...), custom_call_target="tpu_custom_call" | custom-call | tf_op jit(solution)/shard_map/char_fwd/pallas_call | solution.py:356
  203.8 3.6 convolution_convert_fusion
  207.3 4.0 reshape.187
  211.3 3.9 copy.206
  215.2 3.6 all-to-all-start
  218.8 43.3 %all_gather.38 = bf16[256,512]{1,0:T(8,128)(2,1)} all-gather(bf16[256,128]{1,0:T(8,128)(2,1)S(1)} %convert_element_type.134), channel_id=1, replica_groups=mesh['dp'=8,'head'=4] {'head'}, dimensions={1}, use_global_device_ids=true | all-gather | bytes 327680 | tf_op jit(solution)/shard_map/all_gather | solution.py:521
  265.9 4.8 fusion.3
  270.7 3.7 fusion.2
  276.4 5.0 fusion.57
  283.1 20.1 %all_to_all.66 = bf16[4,2,32768]{2,1,0:T(2,128)(2,1)S(1)} all-to-all(bf16[4,2,32768]{2,1,0:T(2,128)(2,1)S(1)} %reshape.188), channel_id=1, replica_groups=mesh['dp'=8,'head'=4] {'head'}, dimensions={0} | all-to-all | bytes 1048576 | tf_op jit(solution)/shard_map/all_to_all | solution.py:571
  307.8 3.6 multiply_convert_fusion.1
  311.5 4.6 fusion.38
  323.6 4.3 all-to-all-start.2
  328.0 14.1 %all-to-all-done.2 = bf16[2,256,8,64]{1,0,3,2:T(2,128)(2,1)} async-done(((bf16[2,256,8,64]{1,0,3,2:T(2,128)(2,1)}), bf16[2,256,8,64]{1,0,3,2:T(2,128)(2,1)}, u32[]{:S(2)}, u32[]{:S(2)}) %all-to-all-start.2) | async-done | bytes 524320 | tf_op jit(solution)/shard_map/all_to_all | solution.py:593
  342.0 2.2 copy.260
  344.3 2.2 all_to_all.58
  346.5 9.5 %fusion.69 = f32[2,2,1024,1024]{2,3,1,0:T(8,128)} fusion(bf16[2,1024,2,64]{1,3,2,0:T(8,128)(2,1)} %all_to_all.58, bf16[2,1024,3,2,64]{1,4,3,0,2:T(8,128)(2,1)} %copy-done.11), kind=kOutput, calls=%fused_computation.84 | convolution fusion | flops 536870912 | bytes 17825792 | tf_op jit(solution)/shard_map/bqhd,bkhd->bhqk/dot_general | solution.py:100
  355.9 8.9 fusion.64
  364.9 25.0 %fusion.58 = bf16[2,1024,1,2,64]{1,4,3,0,2:T(8,128)(2,1)} fusion(f32[2,2,1024,1024]{2,3,1,0:T(8,128)} %fusion.69, f32[2,2,1024,1024]{2,3,1,0:T(8,128)} %copy-done, f32[2,2,1024]{2,1,0:T(2,128)S(1)} %log_add_fusion, pred[1024,1024]{0,1:T(8,128)(4,1)} %iota_compare_fusion, bf16[2,1024,3,2,64]{1,4,3,0,2:T(8,128)(2,1)} %copy-done.11), kind=kOutput, calls=%fused_computation.59 | convolution fusion | flops 583275520 | bytes 70287360 | tf_op jit(solution)/shard_map/bhqk,bqhd->bkhd/dot_general | solution.py:116
  389.9 24.8 %fusion.61 = bf16[2,1024,1,2,64]{1,4,3,0,2:T(8,128)(2,1)} fusion(f32[2,2,1024,1024]{2,3,1,0:T(8,128)} %fusion.69, f32[2,2,1024,1024]{2,3,1,0:T(8,128)} %copy-done, f32[2,2,1024]{2,1,0:T(2,128)S(1)} %log_add_fusion, pred[1024,1024]{0,1:T(8,128)(4,1)} %iota_compare_fusion, bf16[2,1024,3,2,64]{1,4,3,0,2:T(8,128)(2,1)} %copy-done.11), kind=kOutput, calls=%fused_computation.60 | convolution fusion | flops 583275520 | bytes 70287360 | tf_op jit(solution)/shard_map/bhqk,bkhd->bqhd/dot_general | solution.py:113
  414.8 2.7 pad_maximum_fusion.2
  417.5 8.5 copy.216
  425.9 5.1 reshape.190
  431.0 4.4 all-to-all-start.3
  437.7 2.4 fusion.77
  440.1 5.1 fusion.128
  445.2 3.4 fusion.104
  448.6 23.2 %all-to-all-done.3 = bf16[4,2,98304]{2,1,0:T(2,128)(2,1)} async-done(((bf16[4,2,98304]{2,1,0:T(2,128)(2,1)}), bf16[4,2,98304]{2,1,0:T(2,128)(2,1)}, u32[]{:S(2)}, u32[]{:S(2)}) %all-to-all-start.3) | async-done | bytes 1572896 | tf_op jit(solution)/shard_map/all_to_all | solution.py:602
  471.9 4.9 reshape.191
  476.8 8.7 copy.217
  488.5 3.2 multiply_reduce_fusion.5
  495.8 44.3 %char_bwd.3 = (f32[256,256]{1,0:T(8,128)}, f32[256,768]{1,0:T(8,128)}, f32[256,256]{1,0:T(8,128)}, f32[256,1024]{1,0:T(8,128)}, f32[1024,256]{1,0:T(8,128)}, /*index=5*/f32[256,128]{1,0:T(8,128)}, f32[256,128]{1,0:T(8,128)}) custom-call(s32[1]{0:T(128)} %get-tuple-element.286.tiles_ref, s32[4,32,128]{2,1,0:T(8,128)} %get-tuple-element.278.refs_0_, ...), custom_call_target="tpu_custom_call" | custom-call | tf_op jit(solution)/shard_map/char_bwd/pallas_call | solution.py:466
  540.2 48.6 %char_bwd.2 = (f32[256,256]{1,0:T(8,128)}, f32[256,768]{1,0:T(8,128)}, f32[256,256]{1,0:T(8,128)}, f32[256,1024]{1,0:T(8,128)}, f32[1024,256]{1,0:T(8,128)}, /*index=5*/f32[256,128]{1,0:T(8,128)}, f32[256,128]{1,0:T(8,128)}) custom-call(s32[1]{0:T(128)} %get-tuple-element.285.tiles_ref, s32[4,32,128]{2,1,0:T(8,128)} %get-tuple-element.277.refs_0_, ...), custom_call_target="tpu_custom_call" | custom-call | tf_op jit(solution)/shard_map/char_bwd/pallas_call | solution.py:466
  593.4 3.8 pad_maximum_fusion
  602.6 3.7 fusion.55
  606.7 39.3 %psum.47 = f32[1536]{0:T(1024)S(1)} all-reduce(f32[1536]{0:T(1024)S(1)} %pad_maximum_fusion.5), channel_id=1, replica_groups=mesh['dp'=8,'head'=4] {'dp','head'}, use_global_device_ids=true, to_apply=%region_21.22 | all-reduce | flops 1536 | bytes 12288 | tf_op jit(solution)/shard_map/psum | solution.py:642
  646.5 242.0 %all-reduce.3.cloned.1.call-done = (f32[1024,256]{1,0:T(8,128)}, f32[256,2560]{1,0:T(8,128)}, f32[1024,256]{1,0:T(8,128)}, f32[512,4096]{1,0:T(8,128)}, f32[2048,512]{1,0:T(8,128)}) async-done(((f32[1024,256]{1,0:T(8,128)}, f32[256,2560]{1,0:T(8,128)}, f32[1024,256]{1,0:T(8,128)}, f32[512,4096]{1,0:T(8,128)}, f32[2048,512]{1,0:T(8,128)}), (f32[1024,256]{1,0:T(8,128)}, f32[256,2560]{1,0:T(8,128)}, ...) | async-done | bytes 17301520 | tf_op jit(solution)/shard_map/psum | solution.py:642
  888.6 2.2 multiply_reduce_fusion.7
  890.8 3.0 multiply_reduce_fusion.3
  894.6 6.3 multiply_reduce_fusion.1
  (240 shorter events, 86.3 us)
Async XLA Ops:
  7.2 93.1 %copy-start.54 = (s32[2,256]{1,0:T(2,128)S(1)}, s32[2,256]{1,0:T(2,128)}, u32[]{:S(2)}) copy-start(s32[2,256]{1,0:T(2,128)} %param.24) | copy-start | bytes 6148
  7.2 68.8 %copy-start.40 = (f32[128,64]{0,1:T(8,128)S(1)}, f32[128,64]{0,1:T(8,128)}, u32[]{:S(2)}) copy-start(f32[128,64]{0,1:T(8,128)} %param.30) | copy-start | bytes 98308
  7.2 102.0 %all-gather.4.cloned.1.call-start = ((), (), s32[]{:S(2)}) async-start(), calls=%async_computation.4 | async-start | bytes 1474560 | tf_op jit(solution)/shard_map/all_gather | solution.py:525
  24.2 178.7 %all-gather.6.cloned.1.call-start = ((), (), s32[]{:S(2)}) async-start(), calls=%async_computation.5 | async-start | bytes 4718592 | tf_op jit(solution)/shard_map/all_gather | solution.py:527
  25.2 81.7 %copy-start.52 = (f32[1536]{0:T(1024)S(1)}, f32[1536]{0:T(1024)}, u32[]{:S(2)}) copy-start(f32[1536]{0:T(1024)} %param.33) | copy-start | bytes 18436
  99.3 18.0 %copy-start.4 = (bf16[1024,256]{1,0:T(8,128)(2,1)}, bf16[1024,256]{1,0:T(8,128)(2,1)S(1)}, u32[]{:S(2)}) copy-start(bf16[1024,256]{1,0:T(8,128)(2,1)S(1)} %all_gather.35.refs_6_) | copy-start | bytes 1572868
  100.3 101.0 %copy-start.60 = (f32[1,2,2,128]{3,1,2,0:T(2,128)}, f32[1,2,2,128]{3,1,2,0:T(2,128)S(1)}, u32[]{:S(2)}) copy-start(f32[1,2,2,128]{3,1,2,0:T(2,128)S(1)} %copy.252) | copy-start | bytes 6148
  114.3 87.1 %copy-start.62 = (bf16[2,256,512]{2,1,0:T(8,128)(2,1)S(1)}, bf16[2,256,512]{2,1,0:T(8,128)(2,1)}, u32[]{:S(2)}) copy-start(bf16[2,256,512]{2,1,0:T(8,128)(2,1)} %param.26) | copy-start | bytes 1572868
  211.3 7.5 copy-start.25
  215.2 48.3 %all-to-all-start = ((bf16[2,256,3,8,64]{1,0,4,2,3:T(2,128)(2,1)}), bf16[2,256,3,8,64]{1,0,4,2,3:T(2,128)(2,1)S(1)}, u32[]{:S(2)}, u32[]{:S(2)}) async-start(bf16[2,256,3,8,64]{1,0,4,2,3:T(2,128)(2,1)} %copy.206), calls=%async_computation | async-start | bytes 3145728 | tf_op jit(solution)/shard_map/all_to_all | solution.py:567
  218.8 92.7 %all-gather.8.cloned.1.call-start = ((), (), s32[]{:S(2)}) async-start(), calls=%async_computation.6 | async-start | bytes 2359296 | tf_op jit(solution)/shard_map/all_gather | solution.py:528
  265.8 8.5 copy-start.11
  265.8 4.8 copy-start.8
  270.7 5.8 copy-start
  281.4 24.2 %copy-start.3 = (f32[512,512]{1,0:T(8,128)S(1)}, f32[512,512]{1,0:T(8,128)}, u32[]{:S(2)}) copy-start(f32[512,512]{1,0:T(8,128)} %copy-done.2) | copy-start | bytes 3145732
  311.5 4.6 copy-start.34
  323.6 18.4 %all-to-all-start.2 = ((bf16[2,256,8,64]{1,0,3,2:T(2,128)(2,1)}), bf16[2,256,8,64]{1,0,3,2:T(2,128)(2,1)}, u32[]{:S(2)}, u32[]{:S(2)}) async-start(bf16[2,256,8,64]{1,0,3,2:T(2,128)(2,1)} %reshape.183), calls=%async_computation.2 | async-start | bytes 1048576 | tf_op jit(solution)/shard_map/all_to_all | solution.py:593
  346.5 9.5 %copy-start.9 = (pred[1024,1024]{0,1:T(8,128)(4,1)S(1)}, pred[1024,1024]{0,1:T(8,128)(4,1)}, u32[]{:S(2)}) copy-start(pred[1024,1024]{0,1:T(8,128)(4,1)} %iota_compare_fusion) | copy-start | bytes 3145732
  346.5 9.5 %copy-start.12 = (bf16[2,1024,2,64]{1,3,2,0:T(8,128)(2,1)S(1)}, bf16[2,1024,2,64]{1,3,2,0:T(8,128)(2,1)}, u32[]{:S(2)}) copy-start(bf16[2,1024,2,64]{1,3,2,0:T(8,128)(2,1)} %all_to_all.58) | copy-start | bytes 1572868
  431.0 40.9 %all-to-all-start.3 = ((bf16[4,2,98304]{2,1,0:T(2,128)(2,1)}), bf16[4,2,98304]{2,1,0:T(2,128)(2,1)}, u32[]{:S(2)}, u32[]{:S(2)}) async-start(bf16[4,2,98304]{2,1,0:T(2,128)(2,1)} %reshape.190), calls=%async_computation.3 | async-start | bytes 3145728 | tf_op jit(solution)/shard_map/all_to_all | solution.py:602
  435.4 453.2 %all-reduce.3.cloned.1.call-start = ((), (), s32[]{:S(2)}) async-start(), calls=%async_computation.7 | async-start | bytes 34603008 | tf_op jit(solution)/shard_map/psum | solution.py:642
  440.1 5.1 copy-start.16
  492.6 47.5 %copy-start.18 = (f32[512,512]{1,0:T(8,128)}, f32[512,512]{1,0:T(8,128)S(1)}, u32[]{:S(2)}) copy-start(f32[512,512]{1,0:T(8,128)S(1)} %multiply_add_fusion) | copy-start | bytes 3145732
  540.1 48.6 %copy-start.20 = (f32[256,1024]{1,0:T(8,128)S(1)}, f32[256,1024]{1,0:T(8,128)}, u32[]{:S(2)}) copy-start(f32[256,1024]{1,0:T(8,128)} %get-tuple-element.86) | copy-start | bytes 3145732
  540.2 50.2 %copy-start.30 = (f32[256,256]{1,0:T(8,128)S(1)}, f32[256,256]{1,0:T(8,128)}, u32[]{:S(2)}) copy-start(f32[256,256]{1,0:T(8,128)} %get-tuple-element.84) | copy-start | bytes 786436
  588.8 4.6 copy-start.1
  588.8 4.5 copy-start.7
  593.3 3.9 copy-start.36
  593.3 3.9 copy-start.57
  602.6 3.9 copy-start.42
  602.6 3.9 copy-start.44
  602.6 4.0 copy-start.58
  602.6 4.0 copy-start.59
  645.9 268.8 %copy-start.48 = (f32[1536]{0:T(1024)}, f32[1536]{0:T(1024)S(1)}, u32[]{:S(2)}) copy-start(f32[1536]{0:T(1024)S(1)} %psum.47) | copy-start | bytes 18436
  888.6 5.2 copy-start.17
  894.6 6.4 copy-start.6
  900.9 13.9 %copy-start.53 = (f32[1536]{0:T(1024)S(1)}, f32[1536]{0:T(1024)}, u32[]{:S(2)}) copy-start(f32[1536]{0:T(1024)} %param.33) | copy-start | bytes 18436
  900.9 13.9 %copy-start.55 = (f32[1536]{0:T(1024)S(1)}, f32[1536]{0:T(1024)}, u32[]{:S(2)}) copy-start(f32[1536]{0:T(1024)} %param.45) | copy-start | bytes 18436
  900.9 13.9 %copy-start.56 = (f32[1536]{0:T(1024)S(1)}, f32[1536]{0:T(1024)}, u32[]{:S(2)}) copy-start(f32[1536]{0:T(1024)} %param.44) | copy-start | bytes 18436
  900.9 14.5 %copy-start.27 = (f32[32,640]{1,0:T(8,128)S(1)}, f32[32,640]{1,0:T(8,128)}, u32[]{:S(2)}) copy-start(f32[32,640]{1,0:T(8,128)} %param.29) | copy-start | bytes 245764
  900.9 14.5 %copy-start.46 = (f32[32,640]{1,0:T(8,128)S(1)}, f32[32,640]{1,0:T(8,128)}, u32[]{:S(2)}) copy-start(f32[32,640]{1,0:T(8,128)} %param.37) | copy-start | bytes 245764
  900.9 14.5 %copy-start.47 = (f32[32,640]{1,0:T(8,128)S(1)}, f32[32,640]{1,0:T(8,128)}, u32[]{:S(2)}) copy-start(f32[32,640]{1,0:T(8,128)} %param.36) | copy-start | bytes 245764
  901.0 16.1 %copy-start.22 = (f32[64,1024]{1,0:T(8,128)S(1)}, f32[64,1024]{1,0:T(8,128)}, u32[]{:S(2)}) copy-start(f32[64,1024]{1,0:T(8,128)} %param.31) | copy-start | bytes 786436
  901.0 16.1 %copy-start.28 = (f32[64,1024]{1,0:T(8,128)S(1)}, f32[64,1024]{1,0:T(8,128)}, u32[]{:S(2)}) copy-start(f32[64,1024]{1,0:T(8,128)} %param.41) | copy-start | bytes 786436
  901.0 16.1 %copy-start.29 = (f32[64,1024]{1,0:T(8,128)S(1)}, f32[64,1024]{1,0:T(8,128)}, u32[]{:S(2)}) copy-start(f32[64,1024]{1,0:T(8,128)} %param.40) | copy-start | bytes 786436
  901.0 18.1 %copy-start.26 = (f32[256,128]{1,0:T(8,128)S(1)}, f32[256,128]{1,0:T(8,128)}, u32[]{:S(2)}) copy-start(f32[256,128]{1,0:T(8,128)} %param.32) | copy-start | bytes 393220
  901.0 18.1 %copy-start.37 = (f32[256,128]{1,0:T(8,128)S(1)}, f32[256,128]{1,0:T(8,128)}, u32[]{:S(2)}) copy-start(f32[256,128]{1,0:T(8,128)} %param.43) | copy-start | bytes 393220
  901.0 18.1 %copy-start.38 = (f32[256,128]{1,0:T(8,128)S(1)}, f32[256,128]{1,0:T(8,128)}, u32[]{:S(2)}) copy-start(f32[256,128]{1,0:T(8,128)} %param.42) | copy-start | bytes 393220
  (22 other events, 47.9 us)
Sparse Core Ops, SparseCore 0:
  24.3 25.7 all-gather.3
  52.0 36.7 all-gather.5
  262.3 28.7 all-gather.7
  600.6 287.9 all-reduce.2

commit v2 on v1

v2 whole, which is shorter than its diff:
```python
import functools

import jax
import jax.numpy as jnp
from jax import lax
from jax.experimental import pallas as pl
from jax.experimental.pallas import tpu as pltpu
from jax.sharding import PartitionSpec as P

D = 512
HEADS = 8
CD = 256
CHEADS = 4
CFF = 1024
CV = 256
STEP = 5


EPS = 1e-05
CLIP = 1.0
MATRIX_RATE = 0.03
GAIN_RATE = 0.25
MATRIX_DECAY = 0.1
BETA_ONE = 0.5
BETA_TWO = 0.5
ADAM_EPS = 1e-08
NEG_FILL = -1e30
SQRT_HALF = 0.7071067811865476
INV_ROOT_TWO_PI = 0.3989422804014327


ROWS = 512
SLOTS = 16
GROUP = 128
VMEM_BYTES = 56 * 1024 * 1024
ERFC_P = 0.39
ERFC = (0.235325887, 0.091384224, 0.649569841, -0.635413203, 0.886672317, -0.227539068)


def dot_nn(left_side, right_side):
    return lax.dot_general(
        left_side, right_side, (((1,), (0,)), ((), ())), preferred_element_type=jnp.float32
    )


def dot_tn(left_side, right_side):
    return lax.dot_general(
        left_side, right_side, (((0,), (0,)), ((), ())), preferred_element_type=jnp.float32
    )


def dot_nt(left_side, right_side):
    return lax.dot_general(
        left_side, right_side, (((1,), (1,)), ((), ())), preferred_element_type=jnp.float32
    )


def gelu_pair(upper):
    size = jnp.abs(upper)
    t = 1.0 / (1.0 + (ERFC_P * SQRT_HALF) * size)
    poly = ERFC[5]
    for c in ERFC[4::-1]:
        poly = poly * t + c
    bell = jnp.exp(upper * upper * -0.5)
    half = 0.5 * (poly * t * bell)
    phi = jnp.where(upper > 0, 1.0 - half, half)
    return upper * phi, phi + upper * (bell * INV_ROOT_TWO_PI)


def iota(shape, dim):
    return lax.broadcasted_iota(jnp.int32, shape, dim)


def split_two(values):
    high = values.astype(jnp.bfloat16)
    return high, (values - high.astype(jnp.float32)).astype(jnp.bfloat16)


def pack_kernel(count_row_ref, count_col_ref, ids_ref, ids_back_ref, out_ref, tiles_ref):
    row = count_row_ref[0]
    col = count_col_ref[0]
    n = row.shape[1]
    sub, lane = iota((n, n), 0), iota((n, n), 1)
    ahead = (row > col) | ((row == col) & (lane < sub))
    rank_col = jnp.sum(ahead.astype(jnp.float32), axis=1, keepdims=True).astype(jnp.int32)
    ahead = (col > row) | ((col == row) & (sub < lane))
    rank_row = jnp.sum(ahead.astype(jnp.float32), axis=0, keepdims=True).astype(jnp.int32)
    clash = (rank_col < rank_row) & (col + row > SLOTS)
    alone = jnp.max(jnp.where(clash, rank_col + rank_row, 0).astype(jnp.float32))
    alone = jnp.maximum(alone.astype(jnp.int32) - n + 2, 0)
    partner = n - 1 + alone - rank_row
    second = (rank_row >= alone) & (rank_row > partner)
    bins = jnp.where(second, partner, rank_row)
    here = sub == bins
    first_map = (here & jnp.logical_not(second)).astype(jnp.float32).astype(jnp.bfloat16)
    second_map = (here & second).astype(jnp.float32).astype(jnp.bfloat16)
    pos = lax.rem(iota((n, GROUP), 1), SLOTS)
    word = iota((n, GROUP), 0) + 1
    wide = jnp.broadcast_to(col, (n, GROUP))
    in_first, in_second = pos < wide, pos >= SLOTS - wide

    def kept(mask, values):
        return jnp.where(mask, values, 0).astype(jnp.float32).astype(jnp.bfloat16)

    groups = n * SLOTS // GROUP
    per = GROUP // SLOTS
    own = iota((groups, per, GROUP), 1) == lax.div(iota((groups, per, GROUP), 2), SLOTS)
    ids, back = ids_ref[0], ids_back_ref[0]
    zero = jnp.zeros_like(wide)
    for k, (one, two) in enumerate(
        ((ids + 1, back + 1), (word, word), (zero, SLOTS - wide), (wide, zero + SLOTS))
    ):
        full = dot_nn(first_map, kept(in_first, one)) + dot_nn(second_map, kept(in_second, two))
        full = jnp.where(own, full.reshape(groups, per, GROUP), 0.0)
        out_ref[0, k] = jnp.sum(full, axis=1).astype(jnp.int32)
    used = alone + lax.div(n - alone + 1, 2)
    tiles_ref[pl.program_id(0)] = lax.div(used * SLOTS + ROWS - 1, ROWS)


def pack_rows(char_ids, char_counts):
    seqs, words, slots = char_ids.shape
    ids = jnp.tile(char_ids, (1, 1, GROUP // slots))
    back = jnp.tile(char_ids[:, :, ::-1], (1, 1, GROUP // slots))
    groups = words * slots // GROUP
    return pl.pallas_call(
        pack_kernel,
        grid=(seqs,),
        in_specs=[
            pl.BlockSpec((1, 1, words), lambda s: (s, 0, 0)),
            pl.BlockSpec((1, words, 1), lambda s: (s, 0, 0)),
            pl.BlockSpec((1, words, GROUP), lambda s: (s, 0, 0)),
            pl.BlockSpec((1, words, GROUP), lambda s: (s, 0, 0)),
        ],
        out_specs=[
            pl.BlockSpec((1, 4, groups, GROUP), lambda s: (s, 0, 0, 0)),
            pl.BlockSpec(memory_space=pltpu.SMEM),
        ],
        out_shape=[
            jax.ShapeDtypeStruct((seqs, 4, groups, GROUP), jnp.int32),
            jax.ShapeDtypeStruct((seqs,), jnp.int32),
        ],
        name="pack",
    )(char_counts[:, None, :], char_counts[:, :, None], ids, back)


def tile_maps(pack_ref, step, words):
    per = ROWS // GROUP
    id_rows = pack_ref[0, pl.ds(step * per, per), :]
    word_rows = pack_ref[1, pl.ds(step * per, per), :]
    letters = iota((CV, GROUP), 0) + 1
    spots = iota((words, GROUP), 0) + 1
    one_hot = [
        (letters == id_rows[g : g + 1]).astype(jnp.float32).astype(jnp.bfloat16) for g in range(per)
    ]
    word_map = [
        (spots == word_rows[g : g + 1]).astype(jnp.float32).astype(jnp.bfloat16) for g in range(per)
    ]
    return jnp.concatenate(one_hot, axis=1), jnp.concatenate(word_map, axis=1)


def column_rms(values):
    inverse = lax.rsqrt(jnp.mean(values * values, axis=0, keepdims=True) + EPS)
    return values * inverse, inverse


def own_block():
    shape = (GROUP // SLOTS, SLOTS, CHEADS * GROUP)
    return iota(shape, 0) == lax.div(lax.rem(iota(shape, 2), GROUP), SLOTS)


def to_compact(block, own):
    return jnp.sum(jnp.where(own, block.reshape(own.shape), 0.0), axis=0)


def from_compact(compact, own):
    wide = jnp.broadcast_to(compact[None], own.shape)
    return jnp.where(own, wide, 0.0).astype(jnp.bfloat16).reshape(GROUP, -1)


def spread_heads(values):
    head = values.shape[0] // CHEADS
    zero = jnp.zeros((head, GROUP), values.dtype)
    rows = []
    for h in range(CHEADS):
        parts = [zero] * CHEADS
        parts[h] = values[h * head : (h + 1) * head]
        rows.append(jnp.concatenate(parts, axis=1))
    return jnp.concatenate(rows, axis=0)


def char_fwd_kernel(tiles_ref, *refs):
    @pl.when(pl.program_id(0) < tiles_ref[0])
    def _():
        char_fwd_tile(*refs)


def char_fwd_tile(
    pack_ref, table_ref, qkv_ref, out_ref, up_ref, down_ref, g1_ref, g2_ref,
    pooled_ref, keep_values, keep_probs, keep_qkv, keep_mixed, keep_first, keep_hidden, keep_slope,
):
    step = pl.program_id(0)
    words = pooled_ref.shape[0]
    per = ROWS // GROUP
    head = CD // CHEADS

    @pl.when(step == 0)
    def _():
        pooled_ref[...] = jnp.zeros_like(pooled_ref)

    one_hot, word_map = tile_maps(pack_ref, step, words)
    embedded = dot_nn(table_ref[...], one_hot)
    act_one = (column_rms(embedded)[0] * g1_ref[...]).astype(jnp.bfloat16)
    triple = dot_nn(qkv_ref[...], act_one).astype(jnp.bfloat16)
    keep_qkv[...] = triple
    low_rows = pack_ref[2, pl.ds(step * per, per), :]
    high_rows = pack_ref[3, pl.ds(step * per, per), :]
    own = own_block()
    key_pos = iota((SLOTS, GROUP), 0)
    key_rows = triple[CD : 2 * CD].T
    keep_values[...] = triple[2 * CD :].T
    mixed = []
    for g in range(per):
        valid = (key_pos >= low_rows[g : g + 1]) & (key_pos < high_rows[g : g + 1])
        valid = jnp.concatenate([valid.astype(jnp.float32)] * CHEADS, axis=1) > 0
        lanes = slice(g * GROUP, (g + 1) * GROUP)
        scores = to_compact(dot_nn(key_rows[lanes], spread_heads(triple[:CD, lanes])), own)
        scores = jnp.where(valid, scores * head**-0.5, NEG_FILL)
        powers = jnp.exp(scores - jnp.max(scores, axis=0, keepdims=True))
        powers = jnp.where(valid, powers, 0.0)
        total = jnp.sum(powers, axis=0, keepdims=True)
        probs = powers / jnp.where(total > 0, total, 1.0)
        keep_probs[:, g * CHEADS * GROUP : (g + 1) * CHEADS * GROUP] = probs
        probs = from_compact(probs, own)
        parts = []
        for h in range(CHEADS):
            v = triple[2 * CD + h * head : 2 * CD + (h + 1) * head, lanes]
            parts.append(dot_nn(v, probs[:, h * GROUP : (h + 1) * GROUP]).astype(jnp.bfloat16))
        mixed.append(jnp.concatenate(parts, axis=0))
    mixed = jnp.concatenate(mixed, axis=1)
    keep_mixed[...] = mixed
    first = embedded + dot_nn(out_ref[...], mixed)
    keep_first[...] = first
    act_two = (column_rms(first)[0] * g2_ref[...]).astype(jnp.bfloat16)
    branch = None
    for c in range(CFF // CD):
        rows = slice(c * CD, (c + 1) * CD)
        hidden, slope = gelu_pair(dot_nn(up_ref[rows, :], act_two))
        hidden = hidden.astype(jnp.bfloat16)
        keep_hidden[rows, :] = hidden
        keep_slope[rows, :] = slope.astype(jnp.bfloat16)
        part = dot_nn(down_ref[:, rows], hidden)
        branch = part if branch is None else branch + part
    high, low = split_two(first + branch)
    pooled_ref[...] += dot_nt(word_map, high) + dot_nt(word_map, low)


KEPT = (
    (3 * CD, jnp.bfloat16),
    (CD, jnp.bfloat16),
    (CD, jnp.float32),
    (CFF, jnp.bfloat16),
    (CFF, jnp.bfloat16),
)


def kept_specs():
    return [
        pl.BlockSpec((ROWS, CD), lambda t, n: (kept_place(t, n)[1], 0)),
        pl.BlockSpec((SLOTS, CHEADS * ROWS), kept_place),
    ] + [pl.BlockSpec((depth, ROWS), kept_place) for depth, _ in KEPT]


def kept_shapes(rows):
    return [
        jax.ShapeDtypeStruct((rows, CD), jnp.bfloat16),
        jax.ShapeDtypeStruct((SLOTS, CHEADS * rows), jnp.float32),
    ] + [jax.ShapeDtypeStruct((depth, rows), dtype) for depth, dtype in KEPT]


def whole(array):
    zeros = (0,) * array.ndim
    return pl.BlockSpec(array.shape, lambda *_: zeros)


def kept_place(step, tiles):
    return 0, jnp.minimum(step, tiles[0] - 1)


def char_fwd(tiles, pack, weights, words):
    rows = words * SLOTS
    operands = (pack,) + weights
    return pl.pallas_call(
        char_fwd_kernel,
        grid_spec=pltpu.PrefetchScalarGridSpec(
            num_scalar_prefetch=1,
            grid=(rows // ROWS,),
            in_specs=[whole(a) for a in operands],
            out_specs=[pl.BlockSpec((words, CD), lambda t, n: (0, 0))]
            + kept_specs(),
        ),
        out_shape=[jax.ShapeDtypeStruct((words, CD), jnp.float32)] + kept_shapes(rows),
        compiler_params=pltpu.CompilerParams(vmem_limit_bytes=VMEM_BYTES),
        name="char_fwd",
    )(tiles, *operands)


def fold_lanes(values):
    total = values[:, :GROUP]
    for g in range(1, values.shape[1] // GROUP):
        total = total + values[:, g * GROUP : (g + 1) * GROUP]
    return total


def column_rms_back(grad_in, gain, normed, inverse):
    scaled = grad_in * gain
    return inverse * (scaled - normed * jnp.mean(scaled * normed, axis=0, keepdims=True))


def char_bwd_kernel(tiles_ref, *refs):
    @pl.when(pl.program_id(0) < tiles_ref[0])
    def _():
        char_bwd_tile(*refs)


def char_bwd_tile(
    pack_ref, spread_ref, table_ref, qkv_ref, out_ref, up_ref, down_ref, g1_ref, g2_ref,
    keep_values, keep_probs, keep_qkv, keep_mixed, keep_first, keep_hidden, keep_slope,
    d_table, d_qkv, d_out, d_up, d_down, d_g1, d_g2,
):
    step = pl.program_id(0)
    words = spread_ref.shape[1]
    per = ROWS // GROUP
    head = CD // CHEADS

    @pl.when(step == 0)
    def _():
        for ref in (d_table, d_qkv, d_out, d_up, d_down, d_g1, d_g2):
            ref[...] = jnp.zeros_like(ref)

    one_hot, word_map = tile_maps(pack_ref, step, words)
    halves = dot_nn(spread_ref[...], word_map)
    grad_second = halves[:CD] + halves[CD:]
    grad_branch = grad_second.astype(jnp.bfloat16)
    first = keep_first[...]
    normed_two, inverse_two = column_rms(first)
    act_two = (normed_two * g2_ref[...]).astype(jnp.bfloat16)
    grad_act_two = None
    for c in range(CFF // CD):
        rows = slice(c * CD, (c + 1) * CD)
        d_down[rows, :] += dot_nt(keep_hidden[rows, :], grad_branch)
        grad_upper = dot_nn(down_ref[rows, :], grad_branch) * keep_slope[rows, :].astype(
            jnp.float32
        )
        grad_upper = grad_upper.astype(jnp.bfloat16)
        d_up[:, rows] += dot_nt(act_two, grad_upper)
        part = dot_nn(up_ref[:, rows], grad_upper)
        grad_act_two = part if grad_act_two is None else grad_act_two + part
    d_g2[...] += fold_lanes(grad_act_two * normed_two)
    grad_first = grad_second + column_rms_back(
        grad_act_two, g2_ref[...], normed_two, inverse_two
    )
    grad_attn = grad_first.astype(jnp.bfloat16)
    d_out[...] += dot_nt(keep_mixed[...], grad_attn)
    grad_mixed = dot_nn(out_ref[...], grad_attn).astype(jnp.bfloat16)
    own = own_block()
    triple = keep_qkv[...]
    columns = []
    for g in range(per):
        lanes = slice(g * GROUP, (g + 1) * GROUP)
        wide = slice(g * CHEADS * GROUP, (g + 1) * CHEADS * GROUP)
        probs = keep_probs[:, wide]
        grad_probs = to_compact(
            dot_nn(keep_values[lanes, :], spread_heads(grad_mixed[:, lanes])), own
        )
        grad_scores = probs * (
            grad_probs - jnp.sum(probs * grad_probs, axis=0, keepdims=True)
        )
        grad_raw = from_compact(grad_scores * head**-0.5, own)
        probs = from_compact(probs, own)
        gq, gk, gv = [], [], []
        for h in range(CHEADS):
            q = triple[h * head : (h + 1) * head, lanes]
            k = triple[CD + h * head : CD + (h + 1) * head, lanes]
            grad_o = grad_mixed[h * head : (h + 1) * head, lanes]
            part = slice(h * GROUP, (h + 1) * GROUP)
            gq.append(dot_nn(k, grad_raw[:, part]).astype(jnp.bfloat16))
            gk.append(dot_nt(q, grad_raw[:, part]).astype(jnp.bfloat16))
            gv.append(dot_nt(grad_o, probs[:, part]).astype(jnp.bfloat16))
        columns.append(jnp.concatenate(gq + gk + gv, axis=0))
    grad_triple = jnp.concatenate(columns, axis=1)
    embedded = dot_nn(table_ref[...], one_hot)
    normed_one, inverse_one = column_rms(embedded)
    act_one = (normed_one * g1_ref[...]).astype(jnp.bfloat16)
    d_qkv[...] += dot_nt(act_one, grad_triple)
    grad_act_one = dot_nn(qkv_ref[...], grad_triple)
    d_g1[...] += fold_lanes(grad_act_one * normed_one)
    back_one = column_rms_back(grad_act_one, g1_ref[...], normed_one, inverse_one)
    grad_embedded = (grad_first + back_one).astype(jnp.bfloat16)
    d_table[...] += dot_nt(one_hot, grad_embedded)


def char_bwd(tiles, pack, spread, weights, kept):
    operands = (pack, spread) + weights
    shapes = ((CV, CD), (CD, 3 * CD), (CD, CD), (CD, CFF), (CFF, CD), (CD, GROUP), (CD, GROUP))
    return pl.pallas_call(
        char_bwd_kernel,
        grid_spec=pltpu.PrefetchScalarGridSpec(
            num_scalar_prefetch=1,
            grid=(kept[0].shape[0] // ROWS,),
            in_specs=[whole(a) for a in operands]
            + kept_specs(),
            out_specs=[pl.BlockSpec(s, lambda t, n: (0, 0)) for s in shapes],
        ),
        out_shape=[jax.ShapeDtypeStruct(s, jnp.float32) for s in shapes],
        compiler_params=pltpu.CompilerParams(vmem_limit_bytes=VMEM_BYTES),
        name="char_bwd",
    )(tiles, *operands, *kept)


def cost(flops, moved, powers):
    return pl.CostEstimate(flops=int(flops), bytes_accessed=int(moved), transcendentals=int(powers))


def single(kernel, outs, name, flops):
    return pl.pallas_call(
        kernel,
        out_shape=[jax.ShapeDtypeStruct(shape, dtype) for shape, dtype in outs],
        compiler_params=pltpu.CompilerParams(vmem_limit_bytes=VMEM_BYTES),
        cost_estimate=cost(flops, 8e6, 1e5),
        name=name,
    )


def word_in_kernel(sum_ref, count_ref, words_ref, pool_ref, qkv_ref, g3_ref, start_ref, triple_ref):
    pooled = (sum_ref[...] / count_ref[...]).astype(jnp.bfloat16)
    words = words_ref[...].astype(jnp.float32).T
    start = words + dot_nt(pool_ref[...], pooled)
    start_ref[...] = start
    act = (column_rms(start)[0] * g3_ref[...]).astype(jnp.bfloat16)
    parts, depth, _ = triple_ref.shape
    for p in range(parts):
        rows = slice(p * depth, (p + 1) * depth)
        triple_ref[p] = dot_nn(qkv_ref[rows, :], act).astype(jnp.bfloat16)


def chunk_scores(ref, h, i, j, width):
    head = D // HEADS
    own = ref.shape[1] // 3
    lo = h * head
    q = ref[i, lo : lo + head, :]
    k = ref[j, own + lo : own + lo + head, :]
    scores = dot_tn(k, q) * head**-0.5
    if i == j:
        scores = jnp.where(
            iota((width, width), 0) <= iota((width, width), 1), scores, NEG_FILL
        )
    return scores


def word_attn_kernel(triple_ref, mixed_ref, lse_ref):
    parts, depth, width = triple_ref.shape
    head = D // HEADS
    own = depth // 3
    for h in range(own // head):
        lo = h * head
        for i in range(parts):
            scores = [chunk_scores(triple_ref, h, i, j, width) for j in range(i + 1)]
            highest = jnp.max(scores[0], axis=0, keepdims=True)
            for block in scores[1:]:
                highest = jnp.maximum(highest, jnp.max(block, axis=0, keepdims=True))
            powers = [jnp.exp(block - highest) for block in scores]
            total = jnp.sum(powers[0], axis=0, keepdims=True)
            for block in powers[1:]:
                total = total + jnp.sum(block, axis=0, keepdims=True)
            inverse = 1.0 / total
            mixed = None
            for j, block in enumerate(powers):
                v = triple_ref[j, 2 * own + lo : 2 * own + lo + head, :]
                part = dot_nn(v, (block * inverse).astype(jnp.bfloat16))
                mixed = part if mixed is None else mixed + part
            mixed_ref[i, lo : lo + head, :] = mixed.astype(jnp.bfloat16)
            lse_ref[h * parts + i : h * parts + i + 1, :] = highest + jnp.log(total)


def word_attn_back_kernel(triple_ref, lse_ref, grad_ref, out_ref, dk, dv):
    parts, depth, width = triple_ref.shape
    head = D // HEADS
    own = depth // 3
    for h in range(own // head):
        lo = h * head
        for i in range(parts):
            grad_o = grad_ref[i, lo : lo + head, :]
            lse = lse_ref[h * parts + i : h * parts + i + 1, :]
            probs, grads = [], []
            dot_sum = None
            for j in range(i + 1):
                probs.append(jnp.exp(chunk_scores(triple_ref, h, i, j, width) - lse))
                v = triple_ref[j, 2 * own + lo : 2 * own + lo + head, :]
                grads.append(dot_tn(v, grad_o))
                part = jnp.sum(probs[-1] * grads[-1], axis=0, keepdims=True)
                dot_sum = part if dot_sum is None else dot_sum + part
            q = triple_ref[i, lo : lo + head, :]
            grad_q = None
            for j in range(i + 1):
                k = triple_ref[j, own + lo : own + lo + head, :]
                raw = (probs[j] * (grads[j] - dot_sum) * head**-0.5).astype(jnp.bfloat16)
                part = dot_nn(k, raw)
                grad_q = part if grad_q is None else grad_q + part
                part_k = dot_nt(q, raw)
                part_v = dot_nt(grad_o, probs[j].astype(jnp.bfloat16))
                if i == j:
                    dk[j] = part_k
                    dv[j] = part_v
                else:
                    dk[j] += part_k
                    dv[j] += part_v
            out_ref[i, lo : lo + head, :] = grad_q.astype(jnp.bfloat16)
        for j in range(parts):
            out_ref[j, own + lo : own + lo + head, :] = dk[j].astype(jnp.bfloat16)
            out_ref[j, 2 * own + lo : 2 * own + lo + head, :] = dv[j].astype(jnp.bfloat16)


def word_mid_kernel(has_prev, *refs):
    (mixed_ref, start_ref, cot_ref, g4_ref, outt_ref, out_ref) = refs[:6]
    (upt_ref, up_ref, downt_ref, down_ref) = refs[6:10]
    place = 10
    prev = (None, None, None, None)
    if has_prev:
        prev = refs[10:14]
        place = 14
    (output_ref, after_grad_ref, mixed_grad_ref, d_up, d_down, d_out, d_g4) = refs[place : place + 7]
    (after, act, result, act_grad, cot_t) = refs[place + 7 :]
    step = pl.program_id(0)
    prev_up, prev_down, prev_out, prev_g4 = prev

    def put(ref, value, old):
        if old is not None:
            value = value + old[...]
        ref[...] = value.astype(ref.dtype)

    mixed = mixed_ref[...].reshape(D, -1)

    @pl.when(step == 0)
    def _():
        value = start_ref[...] + dot_nn(outt_ref[...], mixed)
        after[...] = value
        act[...] = (column_rms(value)[0] * g4_ref[...]).astype(jnp.bfloat16)
        result[...] = value
        act_grad[...] = jnp.zeros_like(act_grad)
        cot_t[...] = cot_ref[...].astype(jnp.float32).T.astype(jnp.bfloat16)

    hidden, slope = gelu_pair(dot_nn(upt_ref[...], act[...]))
    hidden = hidden.astype(jnp.bfloat16)
    result[...] += dot_nn(downt_ref[...], hidden)
    put(d_down, dot_nt(hidden, cot_t[...]), prev_down)
    grad_upper = (dot_nn(down_ref[...], cot_t[...]) * slope).astype(jnp.bfloat16)
    put(d_up, dot_nt(act[...], grad_upper), prev_up)
    act_grad[...] += dot_nn(up_ref[...], grad_upper)

    @pl.when(step == pl.num_programs(0) - 1)
    def _():
        output_ref[...] = result[...].T.astype(jnp.bfloat16)
        normed, inverse = column_rms(after[...])
        grad = act_grad[...]
        put(d_g4, fold_lanes(grad * normed), prev_g4)
        total = cot_t[...].astype(jnp.float32) + column_rms_back(
            grad, g4_ref[...], normed, inverse
        )
        after_grad_ref[...] = total
        low = total.astype(jnp.bfloat16)
        put(d_out, dot_nt(mixed, low), prev_out)
        mixed_grad_ref[...] = dot_nn(out_ref[...], low).astype(jnp.bfloat16).reshape(
            mixed_grad_ref.shape
        )


def word_mid(mixed, start, cot, g4, parts, prev):
    outt, out, upt, up, downt, down = parts
    width = start.shape[1]
    hidden = up.shape[1]
    block = D
    fixed = (mixed, start, cot, g4, outt, out)
    rows = pl.BlockSpec((block, D), lambda c: (c, 0))
    cols = pl.BlockSpec((D, block), lambda c: (0, c))

    def still(shape):
        return pl.BlockSpec(shape, lambda c: (0,) * len(shape))

    kind = jnp.float32 if prev is None else jnp.bfloat16
    earlier = () if prev is None else tuple(prev)
    return pl.pallas_call(
        functools.partial(word_mid_kernel, prev is not None),
        grid=(hidden // block,),
        in_specs=[still(a.shape) for a in fixed]
        + [rows, cols, cols, rows]
        + ([] if prev is None else [cols, rows, still((D, D)), still((D, GROUP))]),
        out_specs=[
            still((width, D)),
            still((D, width)),
            still(mixed.shape),
            cols,
            rows,
            still((D, D)),
            still((D, GROUP)),
        ],
        out_shape=[
            jax.ShapeDtypeStruct((width, D), jnp.bfloat16),
            jax.ShapeDtypeStruct((D, width), jnp.float32),
            jax.ShapeDtypeStruct(mixed.shape, jnp.bfloat16),
            jax.ShapeDtypeStruct((D, hidden), kind),
            jax.ShapeDtypeStruct((hidden, D), kind),
            jax.ShapeDtypeStruct((D, D), kind),
            jax.ShapeDtypeStruct((D, GROUP), jnp.float32),
        ],
        scratch_shapes=[
            pltpu.VMEM((D, width), jnp.float32),
            pltpu.VMEM((D, width), jnp.bfloat16),
            pltpu.VMEM((D, width), jnp.float32),
            pltpu.VMEM((D, width), jnp.float32),
            pltpu.VMEM((D, width), jnp.bfloat16),
        ],
        compiler_params=pltpu.CompilerParams(vmem_limit_bytes=VMEM_BYTES),
        cost_estimate=cost(6 * width * D * (2 * hidden + D), 2e7, 2 * width * hidden),
        name="word_mid",
    )(*fixed, upt, up, downt, down, *earlier)


def word_out_kernel(has_prev, *refs):
    (triple_ref, start_ref, after_grad_ref, qkv_ref, pool_ref, g3_ref) = refs[:6]
    (sum_ref, count_ref, count_row_ref) = refs[6:9]
    place = 9
    prev = (None, None, None)
    if has_prev:
        prev = refs[9:12]
        place = 12
    (input_grad_ref, spread_ref, d_qkv, d_pool, d_g3) = refs[place:]
    normed, inverse = column_rms(start_ref[...])
    act = (normed * g3_ref[...]).astype(jnp.bfloat16)
    parts, depth, _ = triple_ref.shape
    own = depth // 3
    grad = None
    for p in range(parts):
        triple = triple_ref[p]
        part = dot_nn(qkv_ref[:, p * depth : (p + 1) * depth], triple)
        grad = part if grad is None else grad + part
        weight = dot_nt(act, triple)
        for t in range(3):
            cols = slice(t * D + p * own, t * D + (p + 1) * own)
            value = weight[:, t * own : (t + 1) * own]
            if has_prev:
                value = value + prev[0][:, cols]
            d_qkv[:, cols] = value.astype(d_qkv.dtype)
    gain = fold_lanes(grad * normed)
    if has_prev:
        gain = gain + prev[2][...]
    d_g3[...] = gain
    total = after_grad_ref[...] + column_rms_back(grad, g3_ref[...], normed, inverse)
    input_grad_ref[...] = total.T
    low = total.astype(jnp.bfloat16)
    pooled = (sum_ref[...] / count_ref[...]).T.astype(jnp.bfloat16)
    value = dot_nt(pooled, low)
    if has_prev:
        value = value + prev[1][...]
    d_pool[...] = value.astype(d_pool.dtype)
    high, low = split_two(dot_nn(pool_ref[...], low) / count_row_ref[...])
    spread_ref[:CD, :] = high
    spread_ref[CD:, :] = low


def adam_step(weight, grad, first_old, second_old, clip_factor, rate, decay):
    clipped = grad * clip_factor
    first_new = BETA_ONE * first_old + (1.0 - BETA_ONE) * clipped
    second_new = BETA_TWO * second_old + (1.0 - BETA_TWO) * clipped * clipped
    first_hat = first_new / (1.0 - BETA_ONE**STEP)
    second_hat = second_new / (1.0 - BETA_TWO**STEP)
    weight_new = weight - rate * (first_hat / (jnp.sqrt(second_hat) + ADAM_EPS) + decay * weight)
    return (grad, first_new, second_new, weight_new, weight_new.astype(jnp.bfloat16))


class Ring:
    def __init__(self, dp, ranks):
        self.chips, self.ranks = dp // 2, ranks
        self.d, self.h = lax.axis_index("dp"), lax.axis_index("head")
        self.chip, self.core = lax.div(self.d, 2), lax.rem(self.d, 2)

    def sibling(self):
        return (self.d + 1 - 2 * self.core, self.h)

    def chip_at(self, k):
        return lax.rem(self.chip + k, self.chips)

    def plane(self, k):
        return (2 * self.chip_at(k) + self.core, self.h)

    def rank_at(self, k):
        return lax.rem(self.h + k, self.ranks)

    def line(self, k):
        return (self.d, self.rank_at(k))

    def meet(self):
        barrier = pltpu.get_barrier_semaphore()
        peers = [self.sibling()]
        peers += [self.plane(k) for k in range(1, self.chips)]
        peers += [self.line(k) for k in range(1, self.ranks)]
        for peer in peers:
            pl.semaphore_signal(barrier, inc=1, device_id=peer, device_id_type=pl.DeviceIdType.MESH)
        pl.semaphore_wait(barrier, len(peers))


def send(src, dst, sems, place, peer):
    copy = pltpu.make_async_remote_copy(
        src_ref=src,
        dst_ref=dst,
        send_sem=sems.at[(0,) + place],
        recv_sem=sems.at[(1,) + place],
        device_id=peer,
        device_id_type=pl.DeviceIdType.MESH,
    )
    copy.start()
    return copy


def gather_kernel(dp, ranks, count, *refs):
    shards, outs = refs[:count], refs[count : 2 * count]
    own_sem, line_sem, plane_sem, pair_sem = refs[2 * count :]
    ring = Ring(dp, ranks)
    ring.meet()
    sent, first, own = [], [], []
    for m in range(count):
        place = outs[m].at[ring.d, ring.h]
        own.append(pltpu.make_async_copy(shards[m], place, own_sem.at[m]))
        own[-1].start()
        first.append(
            [send(shards[m], place, line_sem, (m, k), ring.line(k)) for k in range(1, ranks)]
        )
    second = []
    for m in range(count):
        own[m].wait()
        for copy in first[m]:
            copy.wait_recv()
        block = outs[m].at[ring.d]
        second.append(
            [send(block, block, plane_sem, (m, k), ring.plane(k)) for k in range(1, ring.chips)]
        )
        sent.append(send(block, block, pair_sem, (m, 0), ring.sibling()))
    for m in range(count):
        for k in range(1, ring.chips):
            second[m][k - 1].wait_recv()
            block = outs[m].at[2 * ring.chip_at(ring.chips - k) + ring.core]
            sent.append(send(block, block, pair_sem, (m, k), ring.sibling()))
    for copy in sent:
        copy.wait()
    for m in range(count):
        for copy in first[m] + second[m]:
            copy.wait_send()


def gather(shards, collective):
    dp, ranks = lax.axis_size("dp"), lax.axis_size("head")
    count = len(shards)
    return pl.pallas_call(
        functools.partial(gather_kernel, dp, ranks, count),
        in_specs=[pl.BlockSpec(memory_space=pl.ANY)] * count,
        out_specs=[pl.BlockSpec(memory_space=pl.ANY)] * count,
        out_shape=[jax.ShapeDtypeStruct((dp, ranks) + s.shape, s.dtype) for s in shards],
        scratch_shapes=[
            pltpu.SemaphoreType.DMA((count,)),
            pltpu.SemaphoreType.DMA((2, count, ranks)),
            pltpu.SemaphoreType.DMA((2, count, dp // 2)),
            pltpu.SemaphoreType.DMA((2, count, dp // 2)),
        ],
        compiler_params=pltpu.CompilerParams(collective_id=collective, has_side_effects=True),
        name="gather",
    )(*shards)


def column_cuts(widths, ranks):
    block = sum(widths) // ranks
    cuts, start = [], 0
    for width in widths:
        mine, at = [], 0
        while at < width:
            rank, inside = divmod(start + at, block)
            take = min(width - at, block - inside)
            mine.append((rank, at, at + take, inside))
            at += take
        cuts.append(mine)
        start += width
    return cuts


def reduce_kernel(dp, ranks, groups, extra, *refs):
    pieces = sum(len(g) for g in groups)
    mats = len(groups)
    parts = refs[:pieces]
    gain_ref = refs[pieces]
    ready = refs[pieces + 1 : pieces + 1 + extra]
    place = pieces + 1 + extra
    outs = refs[place : place + mats]
    gain_out, square_out = refs[place + mats : place + mats + 2]
    place += mats + 2
    pair_in = refs[place : place + pieces]
    pair_sum = refs[place + pieces : place + 2 * pieces]
    plane_in = refs[place + 2 * pieces : place + 3 * pieces]
    place += 3 * pieces
    line_sum, line_in = refs[place : place + mats], refs[place + mats : place + 2 * mats]
    place += 2 * mats
    small, pair_sem, plane_sem, line_sem, small_sem = refs[place:]
    ring = Ring(dp, ranks)
    chips = ring.chips
    f32, bf16 = jnp.float32, jnp.bfloat16
    ring.meet()
    sent = []

    def share(slot, value, stage):
        others, here, count = (
            (lambda k: ring.sibling(), ring.core, 2),
            (ring.plane, ring.chip, chips),
            (ring.line, ring.h, ranks),
        )[stage]
        small[slot, stage, here] = value
        copies = []
        for k in range(1, count):
            spot = small.at[slot, stage, here]
            copies.append(send(spot, spot, small_sem, (slot, stage, k), others(k)))
        return copies

    def shared(slot, copies, stage):
        for copy in copies:
            copy.wait()
        count = (2, chips, ranks)[stage]
        total = small[slot, stage, 0]
        for k in range(1, count):
            total = total + small[slot, stage, k]
        return total

    def total_of(slot, value):
        for stage in range(3):
            value = shared(slot, share(slot, value, stage), stage)
        return value

    pairs = [
        send(parts[i].at[:, 1 - ring.core], pair_in[i], pair_sem, (i,), ring.sibling())
        for i in range(pieces)
    ]
    gain = shared(0, share(0, gain_ref[...], 0), 0)
    planes = []
    for i in range(pieces):
        pairs[i].wait()

        def add_pair(p, carry, i=i):
            both = parts[i][p, ring.core].astype(f32) + pair_in[i][p].astype(f32)
            pair_sum[i][p] = both.astype(bf16)
            return carry

        lax.fori_loop(0, chips, add_pair, 0)
        planes.append(
            [
                send(
                    pair_sum[i].at[ring.chip_at(k)],
                    plane_in[i].at[k],
                    plane_sem,
                    (i, k),
                    ring.plane(k),
                )
                for k in range(1, chips)
            ]
        )
    gain = shared(0, share(0, gain, 1), 1)
    gain_out[...] = shared(0, share(0, gain, 2), 2)
    lines, i = [], 0
    for m, widths in enumerate(groups):
        for cuts in column_cuts(widths, ranks):
            total = pair_sum[i][ring.chip].astype(f32)
            for k in range(1, chips):
                planes[i][k - 1].wait()
                total = total + plane_in[i][k].astype(f32)
            total = total.astype(bf16)
            for rank, first, last, inside in cuts:
                line_sum[m][rank, :, inside : inside + last - first] = total[:, first:last]
            i += 1
        lines.append(
            [
                send(
                    line_sum[m].at[ring.rank_at(k)], line_in[m].at[k], line_sem, (m, k), ring.line(k)
                )
                for k in range(1, ranks)
            ]
        )
    square = jnp.zeros(square_out.shape, f32)

    def squares(value):
        value = value * value
        rows, cols = value.shape
        if cols % GROUP:
            value = jnp.concatenate([value, jnp.zeros((rows, GROUP - cols % GROUP), f32)], axis=1)
        return jnp.sum(fold_lanes(value).reshape(rows // 8, 8, GROUP), axis=0)

    for ref in ready:
        square = square + squares(ref[...])
    for m in range(mats):
        total = line_sum[m][ring.h].astype(f32)
        for k in range(1, ranks):
            lines[m][k - 1].wait()
            total = total + line_in[m][k].astype(f32)
        outs[m][...] = total
        square = square + squares(total)
    small_square = jnp.concatenate([square, jnp.zeros_like(square)], axis=0)
    square_out[...] = total_of(1, small_square)[:8]


def reduce_grads(groups, gains, ready, collective):
    dp, ranks = lax.axis_size("dp"), lax.axis_size("head")
    chips = dp // 2
    bf16, f32 = jnp.bfloat16, jnp.float32
    pieces, widths, shards = [], [], []
    for group in groups:
        rows = group[0].shape[0] // dp
        pieces += [p.reshape(chips, 2, rows, p.shape[1]) for p in group]
        widths.append(tuple(p.shape[1] for p in group))
        shards.append((rows, sum(widths[-1]) // ranks))
    blocks = [p.shape[2:] for p in pieces]
    vmem = pl.BlockSpec(memory_space=pltpu.VMEM)
    n, mats = len(pieces), len(groups)
    return pl.pallas_call(
        functools.partial(reduce_kernel, dp, ranks, widths, len(ready)),
        in_specs=[vmem] * (n + 1 + len(ready)),
        out_specs=[vmem] * (mats + 2),
        out_shape=[jax.ShapeDtypeStruct(s, f32) for s in shards]
        + [jax.ShapeDtypeStruct(gains.shape, f32), jax.ShapeDtypeStruct((8, GROUP), f32)],
        scratch_shapes=[pltpu.VMEM((chips,) + b, bf16) for b in blocks] * 3
        + [pltpu.VMEM((ranks,) + s, bf16) for s in shards] * 2
        + [
            pltpu.VMEM((2, 3, max(2, chips, ranks)) + gains.shape, f32),
            pltpu.SemaphoreType.DMA((2, n)),
            pltpu.SemaphoreType.DMA((2, n, chips)),
            pltpu.SemaphoreType.DMA((2, mats, ranks)),
            pltpu.SemaphoreType.DMA((2, 2, 3, max(2, chips, ranks))),
        ],
        compiler_params=pltpu.CompilerParams(
            collective_id=collective, has_side_effects=True, vmem_limit_bytes=VMEM_BYTES
        ),
        name="reduce_grads",
    )(*pieces, gains, *ready)


def update_kernel(count, *refs):
    weights, grads = refs[:count], refs[count : 2 * count]
    firsts, seconds = refs[2 * count : 3 * count], refs[3 * count : 4 * count]
    square_ref = refs[4 * count]
    norm_ref, outs = refs[4 * count + 1], refs[4 * count + 2 :]
    gain_grad = grads[-1][...]
    square = jnp.sum(square_ref[...]) + jnp.sum(gain_grad * gain_grad)
    norm = jnp.sqrt(jnp.full((1, GROUP), square, jnp.float32))
    norm_ref[...] = norm
    clip_factor = jnp.minimum(1.0, CLIP / norm)[:, :1]
    for i in range(count):
        gains = i == count - 1
        result = adam_step(
            weights[i][...],
            grads[i][...],
            firsts[i][...],
            seconds[i][...],
            clip_factor,
            GAIN_RATE if gains else MATRIX_RATE,
            0.0 if gains else MATRIX_DECAY,
        )
        for ref, value in zip(outs[5 * i : 5 * i + 5], result):
            ref[...] = value


def update(weights, grads, firsts, seconds, square):
    count = len(weights)
    shapes = [jax.ShapeDtypeStruct((1, GROUP), jnp.float32)]
    for w in weights:
        shapes += [jax.ShapeDtypeStruct(w.shape, jnp.float32)] * 4
        shapes.append(jax.ShapeDtypeStruct(w.shape, jnp.bfloat16))
    return pl.pallas_call(
        functools.partial(update_kernel, count),
        out_shape=shapes,
        compiler_params=pltpu.CompilerParams(vmem_limit_bytes=VMEM_BYTES),
        name="update",
    )(*weights, *grads, *firsts, *seconds, square)


def body(
    char_ids,
    char_counts,
    language,
    words_in,
    out_cotangent,
    char_table,
    char_in,
    char_down,
    word_in,
    word_down,
    norm_gains,
    old_table_first,
    old_table_second,
    old_char_in_first,
    old_char_in_second,
    old_char_down_first,
    old_char_down_second,
    old_word_in_first,
    old_word_in_second,
    old_word_down_first,
    old_word_down_second,
    old_gains_first,
    old_gains_second,
):
    bf16, f32 = jnp.bfloat16, jnp.float32
    blocks = gather(
        (
            char_table.T.astype(bf16),
            char_in.astype(bf16),
            char_down.T.astype(bf16),
            word_in.astype(bf16),
            word_down.astype(bf16),
        ),
        0,
    )

    def joined(block):
        dp, ranks, rows, cols = block.shape
        return block.transpose(0, 2, 1, 3).reshape(dp * rows, ranks * cols)

    def joined_flat(block):
        dp, ranks, cols, rows = block.shape
        return block.transpose(1, 2, 0, 3).reshape(ranks * cols, dp * rows)

    table_t_low, char_in_low = joined_flat(blocks[0]), joined(blocks[1])
    char_down_t = joined_flat(blocks[2])
    word_in_low, word_down_low = joined(blocks[3]), joined(blocks[4])
    seq_count, local_words = (words_in.shape[0], words_in.shape[1])
    ranks = lax.axis_size("head")
    width = 3 * D // ranks
    own = width // 3
    packed, tiles = pack_rows(char_ids, char_counts)
    languages = table_t_low.shape[1] // CV

    def lanes(gain, width):
        return jnp.broadcast_to(gain[:, None], (gain.shape[0], width))

    gains = (lanes(norm_gains[:CD], ROWS), lanes(norm_gains[CD : 2 * CD], ROWS))
    g3 = lanes(norm_gains[2 * CD : 2 * CD + D], local_words)
    g4 = lanes(norm_gains[2 * CD + D :], local_words)
    table_t = [
        lax.dynamic_slice_in_dim(table_t_low, language[i] * CV, CV, axis=1)
        for i in range(seq_count)
    ]
    char_parts = (
        char_in_low[:, : 3 * CD],
        char_in_low[:, 3 * CD : 4 * CD],
        char_in_low[:, 4 * CD : 4 * CD + CFF],
        char_down_t.T,
    )
    flipped = tuple(part.T for part in char_parts[:3]) + (char_down_t,)
    pool = char_in_low[:, 4 * CD + CFF :]
    pool_t = pool.T
    qkv = word_in_low[:, : 3 * D].reshape(D, 3, ranks, own).transpose(0, 2, 1, 3).reshape(D, 3 * D)
    qkv_t = qkv.T
    out = word_in_low[:, 3 * D : 4 * D]
    up = word_in_low[:, 4 * D :]
    mid_parts = (out.T, out, up.T, up, word_down_low.T, word_down_low)
    count_row = char_counts.astype(jnp.float32)[:, None, :]
    count_col = char_counts.astype(jnp.float32)[:, :, None]
    triple_shape = (ranks, width, local_words)
    mixed_shape = (ranks, own, local_words)

    def swap(values):
        return lax.all_to_all(values, "head", 0, 0, tiled=True)

    seqs = range(seq_count)
    kept, sums, starts, triples = [], [], [], []
    for i in seqs:
        total, *saved = char_fwd(
            tiles[i : i + 1], packed[i], (table_t[i],) + flipped + gains, local_words
        )
        kept.append(saved)
        sums.append(total)
        start, triple = single(
            word_in_kernel,
            [((D, local_words), f32), (triple_shape, bf16)],
            "word_in",
            2 * local_words * D * 3 * D,
        )(total, count_col[i], words_in[i], pool_t, qkv_t, g3)
        starts.append(start)
        triples.append(swap(triple))
    mixes, lses = [], []
    for i in seqs:
        mixed, lse = single(
            word_attn_kernel,
            [(mixed_shape, bf16), ((own // (D // HEADS) * ranks, local_words), f32)],
            "word_attn",
            4e9,
        )(triples[i])
        lses.append(lse)
        mixes.append(swap(mixed))
    outputs, after_grads, mixed_grads = [], [], []
    mid = None
    for i in seqs:
        output, after_grad, mixed_grad, *mid = word_mid(
            mixes[i], starts[i], out_cotangent[i], g4, mid_parts, mid
        )
        outputs.append(output)
        after_grads.append(after_grad)
        mixed_grads.append(swap(mixed_grad))
    triple_grads = []
    for i in seqs:
        grads = pl.pallas_call(
            word_attn_back_kernel,
            out_shape=jax.ShapeDtypeStruct(triple_shape, bf16),
            scratch_shapes=[pltpu.VMEM((ranks, D // HEADS, local_words), f32)] * 2,
            compiler_params=pltpu.CompilerParams(vmem_limit_bytes=VMEM_BYTES),
            cost_estimate=cost(1e10, 2e6, 1e6),
            name="word_attn_back",
        )(triples[i], lses[i], mixed_grads[i])
        triple_grads.append(swap(grads))
    input_grads, last = [], None
    char_last = None
    tables_out = []
    for i in seqs:
        kind = f32 if last is None else bf16
        earlier = () if last is None else tuple(last)
        input_grad, spread, *last = single(
            functools.partial(word_out_kernel, last is not None),
            [
                ((local_words, D), f32),
                ((2 * CD, local_words), bf16),
                ((D, 3 * D), kind),
                ((CD, D), kind),
                ((D, GROUP), f32),
            ],
            "word_out",
            4 * local_words * D * 3 * D,
        )(
            triple_grads[i],
            starts[i],
            after_grads[i],
            qkv,
            pool,
            g3,
            sums[i],
            count_col[i],
            count_row[i],
            *earlier,
        )
        input_grads.append(input_grad)
        one_table, *rest = char_bwd(
            tiles[i : i + 1], packed[i], spread, (table_t[i],) + char_parts + gains, kept[i]
        )
        tables_out.append(one_table)
        char_last = rest if char_last is None else [a + b for a, b in zip(char_last, rest)]
    output = jnp.stack(outputs)
    input_grad = jnp.stack(input_grads)
    grad_table = sum(
        jnp.where(
            (jnp.arange(languages) == language[i])[:, None, None], tables_out[i][None], 0.0
        )
        for i in seqs
    ).reshape(-1, CD)
    grad_up, grad_down, grad_out, gain_four = mid
    grad_qkv, grad_pool, gain_three = last
    c_qkv, c_out, c_up, c_down, gain_one, gain_two = char_last

    gain_grads = jnp.concatenate(
        [jnp.sum(g, axis=1) for g in (gain_one, gain_two, gain_three, gain_four)]
    )
    flat = (gain_grads.shape[0] // GROUP, GROUP)
    rest = 16 - flat[0]
    *shards, gains_sum, square = reduce_grads(
        [
            [grad_table.astype(bf16)],
            [g.astype(bf16) for g in (c_qkv, c_out, c_up, grad_pool)],
            [c_down.astype(bf16)],
            [grad_qkv, grad_out, grad_up],
            [grad_down],
        ],
        jnp.pad(gain_grads.reshape(flat), ((0, rest), (0, 0))),
        [],
        1,
    )
    norm, *updated = update(
        (char_table, char_in, char_down, word_in, word_down, norm_gains.reshape(flat)),
        (*shards, gains_sum[: flat[0]]),
        (
            old_table_first,
            old_char_in_first,
            old_char_down_first,
            old_word_in_first,
            old_word_down_first,
            old_gains_first.reshape(flat),
        ),
        (
            old_table_second,
            old_char_in_second,
            old_char_down_second,
            old_word_in_second,
            old_word_down_second,
            old_gains_second.reshape(flat),
        ),
        square,
    )
    updated[-5:] = [part.reshape(norm_gains.shape) for part in updated[-5:]]
    return (output, input_grad, norm[0, 0], *updated)


def solution(mesh):
    return jax.shard_map(
        body,
        mesh=mesh,
        in_specs=(
            P("dp", "head", None),
            P("dp", "head"),
            P("dp"),
            P("dp", "head", None),
            P("dp", "head", None),
            P("dp", "head"),
            P("dp", "head"),
            P("dp", "head"),
            P("dp", "head"),
            P("dp", "head"),
            P(),
            P("dp", "head"),
            P("dp", "head"),
            P("dp", "head"),
            P("dp", "head"),
            P("dp", "head"),
            P("dp", "head"),
            P("dp", "head"),
            P("dp", "head"),
            P("dp", "head"),
            P("dp", "head"),
            P(),
            P(),
        ),
        out_specs=(
            P("dp", "head", None),
            P("dp", "head", None),
            P(),
            P("dp", "head"),
            P("dp", "head"),
            P("dp", "head"),
            P("dp", "head"),
            P("dp", "head"),
            P("dp", "head"),
            P("dp", "head"),
            P("dp", "head"),
            P("dp", "head"),
            P("dp", "head"),
            P("dp", "head"),
            P("dp", "head"),
            P("dp", "head"),
            P("dp", "head"),
            P("dp", "head"),
            P("dp", "head"),
            P("dp", "head"),
            P("dp", "head"),
            P("dp", "head"),
            P("dp", "head"),
            P("dp", "head"),
            P("dp", "head"),
            P("dp", "head"),
            P("dp", "head"),
            P("dp", "head"),
            P(),
            P(),
            P(),
            P(),
            P(),
        ),
        check_vma=False,
    )
```

time: 940 us -> 542 us (0.58)
  waiting for transfers between devices: 279 us -> 25.4 us
  Pallas kernels: 177 us -> 366 us
  blocking collectives: 182 us -> 0 us
  matrix products: 117 us -> 0 us
  other arithmetic: 47.3 us -> 18.4 us
  starting transfers between devices: 12.6 us -> 38.3 us
  between operations: 24.2 us -> 2.93 us
  local copies, waits for them, and re-layouts: 90 us -> 80.4 us
    psum x1 -> x0, waiting for transfers between devices: 242 us -> none  [body(): lax.psum((grad_table, grad_cin, grad_cdown, grad_win, grad_wdown, gain_gr...]
    pallas_call x0 -> x13, Pallas kernels: none -> 241 us  [the longest x1 103 us: reduce_grads(): pl.pallas_call(functools.partial(reduce_kernel, dp, ranks, widths, len(re...]
    all_gather x7 -> x0, blocking collectives: 122 us -> none  [the longest x1 43.3 us: body(): lax.all_gather(word_down.astype(jnp.bfloat16), 'head', axis=1, tiled=True)]
    dot_general x21 -> x0, matrix products: 117 us -> none  [the longest x1 25 us: attend_backward(): jnp.einsum('bhqk,bqhd->bkhd', grad_raw, queries, preferred_element_type=j...]
    psum x1 -> x0, blocking collectives: 39.3 us -> none  [body(): lax.psum((grad_table, grad_cin, grad_cdown, grad_win, grad_wdown, gain_gr...]
    pallas_call x2, Pallas kernels: 92.9 us -> 63.3 us  [char_bwd(): pl.pallas_call(char_bwd_kernel, grid_spec=pltpu.PrefetchScalarGridSpec(nu...]
    all_to_all x3 -> x8, starting transfers between devices: 12.2 us -> 38.3 us  [swap(): return lax.all_to_all(values, 'head', 0, 0, tiled=True)]
    pallas_call x2, Pallas kernels: 80.3 us -> 58.5 us  [char_fwd(): pl.pallas_call(char_fwd_kernel, grid_spec=pltpu.PrefetchScalarGridSpec(nu...]
  transfers between devices with their start and end apart: 7 -> 8, of which waited for: 3 -> 4; matrix products, arithmetic and copies ran while one was open for 8% -> 5% of each run, Pallas kernels for 9% -> 17%
where the time goes in v2:
time: 542 us; the launch traced here: 531 us
  Pallas kernels  366 us (68%)
  local copies, waits for them, and re-layouts  80.4 us (15%)
  starting transfers between devices  38.3 us (7%)
  waiting for transfers between devices  25.4 us (5%)
  other arithmetic  18.4 us (3%)
    pallas_call x1, Pallas kernels, reduce_grads(): pl.pallas_call(functools.partial(reduce_kernel, dp, ranks, widths, len(re...  103 us
    pallas_call x2, Pallas kernels, char_bwd(): pl.pallas_call(char_bwd_kernel, grid_spec=pltpu.PrefetchScalarGridSpec(nu...  63.3 us
    pallas_call x1, Pallas kernels, gather(): pl.pallas_call(functools.partial(gather_kernel, dp, ranks, count), in_spe...  62.5 us
    pallas_call x2, Pallas kernels, char_fwd(): pl.pallas_call(char_fwd_kernel, grid_spec=pltpu.PrefetchScalarGridSpec(nu...  58.5 us
    all_to_all x8, starting transfers between devices, swap(): return lax.all_to_all(values, 'head', 0, 0, tiled=True)  38.3 us
    unnamed x103, local copies, waits for them, and re-layouts  28.8 us
    pallas_call x2, Pallas kernels, word_mid(): pl.pallas_call(functools.partial(word_mid_kernel, prev is not None), grid...  26.2 us
    all_to_all x8, waiting for transfers between devices, swap(): return lax.all_to_all(values, 'head', 0, 0, tiled=True)  25.4 us
  transfers between devices with their start and end apart: 8, of which 4 were waited for; matrix products, arithmetic and copies ran while one was open for 5% of the time, Pallas kernels for 17%

profile of v2, /device:TPU:0, one launch (start us, length us, event | category | flops | bytes accessed | tf_op | source)
XLA Modules:
  0.0 531.4 jit_solution(3319913333442385823)
XLA Ops:
  3.3 1.6 convert_element_type.46.refs_3_
  4.9 1.5 convert_element_type.47.refs_4_
  9.4 62.5 %gather.1 = (bf16[8,4,64,128]{3,2,1,0:T(8,128)(2,1)}, bf16[8,4,32,640]{3,2,1,0:T(8,128)(2,1)}, bf16[8,4,64,128]{3,2,1,0:T(8,128)(2,1)}, bf16[8,4,64,1024]{3,2,1,0:T(8,128)(2,1)}, bf16[8,4,256,128]{3,2,1,0:T(8,128)(2,1)}) custom-call(bf16[64,128]{1,0:T(8,128)(2,1)} %get-tuple-element.348.refs_0_, bf16[32,640]{1,0:T(8,128)(2,1)} %convert_element_type.43.refs_1_, ...), custom_call_target="tpu_custom_call" | custom-call | tf_op jit(solution)/shard_map/gather/pallas_call | solution.py:762
  71.9 2.0 copy.102
  85.7 3.4 pack.1
  92.8 5.4 %copy.107 = bf16[8,64,4,1024]{3,2,1,0:T(4,128)(2,1)S(1)} copy(bf16[8,64,4,1024]{3,1,2,0:T(8,128)(2,1)} %bitcast.122) | data formatting | bytes 8388608 | tf_op jit(solution)/shard_map/transpose | solution.py:1026
  98.2 2.3 copy.147
  100.5 2.0 copy-done.2
  103.1 2.6 copy.108
  110.4 29.4 %char_fwd.2 = (f32[256,256]{1,0:T(8,128)}, bf16[4096,256]{1,0:T(8,128)(2,1)}, f32[16,16384]{1,0:T(8,128)}, bf16[768,4096]{1,0:T(8,128)(2,1)}, bf16[256,4096]{1,0...) custom-call(s32[1]{0:T(128)} %get-tuple-element.345.tiles_ref, ...), custom_call_target="tpu_custom_call" | custom-call | tf_op jit(solution)/shard_map/char_fwd/pallas_call | solution.py:292
  140.7 3.8 word_in.2
  144.5 6.3 %all-to-all-start = ((bf16[4,384,256]{2,1,0:T(8,128)(2,1)}), bf16[4,384,256]{2,1,0:T(8,128)(2,1)S(1)}, u32[]{:S(2)}, u32[]{:S(2)}) async-start(bf16[4,384,256]{2,1,0:T(8,128)(2,1)} %get-tuple-element.147), calls=%async_computation | async-start | bytes 1572864 | tf_op jit(solution)/shard_map/all_to_all | solution.py:1072
  151.6 29.2 %char_fwd.3 = (f32[256,256]{1,0:T(8,128)}, bf16[4096,256]{1,0:T(8,128)(2,1)}, f32[16,16384]{1,0:T(8,128)}, bf16[768,4096]{1,0:T(8,128)(2,1)}, bf16[256,4096]{1,0...) custom-call(s32[1]{0:T(128)} %get-tuple-element.346.tiles_ref, ...), custom_call_target="tpu_custom_call" | custom-call | tf_op jit(solution)/shard_map/char_fwd/pallas_call | solution.py:292
  180.8 3.8 word_in.3
  184.6 5.5 %all-to-all-start.2 = ((bf16[4,384,256]{2,1,0:T(8,128)(2,1)}), bf16[4,384,256]{2,1,0:T(8,128)(2,1)}, u32[]{:S(2)}, u32[]{:S(2)}) async-start(bf16[4,384,256]{2,1,0:T(8,128)(2,1)} %get-tuple-element.153), calls=%async_computation.2 | async-start | bytes 1572864 | tf_op jit(solution)/shard_map/all_to_all | solution.py:1072
  190.1 3.4 fusion.1
  193.6 5.2 word_attn.2
  198.8 11.6 %all-to-all-done.2.triple_ref = bf16[4,384,256]{2,1,0:T(8,128)(2,1)} async-done(((bf16[4,384,256]{2,1,0:T(8,128)(2,1)}), bf16[4,384,256]{2,1,0:T(8,128)(2,1)}, u32[]{:S(2)}, u32[]{:S(2)}) %all-to-all-start.2) | async-done | bytes 786464 | tf_op jit(solution)/shard_map/all_to_all | solution.py:1072
  210.3 3.4 all-to-all-start.1
  213.7 1.9 fusion.2
  215.7 5.3 word_attn.3
  222.8 3.9 all-to-all-start.3
  227.5 2.6 copy.113.refs_6_
  231.1 3.2 copy.111
  234.7 2.7 copy.114.refs_8_
  238.3 12.4 %word_mid.2 = (bf16[256,512]{1,0:T(8,128)(2,1)}, f32[512,256]{1,0:T(8,128)}, bf16[4,128,256]{2,1,0:T(8,128)(2,1)}, f32[512,2048]{1,0:T(8,128)}, f32[2048,512]{1,...) custom-call(bf16[4,128,256]{2,1,0:T(8,128)(2,1)} %copy-done.24, f32[512,256]{1,0:T(8,128)} %get-tuple-element.149.refs_1_, ...), custom_call_target="tpu_custom_call" | custom-call | flops 3623878656 | bytes 20000000 | tf_op jit(solution)/shard_map/word_mid/pallas_call | solution.py:591
  250.8 5.3 all-to-all-start.4
  256.1 13.7 %word_mid.3 = (bf16[256,512]{1,0:T(8,128)(2,1)}, f32[512,256]{1,0:T(8,128)}, bf16[4,128,256]{2,1,0:T(8,128)(2,1)}, bf16[512,2048]{1,0:T(8,128)(2,1)}, bf16[2048,...) custom-call(bf16[4,128,256]{2,1,0:T(8,128)(2,1)} %copy-done.7, ...), custom_call_target="tpu_custom_call" | custom-call | flops 3623878656 | bytes 20000000 | tf_op jit(solution)/shard_map/word_mid/pallas_call | solution.py:591
  269.8 5.1 all-to-all-start.6
  274.9 7.3 %word_attn_back.2 = bf16[4,384,256]{2,1,0:T(8,128)(2,1)} custom-call(bf16[4,384,256]{2,1,0:T(8,128)(2,1)} %copy-done.11, f32[8,256]{1,0:T(8,128)} %get-tuple-element.161.lse_ref, bf16[4,128,256]{2,1,0:T(8,128)(2,1)} %copy-done.26), custom_call_target="tpu_custom_call" | custom-call | flops 10000000000 | bytes 2000000 | tf_op jit(solution)/shard_map/word_attn_back/pallas_call | solution.py:1111
  282.2 5.1 all-to-all-start.5
  287.3 7.4 %word_attn_back.3 = bf16[4,384,256]{2,1,0:T(8,128)(2,1)} custom-call(bf16[4,384,256]{2,1,0:T(8,128)(2,1)} %all-to-all-done.2.triple_ref, f32[8,256]{1,0:T(8,128)} %get-tuple-element.165.lse_ref, bf16[4,128,256]{2,1,0:T(8,128)(2,1)} %copy-done.27), custom_call_target="tpu_custom_call" | custom-call | flops 10000000000 | bytes 2000000 | tf_op jit(solution)/shard_map/word_attn_back/pallas_call | solution.py:1111
  294.7 10.0 %all-to-all-done.5.refs_0_ = bf16[4,384,256]{2,1,0:T(8,128)(2,1)S(1)} async-done(((bf16[4,384,256]{2,1,0:T(8,128)(2,1)}), bf16[4,384,256]{2,1,0:T(8,128)(2,1)S(1)}, u32[]{:S(2)}, u32[]{:S(2)}) %all-to-all-start.5) | async-done | bytes 786464 | tf_op jit(solution)/shard_map/all_to_all | solution.py:1072
  305.5 3.7 all-to-all-start.7
  311.8 1.6 copy.123.refs_3_
  318.6 6.2 %word_out.2 = (f32[256,512]{1,0:T(8,128)}, bf16[512,256]{1,0:T(8,128)(2,1)}, f32[512,1536]{1,0:T(8,128)}, f32[256,512]{1,0:T(8,128)}, f32[512,128]{1,0:T(8,128)}) custom-call(bf16[4,384,256]{2,1,0:T(8,128)(2,1)} %copy-done.5, f32[512,256]{1,0:T(8,128)} %get-tuple-element.149.refs_1_, f32[512,256]{1,0:T(8,128)} %get-tuple-element.163.refs_2_, ...), custom_call_target="tpu_custom_call" | custom-call | flops 805306368 | bytes 8000000 | tf_op jit(solution)/shard_map/word_out/pallas_call | solution.py:1126
  324.8 2.7 all-to-all-done.7.refs_0_
  328.3 6.9 %word_out.3 = (f32[256,512]{1,0:T(8,128)}, bf16[512,256]{1,0:T(8,128)(2,1)}, bf16[512,1536]{1,0:T(8,128)(2,1)}, bf16[256,512]{1,0:T(8,128)(2,1)}, f32[512,128]{1,0:T(8,128)}) custom-call(bf16[4,384,256]{2,1,0:T(8,128)(2,1)} %copy-done.4, f32[512,256]{1,0:T(8,128)} %get-tuple-element.155.refs_1_, f32[512,256]{1,0:T(8,128)} %get-tuple-element.167.refs_2_, ...), custom_call_target="tpu_custom_call" | custom-call | flops 805306368 | bytes 8000000 | tf_op jit(solution)/shard_map/word_out/pallas_call | solution.py:1126
  336.3 31.5 %char_bwd.2 = (f32[256,256]{1,0:T(8,128)}, f32[256,768]{1,0:T(8,128)}, f32[256,256]{1,0:T(8,128)}, f32[256,1024]{1,0:T(8,128)}, f32[1024,256]{1,0:T(8,128)}, /*index=5*/f32[256,128]{1,0:T(8,128)}, f32[256,128]{1,0:T(8,128)}) custom-call(s32[1]{0:T(128)} %get-tuple-element.345.tiles_ref, s32[4,32,128]{2,1,0:T(8,128)} %get-tuple-element.333.refs_0_, ...), custom_call_target="tpu_custom_call" | custom-call | tf_op jit(solution)/shard_map/char_bwd/pallas_call | solution.py:405
  367.8 31.8 %char_bwd.3 = (f32[256,256]{1,0:T(8,128)}, f32[256,768]{1,0:T(8,128)}, f32[256,256]{1,0:T(8,128)}, f32[256,1024]{1,0:T(8,128)}, f32[1024,256]{1,0:T(8,128)}, /*index=5*/f32[256,128]{1,0:T(8,128)}, f32[256,128]{1,0:T(8,128)}) custom-call(s32[1]{0:T(128)} %get-tuple-element.346.tiles_ref, s32[4,32,128]{2,1,0:T(8,128)} %get-tuple-element.334.refs_0_, ...), custom_call_target="tpu_custom_call" | custom-call | tf_op jit(solution)/shard_map/char_bwd/pallas_call | solution.py:405
  402.5 2.2 add_convert_fusion
  408.3 102.7 %reduce_grads.1 = (f32[128,64]{1,0:T(8,128)}, f32[32,640]{1,0:T(8,128)}, f32[128,64]{1,0:T(8,128)}, f32[64,1024]{1,0:T(8,128)}, f32[256,128]{1,0:T(8,128)}, /*index=5*/f32[16,128]{1,0:T(8,128)}, f32[8,128]{1,0:T(8,128)}) custom-call(bf16[4,2,128,256]{3,2,1,0:T(8,128)(2,1)} %add_convert_fusion.2.refs_0_, bf16[4,2,32,768]{3,2,1,0:T(8,128)(2,1)} %bitcast.130, ...), custom_call_target="tpu_custom_call" | custom-call | tf_op jit(solution)/shard_map/reduce_grads/pallas_call | solution.py:926
  511.1 3.7 update.1
  514.7 1.5 copy.134
  517.8 1.5 copy.136
  519.3 1.5 copy.137
  523.9 1.5 copy.141
  525.5 1.5 copy.142
  (153 shorter events, 57.1 us)
Async XLA Ops:
  74.0 3.2 copy-start.39
  74.1 3.2 copy-start.40
  74.1 3.8 copy-start.17
  77.9 4.0 copy-start.16
  79.1 4.0 copy-start.32
  100.5 2.0 copy-start.2
  103.1 4.0 copy-start.14
  103.1 4.8 copy-start.6
  144.5 40.1 %all-to-all-start = ((bf16[4,384,256]{2,1,0:T(8,128)(2,1)}), bf16[4,384,256]{2,1,0:T(8,128)(2,1)S(1)}, u32[]{:S(2)}, u32[]{:S(2)}) async-start(bf16[4,384,256]{2,1,0:T(8,128)(2,1)} %get-tuple-element.147), calls=%async_computation | async-start | bytes 1572864 | tf_op jit(solution)/shard_map/all_to_all | solution.py:1072
  184.6 8.9 %copy-start.11 = (bf16[4,384,256]{2,1,0:T(8,128)(2,1)}, bf16[4,384,256]{2,1,0:T(8,128)(2,1)S(1)}, u32[]{:S(2)}) copy-start(bf16[4,384,256]{2,1,0:T(8,128)(2,1)S(1)} %all-to-all-done.triple_ref) | copy-start | bytes 2359300
  184.6 25.7 %all-to-all-start.2 = ((bf16[4,384,256]{2,1,0:T(8,128)(2,1)}), bf16[4,384,256]{2,1,0:T(8,128)(2,1)}, u32[]{:S(2)}, u32[]{:S(2)}) async-start(bf16[4,384,256]{2,1,0:T(8,128)(2,1)} %get-tuple-element.153), calls=%async_computation.2 | async-start | bytes 1572864 | tf_op jit(solution)/shard_map/all_to_all | solution.py:1072
  210.3 11.8 %all-to-all-start.1 = ((bf16[4,128,256]{2,1,0:T(8,128)(2,1)}), bf16[4,128,256]{2,1,0:T(8,128)(2,1)S(1)}, u32[]{:S(2)}, u32[]{:S(2)}) async-start(bf16[4,128,256]{2,1,0:T(8,128)(2,1)} %get-tuple-element.148), calls=%async_computation.1 | async-start | bytes 524288 | tf_op jit(solution)/shard_map/all_to_all | solution.py:1072
  215.7 11.0 %copy-start.15 = (bf16[2,256,512]{2,1,0:T(8,128)(2,1)S(1)}, bf16[2,256,512]{2,1,0:T(8,128)(2,1)}, u32[]{:S(2)}) copy-start(bf16[2,256,512]{2,1,0:T(8,128)(2,1)} %param.27) | copy-start | bytes 1572868
  222.8 28.0 %all-to-all-start.3 = ((bf16[4,128,256]{2,1,0:T(8,128)(2,1)}), bf16[4,128,256]{2,1,0:T(8,128)(2,1)S(1)}, u32[]{:S(2)}, u32[]{:S(2)}) async-start(bf16[4,128,256]{2,1,0:T(8,128)(2,1)} %get-tuple-element.154), calls=%async_computation.3 | async-start | bytes 524288 | tf_op jit(solution)/shard_map/all_to_all | solution.py:1072
  234.6 2.7 copy-start.1
  250.8 5.3 copy-start.7
  250.8 19.0 %all-to-all-start.4 = ((bf16[4,128,256]{2,1,0:T(8,128)(2,1)}), bf16[4,128,256]{2,1,0:T(8,128)(2,1)S(1)}, u32[]{:S(2)}, u32[]{:S(2)}) async-start(bf16[4,128,256]{2,1,0:T(8,128)(2,1)} %get-tuple-element.162), calls=%async_computation.4 | async-start | bytes 524288 | tf_op jit(solution)/shard_map/all_to_all | solution.py:1072
  269.8 5.1 copy-start.26
  269.8 12.4 %all-to-all-start.6 = ((bf16[4,128,256]{2,1,0:T(8,128)(2,1)}), bf16[4,128,256]{2,1,0:T(8,128)(2,1)S(1)}, u32[]{:S(2)}, u32[]{:S(2)}) async-start(bf16[4,128,256]{2,1,0:T(8,128)(2,1)} %get-tuple-element.166), calls=%async_computation.6 | async-start | bytes 524288 | tf_op jit(solution)/shard_map/all_to_all | solution.py:1072
  282.2 5.1 copy-start.27
  282.2 22.5 %all-to-all-start.5 = ((bf16[4,384,256]{2,1,0:T(8,128)(2,1)}), bf16[4,384,256]{2,1,0:T(8,128)(2,1)S(1)}, u32[]{:S(2)}, u32[]{:S(2)}) async-start(bf16[4,384,256]{2,1,0:T(8,128)(2,1)} %word_attn_back.2), calls=%async_computation.5 | async-start | bytes 1572864 | tf_op jit(solution)/shard_map/all_to_all | solution.py:1072
  287.3 22.0 %copy-start.3 = (bf16[32,8,8,128]{3,1,2,0:T(8,128)(2,1)S(1)}, bf16[32,8,8,128]{3,1,2,0:T(8,128)(2,1)}, u32[]{:S(2)}) copy-start(bf16[32,8,8,128]{3,1,2,0:T(8,128)(2,1)} %copy.155) | copy-start | bytes 1572868
  294.6 15.7 %copy-start.30 = (f32[128,64]{0,1:T(8,128)S(1)}, f32[128,64]{0,1:T(8,128)}, u32[]{:S(2)}) copy-start(f32[128,64]{0,1:T(8,128)} %param.28) | copy-start | bytes 98308
  294.6 16.4 %copy-start.31 = (f32[128,64]{0,1:T(8,128)S(1)}, f32[128,64]{0,1:T(8,128)}, u32[]{:S(2)}) copy-start(f32[128,64]{0,1:T(8,128)} %param.30) | copy-start | bytes 98308
  294.7 17.1 %copy-start = (bf16[512,3,4,128]{0,3,1,2:T(8,128)(2,1)S(1)}, bf16[512,3,4,128]{0,3,1,2:T(8,128)(2,1)}, u32[]{:S(2)}) copy-start(bf16[512,3,4,128]{0,3,1,2:T(8,128)(2,1)} %copy.108) | copy-start | bytes 4718596
  304.7 0.9 copy-start.5
  305.5 21.9 %all-to-all-start.7 = ((bf16[4,384,256]{2,1,0:T(8,128)(2,1)}), bf16[4,384,256]{2,1,0:T(8,128)(2,1)S(1)}, u32[]{:S(2)}, u32[]{:S(2)}) async-start(bf16[4,384,256]{2,1,0:T(8,128)(2,1)} %word_attn_back.3), calls=%async_computation.7 | async-start | bytes 1572864 | tf_op jit(solution)/shard_map/all_to_all | solution.py:1072
  309.3 4.1 copy-start.35
  309.3 4.8 copy-start.36
  309.3 5.5 %copy-start.37 = (f32[128,64]{0,1:T(8,128)S(1)}, f32[128,64]{0,1:T(8,128)}, u32[]{:S(2)}) copy-start(f32[128,64]{0,1:T(8,128)} %param.35) | copy-start | bytes 98308
  309.3 6.3 %copy-start.38 = (f32[128,64]{0,1:T(8,128)S(1)}, f32[128,64]{0,1:T(8,128)}, u32[]{:S(2)}) copy-start(f32[128,64]{0,1:T(8,128)} %param.39) | copy-start | bytes 98308
  310.3 7.2 %copy-start.22 = (f32[512,128]{1,0:T(8,128)S(1)}, f32[512,128]{1,0:T(8,128)}, u32[]{:S(2)}) copy-start(f32[512,128]{1,0:T(8,128)} %get-tuple-element.208) | copy-start | bytes 786436
  310.3 7.4 %copy-start.28 = (bf16[256,512]{1,0:T(8,128)(2,1)S(1)}, bf16[256,512]{1,0:T(8,128)(2,1)}, u32[]{:S(2)}) copy-start(bf16[256,512]{1,0:T(8,128)(2,1)} %get-tuple-element.151) | copy-start | bytes 786436
  310.3 7.4 %copy-start.29 = (bf16[256,512]{1,0:T(8,128)(2,1)S(1)}, bf16[256,512]{1,0:T(8,128)(2,1)}, u32[]{:S(2)}) copy-start(bf16[256,512]{1,0:T(8,128)(2,1)} %get-tuple-element.160) | copy-start | bytes 786436
  327.5 0.9 copy-start.4
  367.8 31.9 %copy-start.34 = (f32[256,128]{1,0:T(8,128)S(1)}, f32[256,128]{1,0:T(8,128)}, u32[]{:S(2)}) copy-start(f32[256,128]{1,0:T(8,128)} %get-tuple-element.203) | copy-start | bytes 393220
  367.8 33.0 %copy-start.33 = (f32[256,128]{1,0:T(8,128)S(1)}, f32[256,128]{1,0:T(8,128)}, u32[]{:S(2)}) copy-start(f32[256,128]{1,0:T(8,128)} %get-tuple-element.205) | copy-start | bytes 393220
  367.8 34.7 %copy-start.9 = (f32[1024,256]{1,0:T(8,128)S(1)}, f32[1024,256]{1,0:T(8,128)}, u32[]{:S(2)}) copy-start(f32[1024,256]{1,0:T(8,128)} %get-tuple-element.197) | copy-start | bytes 3145732
  399.7 5.1 copy-start.8
  399.7 5.1 copy-start.10
  402.5 3.3 copy-start.23
  402.5 3.3 copy-start.25
  404.8 1.7 copy-start.12
  404.8 1.7 copy-start.13
  404.8 2.5 copy-start.20
  404.8 2.5 copy-start.21
  511.0 18.9 %copy-start.18 = (f32[256,512]{1,0:T(8,128)S(1)}, f32[256,512]{1,0:T(8,128)}, u32[]{:S(2)}) copy-start(f32[256,512]{1,0:T(8,128)} %get-tuple-element.164) | copy-start | bytes 1572868
  511.1 18.9 %copy-start.19 = (f32[256,512]{1,0:T(8,128)S(1)}, f32[256,512]{1,0:T(8,128)}, u32[]{:S(2)}) copy-start(f32[256,512]{1,0:T(8,128)} %get-tuple-element.171) | copy-start | bytes 1572868
  (1 other events, 0.7 us)

commit v3 on v2

v3 whole, which is shorter than its diff:
```python
import functools

import jax
import jax.numpy as jnp
from jax import lax
from jax.experimental import pallas as pl
from jax.experimental.pallas import tpu as pltpu
from jax.sharding import PartitionSpec as P

D = 512
HEADS = 8
CD = 256
CHEADS = 4
CFF = 1024
CV = 256
STEP = 5


EPS = 1e-05
CLIP = 1.0
MATRIX_RATE = 0.03
GAIN_RATE = 0.25
MATRIX_DECAY = 0.1
BETA_ONE = 0.5
BETA_TWO = 0.5
ADAM_EPS = 1e-08
NEG_FILL = -1e30
SQRT_HALF = 0.7071067811865476
INV_ROOT_TWO_PI = 0.3989422804014327


ROWS = 512
SLOTS = 16
GROUP = 128
VMEM_BYTES = 56 * 1024 * 1024
ERFC_P = 0.39
ERFC = (0.235325887, 0.091384224, 0.649569841, -0.635413203, 0.886672317, -0.227539068)


def dot_nn(left_side, right_side):
    return lax.dot_general(
        left_side, right_side, (((1,), (0,)), ((), ())), preferred_element_type=jnp.float32
    )


def dot_tn(left_side, right_side):
    return lax.dot_general(
        left_side, right_side, (((0,), (0,)), ((), ())), preferred_element_type=jnp.float32
    )


def dot_nt(left_side, right_side):
    return lax.dot_general(
        left_side, right_side, (((1,), (1,)), ((), ())), preferred_element_type=jnp.float32
    )


def gelu_pair(upper):
    size = jnp.abs(upper)
    t = 1.0 / (1.0 + (ERFC_P * SQRT_HALF) * size)
    poly = ERFC[5]
    for c in ERFC[4::-1]:
        poly = poly * t + c
    bell = jnp.exp(upper * upper * -0.5)
    half = 0.5 * (poly * t * bell)
    phi = jnp.where(upper > 0, 1.0 - half, half)
    return upper * phi, phi + upper * (bell * INV_ROOT_TWO_PI)


def iota(shape, dim):
    return lax.broadcasted_iota(jnp.int32, shape, dim)


def split_two(values):
    high = values.astype(jnp.bfloat16)
    return high, (values - high.astype(jnp.float32)).astype(jnp.bfloat16)


def pack_words(row, ids, out_ref, tiles_ref, seq):
    n = row.shape[1]
    col = jnp.broadcast_to(row.astype(jnp.float32), (8, n)).T[:, :1].astype(jnp.int32)
    sub, lane = iota((n, n), 0), iota((n, n), 1)
    ahead = (row > col) | ((row == col) & (lane < sub))
    rank_col = jnp.sum(ahead.astype(jnp.float32), axis=1, keepdims=True).astype(jnp.int32)
    ahead = (col > row) | ((col == row) & (sub < lane))
    rank_row = jnp.sum(ahead.astype(jnp.float32), axis=0, keepdims=True).astype(jnp.int32)
    clash = (rank_col < rank_row) & (col + row > SLOTS)
    alone = jnp.max(jnp.where(clash, rank_col + rank_row, 0).astype(jnp.float32))
    alone = jnp.maximum(alone.astype(jnp.int32) - n + 2, 0)
    partner = n - 1 + alone - rank_row
    second = (rank_row >= alone) & (rank_row > partner)
    bins = jnp.where(second, partner, rank_row)
    here = sub == bins
    first_map = (here & jnp.logical_not(second)).astype(jnp.float32).astype(jnp.bfloat16)
    second_map = (here & second).astype(jnp.float32).astype(jnp.bfloat16)
    pos = lax.rem(iota((GROUP, n), 0), SLOTS)
    word = iota((GROUP, n), 1) + 1
    wide = jnp.broadcast_to(row, (GROUP, n))
    in_first, in_second = pos < wide, pos >= SLOTS - wide

    def kept(mask, values):
        return jnp.where(mask, values, 0).astype(jnp.float32).astype(jnp.bfloat16)

    groups = n * SLOTS // GROUP
    per = GROUP // SLOTS
    own = iota((groups, per, GROUP), 1) == lax.div(iota((groups, per, GROUP), 2), SLOTS)
    back = jnp.concatenate([ids[SLOTS - 1 - j : SLOTS - j] for j in range(SLOTS)] * per, axis=0)
    ids = jnp.concatenate([ids] * per, axis=0)
    zero = jnp.zeros_like(wide)
    for k, (one, two) in enumerate(
        ((ids + 1, back + 1), (word, word), (zero, SLOTS - wide), (wide, zero + SLOTS))
    ):
        full = dot_nt(first_map, kept(in_first, one)) + dot_nt(second_map, kept(in_second, two))
        full = jnp.where(own, full.reshape(groups, per, GROUP), 0.0)
        out_ref[seq, k] = jnp.sum(full, axis=1).astype(jnp.int32)
    used = alone + lax.div(n - alone + 1, 2)
    tiles_ref[seq] = lax.div(used * SLOTS + ROWS - 1, ROWS)


def pack_kernel(counts_ref, ids_ref, out_ref, tiles_ref):
    for seq in range(ids_ref.shape[0]):
        pack_words(counts_ref[seq : seq + 1, :], ids_ref[seq], out_ref, tiles_ref, seq)


def pack_rows(char_ids, char_counts):
    seqs, words, slots = char_ids.shape
    vmem = pl.BlockSpec(memory_space=pltpu.VMEM)
    return pl.pallas_call(
        pack_kernel,
        in_specs=[vmem, vmem],
        out_specs=[vmem, pl.BlockSpec(memory_space=pltpu.SMEM)],
        out_shape=[
            jax.ShapeDtypeStruct((seqs, 4, words * slots // GROUP, GROUP), jnp.int32),
            jax.ShapeDtypeStruct((seqs,), jnp.int32),
        ],
        name="pack",
    )(char_counts, char_ids.transpose(0, 2, 1))


def tile_maps(pack_ref, step, words):
    per = ROWS // GROUP
    id_rows = pack_ref[0, pl.ds(step * per, per), :]
    word_rows = pack_ref[1, pl.ds(step * per, per), :]
    letters = iota((CV, GROUP), 0) + 1
    spots = iota((words, GROUP), 0) + 1
    one_hot = [
        (letters == id_rows[g : g + 1]).astype(jnp.float32).astype(jnp.bfloat16) for g in range(per)
    ]
    word_map = [
        (spots == word_rows[g : g + 1]).astype(jnp.float32).astype(jnp.bfloat16) for g in range(per)
    ]
    return jnp.concatenate(one_hot, axis=1), jnp.concatenate(word_map, axis=1)


def column_rms(values):
    inverse = lax.rsqrt(jnp.mean(values * values, axis=0, keepdims=True) + EPS)
    return values * inverse, inverse


def own_block():
    shape = (GROUP // SLOTS, SLOTS, CHEADS * GROUP)
    return iota(shape, 0) == lax.div(lax.rem(iota(shape, 2), GROUP), SLOTS)


def to_compact(block, own):
    return jnp.sum(jnp.where(own, block.reshape(own.shape), 0.0), axis=0)


def from_compact(compact, own):
    wide = jnp.broadcast_to(compact[None], own.shape)
    return jnp.where(own, wide, 0.0).astype(jnp.bfloat16).reshape(GROUP, -1)


def spread_heads(values):
    head = values.shape[0] // CHEADS
    zero = jnp.zeros((head, GROUP), values.dtype)
    rows = []
    for h in range(CHEADS):
        parts = [zero] * CHEADS
        parts[h] = values[h * head : (h + 1) * head]
        rows.append(jnp.concatenate(parts, axis=1))
    return jnp.concatenate(rows, axis=0)


def char_fwd_kernel(tiles_ref, *refs):
    @pl.when(pl.program_id(0) < tiles_ref[0])
    def _():
        char_fwd_tile(*refs)


def char_fwd_tile(
    pack_ref, table_ref, qkv_ref, out_ref, up_ref, down_ref, g1_ref, g2_ref,
    pooled_ref, keep_values, keep_probs, keep_qkv, keep_mixed, keep_first, keep_hidden, keep_slope,
):
    step = pl.program_id(0)
    words = pooled_ref.shape[0]
    per = ROWS // GROUP
    head = CD // CHEADS

    @pl.when(step == 0)
    def _():
        pooled_ref[...] = jnp.zeros_like(pooled_ref)

    one_hot, word_map = tile_maps(pack_ref, step, words)
    embedded = dot_nn(table_ref[...], one_hot)
    act_one = (column_rms(embedded)[0] * g1_ref[...]).astype(jnp.bfloat16)
    triple = dot_nn(qkv_ref[...], act_one).astype(jnp.bfloat16)
    keep_qkv[...] = triple
    low_rows = pack_ref[2, pl.ds(step * per, per), :]
    high_rows = pack_ref[3, pl.ds(step * per, per), :]
    own = own_block()
    key_pos = iota((SLOTS, GROUP), 0)
    key_rows = triple[CD : 2 * CD].T
    keep_values[...] = triple[2 * CD :].T
    mixed = []
    for g in range(per):
        valid = (key_pos >= low_rows[g : g + 1]) & (key_pos < high_rows[g : g + 1])
        valid = jnp.concatenate([valid.astype(jnp.float32)] * CHEADS, axis=1) > 0
        lanes = slice(g * GROUP, (g + 1) * GROUP)
        scores = to_compact(dot_nn(key_rows[lanes], spread_heads(triple[:CD, lanes])), own)
        scores = jnp.where(valid, scores * head**-0.5, NEG_FILL)
        powers = jnp.exp(scores - jnp.max(scores, axis=0, keepdims=True))
        powers = jnp.where(valid, powers, 0.0)
        total = jnp.sum(powers, axis=0, keepdims=True)
        probs = powers / jnp.where(total > 0, total, 1.0)
        keep_probs[:, g * CHEADS * GROUP : (g + 1) * CHEADS * GROUP] = probs
        probs = from_compact(probs, own)
        parts = []
        for h in range(CHEADS):
            v = triple[2 * CD + h * head : 2 * CD + (h + 1) * head, lanes]
            parts.append(dot_nn(v, probs[:, h * GROUP : (h + 1) * GROUP]).astype(jnp.bfloat16))
        mixed.append(jnp.concatenate(parts, axis=0))
    mixed = jnp.concatenate(mixed, axis=1)
    keep_mixed[...] = mixed
    first = embedded + dot_nn(out_ref[...], mixed)
    keep_first[...] = first
    act_two = (column_rms(first)[0] * g2_ref[...]).astype(jnp.bfloat16)
    branch = None
    for c in range(CFF // CD):
        rows = slice(c * CD, (c + 1) * CD)
        hidden, slope = gelu_pair(dot_nn(up_ref[rows, :], act_two))
        hidden = hidden.astype(jnp.bfloat16)
        keep_hidden[rows, :] = hidden
        keep_slope[rows, :] = slope.astype(jnp.bfloat16)
        part = dot_nn(down_ref[:, rows], hidden)
        branch = part if branch is None else branch + part
    high, low = split_two(first + branch)
    pooled_ref[...] += dot_nt(word_map, high) + dot_nt(word_map, low)


KEPT = (
    (3 * CD, jnp.bfloat16),
    (CD, jnp.bfloat16),
    (CD, jnp.float32),
    (CFF, jnp.bfloat16),
    (CFF, jnp.bfloat16),
)


def kept_specs():
    return [
        pl.BlockSpec((ROWS, CD), lambda t, n: (kept_place(t, n)[1], 0)),
        pl.BlockSpec((SLOTS, CHEADS * ROWS), kept_place),
    ] + [pl.BlockSpec((depth, ROWS), kept_place) for depth, _ in KEPT]


def kept_shapes(rows):
    return [
        jax.ShapeDtypeStruct((rows, CD), jnp.bfloat16),
        jax.ShapeDtypeStruct((SLOTS, CHEADS * rows), jnp.float32),
    ] + [jax.ShapeDtypeStruct((depth, rows), dtype) for depth, dtype in KEPT]


def whole(array):
    zeros = (0,) * array.ndim
    return pl.BlockSpec(array.shape, lambda *_: zeros)


def kept_place(step, tiles):
    return 0, jnp.minimum(step, tiles[0] - 1)


def char_fwd(tiles, pack, weights, words):
    rows = words * SLOTS
    operands = (pack,) + weights
    return pl.pallas_call(
        char_fwd_kernel,
        grid_spec=pltpu.PrefetchScalarGridSpec(
            num_scalar_prefetch=1,
            grid=(rows // ROWS,),
            in_specs=[whole(a) for a in operands],
            out_specs=[pl.BlockSpec((words, CD), lambda t, n: (0, 0))]
            + kept_specs(),
        ),
        out_shape=[jax.ShapeDtypeStruct((words, CD), jnp.float32)] + kept_shapes(rows),
        compiler_params=pltpu.CompilerParams(vmem_limit_bytes=VMEM_BYTES),
        name="char_fwd",
    )(tiles, *operands)


def fold_lanes(values):
    total = values[:, :GROUP]
    for g in range(1, values.shape[1] // GROUP):
        total = total + values[:, g * GROUP : (g + 1) * GROUP]
    return total


def column_rms_back(grad_in, gain, normed, inverse):
    scaled = grad_in * gain
    return inverse * (scaled - normed * jnp.mean(scaled * normed, axis=0, keepdims=True))


def char_bwd_kernel(tiles_ref, *refs):
    @pl.when(pl.program_id(0) < tiles_ref[0])
    def _():
        char_bwd_tile(tiles_ref[0] - 1, *refs)


def char_bwd_tile(
    last, pack_ref, spread_ref, table_ref, qkv_ref, out_ref, up_ref, down_ref, g1_ref, g2_ref,
    keep_values, keep_probs, keep_qkv, keep_mixed, keep_first, keep_hidden, keep_slope,
    *refs,
):
    sums = 7
    earlier, results, totals = (), refs[-2 * sums : -sums], refs[-sums:]
    if len(refs) == 3 * sums - 1:
        earlier = refs[: sums - 1]
    d_table, d_qkv, d_out, d_up, d_down, d_g1, d_g2 = totals
    step = pl.program_id(0)
    words = spread_ref.shape[1]
    per = ROWS // GROUP
    head = CD // CHEADS

    @pl.when(step == 0)
    def _():
        d_table[...] = jnp.zeros_like(d_table)
        for i, ref in enumerate(totals[1:]):
            ref[...] = earlier[i][...] if earlier else jnp.zeros_like(ref)

    one_hot, word_map = tile_maps(pack_ref, step, words)
    halves = dot_nn(spread_ref[...], word_map)
    grad_second = halves[:CD] + halves[CD:]
    grad_branch = grad_second.astype(jnp.bfloat16)
    first = keep_first[...]
    normed_two, inverse_two = column_rms(first)
    act_two = (normed_two * g2_ref[...]).astype(jnp.bfloat16)
    grad_act_two = None
    for c in range(CFF // CD):
        rows = slice(c * CD, (c + 1) * CD)
        d_down[rows, :] += dot_nt(keep_hidden[rows, :], grad_branch)
        grad_upper = dot_nn(down_ref[rows, :], grad_branch) * keep_slope[rows, :].astype(
            jnp.float32
        )
        grad_upper = grad_upper.astype(jnp.bfloat16)
        d_up[:, rows] += dot_nt(act_two, grad_upper)
        part = dot_nn(up_ref[:, rows], grad_upper)
        grad_act_two = part if grad_act_two is None else grad_act_two + part
    d_g2[...] += fold_lanes(grad_act_two * normed_two)
    grad_first = grad_second + column_rms_back(
        grad_act_two, g2_ref[...], normed_two, inverse_two
    )
    grad_attn = grad_first.astype(jnp.bfloat16)
    d_out[...] += dot_nt(keep_mixed[...], grad_attn)
    grad_mixed = dot_nn(out_ref[...], grad_attn).astype(jnp.bfloat16)
    own = own_block()
    triple = keep_qkv[...]
    columns = []
    for g in range(per):
        lanes = slice(g * GROUP, (g + 1) * GROUP)
        wide = slice(g * CHEADS * GROUP, (g + 1) * CHEADS * GROUP)
        probs = keep_probs[:, wide]
        grad_probs = to_compact(
            dot_nn(keep_values[lanes, :], spread_heads(grad_mixed[:, lanes])), own
        )
        grad_scores = probs * (
            grad_probs - jnp.sum(probs * grad_probs, axis=0, keepdims=True)
        )
        grad_raw = from_compact(grad_scores * head**-0.5, own)
        probs = from_compact(probs, own)
        gq, gk, gv = [], [], []
        for h in range(CHEADS):
            q = triple[h * head : (h + 1) * head, lanes]
            k = triple[CD + h * head : CD + (h + 1) * head, lanes]
            grad_o = grad_mixed[h * head : (h + 1) * head, lanes]
            part = slice(h * GROUP, (h + 1) * GROUP)
            gq.append(dot_nn(k, grad_raw[:, part]).astype(jnp.bfloat16))
            gk.append(dot_nt(q, grad_raw[:, part]).astype(jnp.bfloat16))
            gv.append(dot_nt(grad_o, probs[:, part]).astype(jnp.bfloat16))
        columns.append(jnp.concatenate(gq + gk + gv, axis=0))
    grad_triple = jnp.concatenate(columns, axis=1)
    embedded = dot_nn(table_ref[...], one_hot)
    normed_one, inverse_one = column_rms(embedded)
    act_one = (normed_one * g1_ref[...]).astype(jnp.bfloat16)
    d_qkv[...] += dot_nt(act_one, grad_triple)
    grad_act_one = dot_nn(qkv_ref[...], grad_triple)
    d_g1[...] += fold_lanes(grad_act_one * normed_one)
    back_one = column_rms_back(grad_act_one, g1_ref[...], normed_one, inverse_one)
    grad_embedded = (grad_first + back_one).astype(jnp.bfloat16)
    d_table[...] += dot_nt(one_hot, grad_embedded)

    @pl.when(step == last)
    def _():
        for ref, total in zip(results, totals):
            ref[...] = total[...].astype(ref.dtype)


def char_bwd(tiles, pack, spread, weights, kept, earlier):
    operands = (pack, spread) + weights
    shapes = ((CV, CD), (CD, 3 * CD), (CD, CD), (CD, CFF), (CFF, CD), (CD, GROUP), (CD, GROUP))
    f32, bf16 = jnp.float32, jnp.bfloat16
    kinds = [f32] * 7 if earlier is None else [f32] + [bf16] * 4 + [f32] * 2
    earlier = () if earlier is None else tuple(earlier)
    return pl.pallas_call(
        char_bwd_kernel,
        grid_spec=pltpu.PrefetchScalarGridSpec(
            num_scalar_prefetch=1,
            grid=(kept[0].shape[0] // ROWS,),
            in_specs=[whole(a) for a in operands] + kept_specs() + [whole(a) for a in earlier],
            out_specs=[pl.BlockSpec(s, lambda t, n: (0, 0)) for s in shapes],
            scratch_shapes=[pltpu.VMEM(s, f32) for s in shapes],
        ),
        out_shape=[jax.ShapeDtypeStruct(s, kind) for s, kind in zip(shapes, kinds)],
        compiler_params=pltpu.CompilerParams(vmem_limit_bytes=VMEM_BYTES),
        name="char_bwd",
    )(tiles, *operands, *kept, *earlier)


def adam_step(weight, grad, first_old, second_old, clip_factor, rate, decay):
    clipped = grad * clip_factor
    first_new = BETA_ONE * first_old + (1.0 - BETA_ONE) * clipped
    second_new = BETA_TWO * second_old + (1.0 - BETA_TWO) * clipped * clipped
    first_hat = first_new / (1.0 - BETA_ONE**STEP)
    second_hat = second_new / (1.0 - BETA_TWO**STEP)
    weight_new = weight - rate * (first_hat / (jnp.sqrt(second_hat) + ADAM_EPS) + decay * weight)
    return (grad, first_new, second_new, weight_new, weight_new.astype(jnp.bfloat16))


class Ring:
    def __init__(self, dp, ranks):
        self.chips, self.ranks = dp // 2, ranks
        self.d, self.h = lax.axis_index("dp"), lax.axis_index("head")
        self.chip, self.core = lax.div(self.d, 2), lax.rem(self.d, 2)

    def sibling(self):
        return (self.d + 1 - 2 * self.core, self.h)

    def chip_at(self, k):
        return lax.rem(self.chip + k, self.chips)

    def plane(self, k):
        return (2 * self.chip_at(k) + self.core, self.h)

    def rank_at(self, k):
        return lax.rem(self.h + k, self.ranks)

    def line(self, k):
        return (self.d, self.rank_at(k))

    def meet(self):
        barrier = pltpu.get_barrier_semaphore()
        peers = [self.sibling()]
        peers += [self.plane(k) for k in range(1, self.chips)]
        peers += [self.line(k) for k in range(1, self.ranks)]
        for peer in peers:
            pl.semaphore_signal(barrier, inc=1, device_id=peer, device_id_type=pl.DeviceIdType.MESH)
        pl.semaphore_wait(barrier, len(peers))


def send(src, dst, sems, place, peer):
    copy = pltpu.make_async_remote_copy(
        src_ref=src,
        dst_ref=dst,
        send_sem=sems.at[(0,) + place],
        recv_sem=sems.at[(1,) + place],
        device_id=peer,
        device_id_type=pl.DeviceIdType.MESH,
    )
    copy.start()
    return copy


def word_scores(q, k, diagonal):
    scores = dot_tn(k, q) * (D // HEADS) ** -0.5
    if diagonal:
        scores = jnp.where(iota(scores.shape, 0) <= iota(scores.shape, 1), scores, NEG_FILL)
    return scores


def head_rows(ref, seq, part, kind, h):
    head = D // HEADS
    start = pl.multiple_of(kind * (ref.shape[2] // 3) + h * head, head)
    return ref[seq, part, pl.ds(start, head), :]


def word_attention(seq, triple_ref, mixed_ref, lse_ref):
    parts, depth, _ = triple_ref.shape[1:]
    head = D // HEADS

    def one_head(h, carry):
        start = pl.multiple_of(h * head, head)
        for i in range(parts):
            q = head_rows(triple_ref, seq, i, 0, h)
            scores = [
                word_scores(q, head_rows(triple_ref, seq, j, 1, h), i == j) for j in range(i + 1)
            ]
            highest = jnp.max(scores[0], axis=0, keepdims=True)
            for block in scores[1:]:
                highest = jnp.maximum(highest, jnp.max(block, axis=0, keepdims=True))
            powers = [jnp.exp(block - highest) for block in scores]
            total = jnp.sum(powers[0], axis=0, keepdims=True)
            for block in powers[1:]:
                total = total + jnp.sum(block, axis=0, keepdims=True)
            inverse = 1.0 / total
            mixed = None
            for j, block in enumerate(powers):
                v = head_rows(triple_ref, seq, j, 2, h)
                part = dot_nn(v, (block * inverse).astype(jnp.bfloat16))
                mixed = part if mixed is None else mixed + part
            mixed_ref[seq, i, pl.ds(start, head), :] = mixed.astype(jnp.bfloat16)
            lse_ref[seq, h, i] = jnp.broadcast_to(highest + jnp.log(total), lse_ref.shape[3:])
        return carry

    lax.fori_loop(0, depth // 3 // head, one_head, 0)


def word_attention_back(seq, triple_ref, lse_ref, grad_ref, out_ref, dk, dv):
    parts, depth, _ = triple_ref.shape[1:]
    head = D // HEADS
    own = depth // 3

    def one_head(h, carry):
        start = pl.multiple_of(h * head, head)
        for i in range(parts):
            q = head_rows(triple_ref, seq, i, 0, h)
            grad_o = grad_ref[seq, i, pl.ds(start, head), :]
            lse = lse_ref[seq, h, i][:1]
            probs, grads = [], []
            dot_sum = None
            for j in range(i + 1):
                scores = word_scores(q, head_rows(triple_ref, seq, j, 1, h), i == j)
                probs.append(jnp.exp(scores - lse))
                grads.append(dot_tn(head_rows(triple_ref, seq, j, 2, h), grad_o))
                part = jnp.sum(probs[-1] * grads[-1], axis=0, keepdims=True)
                dot_sum = part if dot_sum is None else dot_sum + part
            grad_q = None
            for j in range(i + 1):
                k = head_rows(triple_ref, seq, j, 1, h)
                raw = (probs[j] * (grads[j] - dot_sum) * head**-0.5).astype(jnp.bfloat16)
                part = dot_nn(k, raw)
                grad_q = part if grad_q is None else grad_q + part
                part_k = dot_nt(q, raw)
                part_v = dot_nt(grad_o, probs[j].astype(jnp.bfloat16))
                if i == j:
                    dk[j] = part_k
                    dv[j] = part_v
                else:
                    dk[j] += part_k
                    dv[j] += part_v
            out_ref[seq, i, pl.ds(start, head), :] = grad_q.astype(jnp.bfloat16)
        for j in range(parts):
            k_start = pl.multiple_of(own + h * head, head)
            v_start = pl.multiple_of(2 * own + h * head, head)
            out_ref[seq, j, pl.ds(k_start, head), :] = dk[j].astype(jnp.bfloat16)
            out_ref[seq, j, pl.ds(v_start, head), :] = dv[j].astype(jnp.bfloat16)
        return carry

    lax.fori_loop(0, own // head, one_head, 0)


def swap_start(ring, src, dst, seq, sems):
    copies = [
        send(src.at[seq, ring.rank_at(k)], dst.at[seq, ring.h], sems, (seq, k), ring.line(k))
        for k in range(1, ring.ranks)
    ]
    dst[seq, ring.h] = src[seq, ring.h]
    return copies


def wait_all(copies):
    for copy in copies:
        copy.wait()


def word_fwd_kernel(dp, ranks, *refs):
    (sum_ref, count_ref, words_ref, pool_ref, early_ref, g3_ref, up_rows, down_rows) = refs[:8]
    (start_ref, pooled_ref, triple_in, lse_ref, mixed_in, up_ref, down_ref) = refs[8:15]
    triple_ref, mixed_ref, own_sem, late_sem, pair_sem, triple_sem, mixed_sem = refs[15:]
    ring = Ring(dp, ranks)
    ring.meet()
    wide = early_ref.shape[1]
    late = ((up_rows.at[:, wide:], up_ref), (down_rows, down_ref))
    own, planes, pairs = [], [], []
    for m, (rows, out) in enumerate(late):
        own.append(pltpu.make_async_copy(rows, out.at[ring.d], own_sem.at[m]))
        own[-1].start()
        planes.append(
            [
                send(rows, out.at[ring.d], late_sem, (m, k), ring.plane(k))
                for k in range(1, ring.chips)
            ]
        )
        pairs.append(send(rows, out.at[ring.d], pair_sem, (m, 0), ring.sibling()))
    seqs = words_ref.shape[0]
    part = D // ranks
    moving = []
    for s in range(seqs):
        pooled = (sum_ref[s] / count_ref[s]).T.astype(jnp.bfloat16)
        pooled_ref[s] = pooled
        start = words_ref[s].astype(jnp.float32).T + dot_tn(pool_ref[...], pooled)
        start_ref[s] = start
        act = (column_rms(start)[0] * g3_ref[...]).astype(jnp.bfloat16)
        for t in range(3):
            triple = dot_tn(early_ref[:, t * D : (t + 1) * D], act).astype(jnp.bfloat16)
            for r in range(ranks):
                triple_ref[s, r, t * part : (t + 1) * part, :] = triple[r * part : (r + 1) * part]
        moving.append(swap_start(ring, triple_ref, triple_in, s, triple_sem))
    for m, (_, out) in enumerate(late):
        for k in range(1, ring.chips):
            planes[m][k - 1].wait_recv()
            block = out.at[2 * ring.chip_at(ring.chips - k) + ring.core]
            pairs.append(send(block, block, pair_sem, (m, k), ring.sibling()))
    back = []
    for s in range(seqs):
        wait_all(moving[s])
        word_attention(s, triple_in, mixed_ref, lse_ref)
        back.append(swap_start(ring, mixed_ref, mixed_in, s, mixed_sem))
    for m in range(2):
        own[m].wait()
        for copy in planes[m]:
            copy.wait_send()
    wait_all(pairs)
    for copies in back:
        wait_all(copies)


def word_fwd(sums, counts, words, pool, early, g3, up_rows, down_rows, collective):
    dp, ranks = lax.axis_size("dp"), lax.axis_size("head")
    seqs, width, _ = words.shape
    part = D // ranks
    bf16, f32 = jnp.bfloat16, jnp.float32
    vmem = pl.BlockSpec(memory_space=pltpu.VMEM)
    anywhere = pl.BlockSpec(memory_space=pl.ANY)
    triple = (seqs, ranks, 3 * part, width)
    mixed = (seqs, ranks, part, width)
    late = up_rows.shape[1] - early.shape[1]
    dma = pltpu.SemaphoreType.DMA
    return pl.pallas_call(
        functools.partial(word_fwd_kernel, dp, ranks),
        in_specs=[vmem] * 6 + [anywhere] * 2,
        out_specs=[vmem] * 5 + [anywhere] * 2,
        out_shape=[
            jax.ShapeDtypeStruct((seqs, D, width), f32),
            jax.ShapeDtypeStruct((seqs, CD, width), bf16),
            jax.ShapeDtypeStruct(triple, bf16),
            jax.ShapeDtypeStruct((seqs, HEADS // ranks, ranks, 8, width), f32),
            jax.ShapeDtypeStruct(mixed, bf16),
            jax.ShapeDtypeStruct((dp, up_rows.shape[0], late), bf16),
            jax.ShapeDtypeStruct((dp,) + down_rows.shape, bf16),
        ],
        scratch_shapes=[
            pltpu.VMEM(triple, bf16),
            pltpu.VMEM(mixed, bf16),
            dma((2,)),
            dma((2, 2, dp // 2)),
            dma((2, 2, dp // 2)),
            dma((2, seqs, ranks)),
            dma((2, seqs, ranks)),
        ],
        compiler_params=pltpu.CompilerParams(
            collective_id=collective, has_side_effects=True, vmem_limit_bytes=VMEM_BYTES
        ),
        name="word_fwd",
    )(sums, counts, words, pool, early, g3, up_rows, down_rows)


def word_bwd_kernel(dp, ranks, *refs):
    (start_ref, pooled_ref, triple_in, lse_ref, mixed_in, cot_ref, count_ref) = refs[:7]
    (pool_ref, early_ref, up_ref, down_ref, g3_ref, g4_ref) = refs[7:13]
    (output_ref, input_grad_ref, spread_ref, d_qkv, d_pool, d_g3, d_g4) = refs[13:20]
    sums = refs[20:23]
    (acts, hiddens, grad_ups, cots, lows, mixes, triples) = refs[23:30]
    (afters, mixed_ref, mixed_back, triple_ref, triple_back, dk, dv) = refs[30:37]
    grads, pair_in, plane_in = refs[37:40], refs[40:43], refs[43:46]
    mixed_sem, triple_sem, pair_sem, plane_sem = refs[46:]
    ring = Ring(dp, ranks)
    chips = ring.chips
    f32, bf16 = jnp.float32, jnp.bfloat16
    ring.meet()
    seqs, _, width = start_ref.shape
    hidden_size = up_ref.shape[1]
    part = D // ranks
    pairs, planes = {}, {}

    def put_grad(i, value):
        grads[i][...] = value.astype(bf16).reshape(grads[i].shape)
        pairs[i] = send(
            grads[i].at[:, 1 - ring.core], pair_in[i], pair_sem, (i,), ring.sibling()
        )

    def pass_on(i):
        pairs[i].wait()

        def add_pair(p, carry):
            both = grads[i][p, ring.core].astype(f32) + pair_in[i][p].astype(f32)
            pair_in[i][p] = both.astype(bf16)
            return carry

        lax.fori_loop(0, chips, add_pair, 0)
        planes[i] = [
            send(
                pair_in[i].at[ring.chip_at(k)], plane_in[i].at[k], plane_sem, (i, k), ring.plane(k)
            )
            for k in range(1, chips)
        ]

    moving = []
    gain = None
    for s in range(seqs):
        lanes = slice(s * width, (s + 1) * width)
        mixed = mixed_in[s].reshape(D, width)
        mixes[:, lanes] = mixed
        after = start_ref[s] + dot_tn(early_ref[:, 3 * D :], mixed)
        normed, inverse = column_rms(after)
        act = (normed * g4_ref[...]).astype(bf16)
        acts[:, lanes] = act
        cot = cot_ref[s].astype(f32).T
        cot_low = cot.astype(bf16)
        cots[:, lanes] = cot_low
        result, grad = after, None
        for c in range(hidden_size // D):
            rows = slice(c * D, (c + 1) * D)
            hidden, slope = gelu_pair(dot_tn(up_ref[:, rows], act))
            hidden = hidden.astype(bf16)
            hiddens[rows, lanes] = hidden
            result = result + dot_tn(down_ref[rows, :], hidden)
            grad_upper = (dot_nn(down_ref[rows, :], cot_low) * slope).astype(bf16)
            grad_ups[rows, lanes] = grad_upper
            piece = dot_nn(up_ref[:, rows], grad_upper)
            grad = piece if grad is None else grad + piece
        output_ref[s] = result.T.astype(bf16)
        piece = fold_lanes(grad * normed)
        gain = piece if gain is None else gain + piece
        total = cot + column_rms_back(grad, g4_ref[...], normed, inverse)
        afters[s] = total
        low = total.astype(bf16)
        lows[:, lanes] = low
        mixed_ref[s] = dot_nn(early_ref[:, 3 * D :], low).astype(bf16).reshape(ranks, part, width)
        moving.append(swap_start(ring, mixed_ref, mixed_back, s, mixed_sem))
    d_g4[...] = gain
    put_grad(0, dot_nt(hiddens[...], cots[...]))
    moved = []
    for s in range(seqs):
        wait_all(moving[s])
        word_attention_back(s, triple_in, lse_ref, mixed_back, triple_ref, dk, dv)
        moved.append(swap_start(ring, triple_ref, triple_back, s, triple_sem))
        if s == 0:
            pass_on(0)
    put_grad(1, dot_nt(acts[...], grad_ups[...]))
    put_grad(2, dot_nt(mixes[...], lows[...]))
    pass_on(1)
    pass_on(2)
    gain = None
    for s in range(seqs):
        lanes = slice(s * width, (s + 1) * width)
        wait_all(moved[s])
        for t in range(3):
            for r in range(ranks):
                triples[t * D + r * part : t * D + (r + 1) * part, lanes] = triple_back[
                    s, r, t * part : (t + 1) * part, :
                ]
        normed, inverse = column_rms(start_ref[s])
        acts[:, lanes] = (normed * g3_ref[...]).astype(bf16)
        grad = dot_nn(early_ref[:, : 3 * D], triples[:, lanes])
        piece = fold_lanes(grad * normed)
        gain = piece if gain is None else gain + piece
        total = afters[s] + column_rms_back(grad, g3_ref[...], normed, inverse)
        input_grad_ref[s] = total.T
        low = total.astype(bf16)
        lows[:, lanes] = low
        high, rest = split_two(dot_nn(pool_ref[...], low) / count_ref[s])
        spread_ref[s, :CD, :] = high
        spread_ref[s, CD:, :] = rest
    d_g3[...] = gain
    d_qkv[...] = dot_nt(acts[...], triples[...]).astype(bf16)
    d_pool[...] = sum(
        dot_nt(pooled_ref[s], lows[:, s * width : (s + 1) * width]) for s in range(seqs)
    ).astype(bf16)
    for i in range(3):
        total = pair_in[i][ring.chip].astype(f32)
        for k in range(1, chips):
            planes[i][k - 1].wait()
            total = total + plane_in[i][k].astype(f32)
        sums[i][...] = total.astype(bf16)


def word_bwd(saved, cot, counts, weights, gains, collective):
    dp, ranks = lax.axis_size("dp"), lax.axis_size("head")
    start, pooled, triple, lse, mixed = saved
    pool, early, up, down = weights
    seqs, _, width = start.shape
    hidden = up.shape[1]
    chips = dp // 2
    bf16, f32 = jnp.bfloat16, jnp.float32
    vmem = pl.BlockSpec(memory_space=pltpu.VMEM)
    rows = ((hidden // dp, D), (D // dp, hidden), (D // dp, D))
    columns = seqs * width
    dma = pltpu.SemaphoreType.DMA
    operands = (*saved, cot, counts, pool, early, up, down, *gains)
    shapes = [
        ((seqs, width, D), bf16),
        ((seqs, width, D), f32),
        ((seqs, 2 * CD, width), bf16),
        ((D, 3 * D), bf16),
        ((CD, D), bf16),
        ((D, GROUP), f32),
        ((D, GROUP), f32),
    ] + [(r, bf16) for r in rows]
    return pl.pallas_call(
        functools.partial(word_bwd_kernel, dp, ranks),
        in_specs=[vmem] * len(operands),
        out_specs=[vmem] * len(shapes),
        out_shape=[jax.ShapeDtypeStruct(shape, kind) for shape, kind in shapes],
        scratch_shapes=[
            pltpu.VMEM((D, columns), bf16),
            pltpu.VMEM((hidden, columns), bf16),
            pltpu.VMEM((hidden, columns), bf16),
            pltpu.VMEM((D, columns), bf16),
            pltpu.VMEM((D, columns), bf16),
            pltpu.VMEM((D, columns), bf16),
            pltpu.VMEM((3 * D, columns), bf16),
            pltpu.VMEM((seqs, D, width), f32),
            pltpu.VMEM(mixed.shape, bf16),
            pltpu.VMEM(mixed.shape, bf16),
            pltpu.VMEM(triple.shape, bf16),
            pltpu.VMEM(triple.shape, bf16),
            pltpu.VMEM((ranks, D // HEADS, width), f32),
            pltpu.VMEM((ranks, D // HEADS, width), f32),
        ]
        + [pltpu.VMEM((chips, 2) + r, bf16) for r in rows]
        + [pltpu.VMEM((chips,) + r, bf16) for r in rows] * 2
        + [
            dma((2, seqs, ranks)),
            dma((2, seqs, ranks)),
            dma((2, 3)),
            dma((2, 3, chips)),
        ],
        compiler_params=pltpu.CompilerParams(
            collective_id=collective, has_side_effects=True, vmem_limit_bytes=VMEM_BYTES
        ),
        name="word_bwd",
    )(*operands)


def gather_kernel(dp, ranks, *refs):
    shards, outs, low = refs[:5], refs[5:11], refs[11:16]
    own_sem, line_sem, plane_sem, pair_sem, copy_sem = refs[16:]
    table, char_in, down, early, word_rows, down_rows = outs
    ring = Ring(dp, ranks)
    for shard, ref in zip(shards, low):
        ref[...] = shard[...].astype(jnp.bfloat16)
    ring.meet()

    def column(ref, like):
        wide = like.shape[1]
        return ref.at[:, pl.ds(pl.multiple_of(ring.h * wide, GROUP), wide)]

    places = (
        table.at[ring.d, ring.h],
        column(char_in.at[ring.d], low[1]),
        down.at[ring.d, ring.h],
        column(word_rows, low[3]),
        column(down_rows, low[4]),
    )
    own, first = [], []

    def along_line(m):
        own.append(pltpu.make_async_copy(low[m], places[m], own_sem.at[m]))
        own[m].start()
        first.append(
            [send(low[m], places[m], line_sem, (m, k), ring.line(k)) for k in range(1, ranks)]
        )

    def arrived(m):
        own[m].wait()
        for copy in first[m]:
            copy.wait_recv()

    blocks = (table, char_in, down, early)
    second, sent = [], []

    def onward(m, block):
        place = blocks[m].at[ring.d]
        second.append(
            [send(block, place, plane_sem, (m, k), ring.plane(k)) for k in range(1, ring.chips)]
        )
        sent.append(send(block, place, pair_sem, (m, 0), ring.sibling()))

    for m in range(3):
        along_line(m)
    for m in range(3):
        arrived(m)
        onward(m, blocks[m].at[ring.d])
    along_line(3)
    along_line(4)
    arrived(3)
    block = word_rows.at[:, : early.shape[2]]
    copy = pltpu.make_async_copy(block, early.at[ring.d], copy_sem)
    copy.start()
    onward(3, block)
    for m in range(4):
        for k in range(1, ring.chips):
            second[m][k - 1].wait_recv()
            block = blocks[m].at[2 * ring.chip_at(ring.chips - k) + ring.core]
            sent.append(send(block, block, pair_sem, (m, k), ring.sibling()))
    arrived(4)
    copy.wait()
    wait_all(sent)
    for m in range(5):
        for copy in first[m]:
            copy.wait_send()
    for m in range(4):
        for copy in second[m]:
            copy.wait_send()


def gather(shards, collective):
    dp, ranks = lax.axis_size("dp"), lax.axis_size("head")
    bf16 = jnp.bfloat16
    vmem = pl.BlockSpec(memory_space=pltpu.VMEM)
    anywhere = pl.BlockSpec(memory_space=pl.ANY)
    table, char_in, down, word_in, word_down = (s.shape for s in shards)
    dma = pltpu.SemaphoreType.DMA
    outs = [
        (dp, ranks) + table,
        (dp, char_in[0], ranks * char_in[1]),
        (dp, ranks) + down,
        (dp, word_in[0], 4 * D),
        (word_in[0], ranks * word_in[1]),
        (word_down[0], ranks * word_down[1]),
    ]
    return pl.pallas_call(
        functools.partial(gather_kernel, dp, ranks),
        in_specs=[vmem] * 5,
        out_specs=[anywhere] * 6,
        out_shape=[jax.ShapeDtypeStruct(s, bf16) for s in outs],
        scratch_shapes=[pltpu.VMEM(s.shape, bf16) for s in shards]
        + [
            dma((5,)),
            dma((2, 5, ranks)),
            dma((2, 4, dp // 2)),
            dma((2, 4, dp // 2)),
            dma(()),
        ],
        compiler_params=pltpu.CompilerParams(
            collective_id=collective, has_side_effects=True, vmem_limit_bytes=VMEM_BYTES
        ),
        name="gather",
    )(*shards)


def column_cuts(widths, ranks):
    block = sum(widths) // ranks
    cuts, start = [], 0
    for width in widths:
        mine, at = [], 0
        while at < width:
            rank, inside = divmod(start + at, block)
            take = min(width - at, block - inside)
            mine.append((rank, at, at + take, inside))
            at += take
        cuts.append(mine)
        start += width
    return cuts


def reduce_kernel(dp, ranks, groups, extra, *refs):
    pieces = sum(len(g) - done for g, done in groups)
    mats = len(groups)
    parts = refs[:pieces]
    gain_ref = refs[pieces]
    ready = refs[pieces + 1 : pieces + 1 + extra]
    place = pieces + 1 + extra
    outs = refs[place : place + mats]
    gain_out, square_out = refs[place + mats : place + mats + 2]
    place += mats + 2
    pair_in = refs[place : place + pieces]
    pair_sum = refs[place + pieces : place + 2 * pieces]
    plane_in = refs[place + 2 * pieces : place + 3 * pieces]
    place += 3 * pieces
    line_sum, line_in = refs[place : place + mats], refs[place + mats : place + 2 * mats]
    place += 2 * mats
    small, pair_sem, plane_sem, line_sem, small_sem = refs[place:]
    ring = Ring(dp, ranks)
    chips = ring.chips
    f32, bf16 = jnp.float32, jnp.bfloat16
    ring.meet()
    sent = []

    def share(slot, value, stage):
        others, here, count = (
            (lambda k: ring.sibling(), ring.core, 2),
            (ring.plane, ring.chip, chips),
            (ring.line, ring.h, ranks),
        )[stage]
        small[slot, stage, here] = value
        copies = []
        for k in range(1, count):
            spot = small.at[slot, stage, here]
            copies.append(send(spot, spot, small_sem, (slot, stage, k), others(k)))
        return copies

    def shared(slot, copies, stage):
        for copy in copies:
            copy.wait()
        count = (2, chips, ranks)[stage]
        total = small[slot, stage, 0]
        for k in range(1, count):
            total = total + small[slot, stage, k]
        return total

    def total_of(slot, value):
        for stage in range(3):
            value = shared(slot, share(slot, value, stage), stage)
        return value

    pairs = [
        send(parts[i].at[:, 1 - ring.core], pair_in[i], pair_sem, (i,), ring.sibling())
        for i in range(pieces)
    ]
    gain = shared(0, share(0, gain_ref[...], 0), 0)
    planes = []
    for i in range(pieces):
        pairs[i].wait()

        def add_pair(p, carry, i=i):
            both = parts[i][p, ring.core].astype(f32) + pair_in[i][p].astype(f32)
            pair_sum[i][p] = both.astype(bf16)
            return carry

        lax.fori_loop(0, chips, add_pair, 0)
        planes.append(
            [
                send(
                    pair_sum[i].at[ring.chip_at(k)],
                    plane_in[i].at[k],
                    plane_sem,
                    (i, k),
                    ring.plane(k),
                )
                for k in range(1, chips)
            ]
        )
    gain = shared(0, share(0, gain, 1), 1)
    gain_out[...] = shared(0, share(0, gain, 2), 2)
    lines, i, j = [], 0, 0
    for m, (widths, done) in enumerate(groups):
        for at, cuts in enumerate(column_cuts(widths, ranks)):
            if at < len(widths) - done:
                total = pair_sum[i][ring.chip].astype(f32)
                for k in range(1, chips):
                    planes[i][k - 1].wait()
                    total = total + plane_in[i][k].astype(f32)
                total = total.astype(bf16)
                i += 1
            else:
                total = ready[j][...]
                j += 1
            for rank, first, last, inside in cuts:
                line_sum[m][rank, :, inside : inside + last - first] = total[:, first:last]
        lines.append(
            [
                send(
                    line_sum[m].at[ring.rank_at(k)], line_in[m].at[k], line_sem, (m, k), ring.line(k)
                )
                for k in range(1, ranks)
            ]
        )
    square = jnp.zeros(square_out.shape, f32)

    def squares(value):
        value = value * value
        rows, cols = value.shape
        if cols % GROUP:
            value = jnp.concatenate([value, jnp.zeros((rows, GROUP - cols % GROUP), f32)], axis=1)
        return jnp.sum(fold_lanes(value).reshape(rows // 8, 8, GROUP), axis=0)

    for m in range(mats):
        total = line_sum[m][ring.h].astype(f32)
        for k in range(1, ranks):
            lines[m][k - 1].wait()
            total = total + line_in[m][k].astype(f32)
        outs[m][...] = total
        square = square + squares(total)
    small_square = jnp.concatenate([square, jnp.zeros_like(square)], axis=0)
    square_out[...] = total_of(1, small_square)[:8]


def reduce_grads(groups, gains, collective):
    dp, ranks = lax.axis_size("dp"), lax.axis_size("head")
    chips = dp // 2
    bf16, f32 = jnp.bfloat16, jnp.float32
    pieces, ready, widths, shards = [], [], [], []
    for group, done in groups:
        rows = done[0].shape[0] if done else group[0].shape[0] // dp
        pieces += [p.reshape(chips, 2, rows, p.shape[1]) for p in group]
        ready += done
        widths.append((tuple(p.shape[1] for p in group + done), len(done)))
        shards.append((rows, sum(widths[-1][0]) // ranks))
    blocks = [p.shape[2:] for p in pieces]
    vmem = pl.BlockSpec(memory_space=pltpu.VMEM)
    n, mats = len(pieces), len(groups)
    return pl.pallas_call(
        functools.partial(reduce_kernel, dp, ranks, widths, len(ready)),
        in_specs=[vmem] * (n + 1 + len(ready)),
        out_specs=[vmem] * (mats + 2),
        out_shape=[jax.ShapeDtypeStruct(s, f32) for s in shards]
        + [jax.ShapeDtypeStruct(gains.shape, f32), jax.ShapeDtypeStruct((8, GROUP), f32)],
        scratch_shapes=[pltpu.VMEM((chips,) + b, bf16) for b in blocks] * 3
        + [pltpu.VMEM((ranks,) + s, bf16) for s in shards] * 2
        + [
            pltpu.VMEM((2, 3, max(2, chips, ranks)) + gains.shape, f32),
            pltpu.SemaphoreType.DMA((2, n)),
            pltpu.SemaphoreType.DMA((2, n, chips)),
            pltpu.SemaphoreType.DMA((2, mats, ranks)),
            pltpu.SemaphoreType.DMA((2, 2, 3, max(2, chips, ranks))),
        ],
        compiler_params=pltpu.CompilerParams(
            collective_id=collective, has_side_effects=True, vmem_limit_bytes=VMEM_BYTES
        ),
        name="reduce_grads",
    )(*pieces, gains, *ready)


def update_kernel(count, *refs):
    weights, grads = refs[:count], refs[count : 2 * count]
    firsts, seconds = refs[2 * count : 3 * count], refs[3 * count : 4 * count]
    square_ref = refs[4 * count]
    norm_ref, outs = refs[4 * count + 1], refs[4 * count + 2 :]
    gain_grad = grads[-1][...]
    square = jnp.sum(square_ref[...]) + jnp.sum(gain_grad * gain_grad)
    norm = jnp.sqrt(jnp.full((1, GROUP), square, jnp.float32))
    norm_ref[...] = norm
    clip_factor = jnp.minimum(1.0, CLIP / norm)[:, :1]
    for i in range(count):
        gains = i == count - 1
        result = adam_step(
            weights[i][...],
            grads[i][...],
            firsts[i][...],
            seconds[i][...],
            clip_factor,
            GAIN_RATE if gains else MATRIX_RATE,
            0.0 if gains else MATRIX_DECAY,
        )
        for ref, value in zip(outs[5 * i : 5 * i + 5], result):
            ref[...] = value


def update(weights, grads, firsts, seconds, square):
    count = len(weights)
    shapes = [jax.ShapeDtypeStruct((1, GROUP), jnp.float32)]
    for w in weights:
        shapes += [jax.ShapeDtypeStruct(w.shape, jnp.float32)] * 4
        shapes.append(jax.ShapeDtypeStruct(w.shape, jnp.bfloat16))
    return pl.pallas_call(
        functools.partial(update_kernel, count),
        out_shape=shapes,
        compiler_params=pltpu.CompilerParams(vmem_limit_bytes=VMEM_BYTES),
        name="update",
    )(*weights, *grads, *firsts, *seconds, square)


def body(
    char_ids,
    char_counts,
    language,
    words_in,
    out_cotangent,
    char_table,
    char_in,
    char_down,
    word_in,
    word_down,
    norm_gains,
    old_table_first,
    old_table_second,
    old_char_in_first,
    old_char_in_second,
    old_char_down_first,
    old_char_down_second,
    old_word_in_first,
    old_word_in_second,
    old_word_down_first,
    old_word_down_second,
    old_gains_first,
    old_gains_second,
):
    bf16, f32 = jnp.bfloat16, jnp.float32
    packed, tiles = pack_rows(char_ids, char_counts)
    table_t_low, char_in_low, char_down_t, early, up_rows, down_rows = gather(
        (char_table.T, char_in, char_down.T, word_in, word_down), 0
    )

    def joined(block):
        dp, ranks, cols, rows = block.shape
        return block.transpose(1, 2, 0, 3).reshape(ranks * cols, dp * rows)

    def stacked(block):
        return block.reshape(-1, block.shape[2])

    table_t_low, char_down_t = joined(table_t_low), joined(char_down_t)
    char_in_low, early = stacked(char_in_low), stacked(early)
    seq_count, local_words = (words_in.shape[0], words_in.shape[1])
    languages = table_t_low.shape[1] // CV

    def lanes(gain, width):
        return jnp.broadcast_to(gain[:, None], (gain.shape[0], width))

    gains = (lanes(norm_gains[:CD], ROWS), lanes(norm_gains[CD : 2 * CD], ROWS))
    g3 = lanes(norm_gains[2 * CD : 2 * CD + D], local_words)
    g4 = lanes(norm_gains[2 * CD + D :], local_words)
    table_t = [
        lax.dynamic_slice_in_dim(table_t_low, language[i] * CV, CV, axis=1)
        for i in range(seq_count)
    ]
    char_parts = (
        char_in_low[:, : 3 * CD],
        char_in_low[:, 3 * CD : 4 * CD],
        char_in_low[:, 4 * CD : 4 * CD + CFF],
        char_down_t.T,
    )
    flipped = tuple(part.T for part in char_parts[:3]) + (char_down_t,)
    pool = char_in_low[:, 4 * CD + CFF :]
    count_row = char_counts.astype(f32)[:, None, :]
    count_col = char_counts.astype(f32)[:, :, None]
    seqs = range(seq_count)
    kept, sums = [], []
    for i in seqs:
        total, *saved = char_fwd(
            tiles[i : i + 1], packed[i], (table_t[i],) + flipped + gains, local_words
        )
        kept.append(saved)
        sums.append(total)
    *saved, up, down = word_fwd(
        jnp.stack(sums), count_col, words_in, pool, early, g3, up_rows, down_rows, 1
    )
    (
        output,
        input_grad,
        spread,
        grad_qkv,
        grad_pool,
        gain_three,
        gain_four,
        down_sum,
        up_sum,
        out_sum,
    ) = word_bwd(
        tuple(saved),
        out_cotangent,
        count_row,
        (pool, early, stacked(up), stacked(down)),
        (g3, g4),
        2,
    )
    last, tables_out = None, []
    for i in seqs:
        one_table, *last = char_bwd(
            tiles[i : i + 1],
            packed[i],
            spread[i],
            (table_t[i],) + char_parts + gains,
            kept[i],
            last,
        )
        tables_out.append(one_table)
    grad_table = sum(
        jnp.where(
            (jnp.arange(languages) == language[i])[:, None, None], tables_out[i][None], 0.0
        )
        for i in seqs
    ).reshape(-1, CD)
    c_qkv, c_out, c_up, c_down, gain_one, gain_two = last
    gain_grads = jnp.concatenate(
        [jnp.sum(g, axis=1) for g in (gain_one, gain_two, gain_three, gain_four)]
    )
    flat = (gain_grads.shape[0] // GROUP, GROUP)
    rest = 16 - flat[0]
    *shards, gains_sum, square = reduce_grads(
        [
            ([grad_table.astype(bf16)], []),
            ([c_qkv.astype(bf16), c_out.astype(bf16), c_up.astype(bf16), grad_pool], []),
            ([c_down.astype(bf16)], []),
            ([grad_qkv], [out_sum, up_sum]),
            ([], [down_sum]),
        ],
        jnp.pad(gain_grads.reshape(flat), ((0, rest), (0, 0))),
        3,
    )

    def turned(parts):
        parts = list(parts)
        parts[0], parts[2] = parts[0].T, parts[2].T
        parts[5] = parts[5].reshape(flat)
        return parts

    norm, *updated = update(
        turned((char_table, char_in, char_down, word_in, word_down, norm_gains)),
        turned((*shards, gains_sum[: flat[0]])),
        turned(
            (
                old_table_first,
                old_char_in_first,
                old_char_down_first,
                old_word_in_first,
                old_word_down_first,
                old_gains_first,
            )
        ),
        turned(
            (
                old_table_second,
                old_char_in_second,
                old_char_down_second,
                old_word_in_second,
                old_word_down_second,
                old_gains_second,
            )
        ),
        square,
    )
    for place in (*range(5), *range(10, 15)):
        updated[place] = updated[place].T
    updated[-5:] = [part.reshape(norm_gains.shape) for part in updated[-5:]]
    return (output, input_grad, norm[0, 0], *updated)


def solution(mesh):
    return jax.shard_map(
        body,
        mesh=mesh,
        in_specs=(
            P("dp", "head", None),
            P("dp", "head"),
            P("dp"),
            P("dp", "head", None),
            P("dp", "head", None),
            P("dp", "head"),
            P("dp", "head"),
            P("dp", "head"),
            P("dp", "head"),
            P("dp", "head"),
            P(),
            P("dp", "head"),
            P("dp", "head"),
            P("dp", "head"),
            P("dp", "head"),
            P("dp", "head"),
            P("dp", "head"),
            P("dp", "head"),
            P("dp", "head"),
            P("dp", "head"),
            P("dp", "head"),
            P(),
            P(),
        ),
        out_specs=(
            P("dp", "head", None),
            P("dp", "head", None),
            P(),
            P("dp", "head"),
            P("dp", "head"),
            P("dp", "head"),
            P("dp", "head"),
            P("dp", "head"),
            P("dp", "head"),
            P("dp", "head"),
            P("dp", "head"),
            P("dp", "head"),
            P("dp", "head"),
            P("dp", "head"),
            P("dp", "head"),
            P("dp", "head"),
            P("dp", "head"),
            P("dp", "head"),
            P("dp", "head"),
            P("dp", "head"),
            P("dp", "head"),
            P("dp", "head"),
            P("dp", "head"),
            P("dp", "head"),
            P("dp", "head"),
            P("dp", "head"),
            P("dp", "head"),
            P("dp", "head"),
            P(),
            P(),
            P(),
            P(),
            P(),
        ),
        check_vma=False,
    )
```

time: 542 us -> 410 us (0.76); the launches traced: 531 us -> 406 us
  local copies, waits for them, and re-layouts: 80.4 us -> 27.2 us
  starting transfers between devices: 38.3 us -> 0 us
  waiting for transfers between devices: 25.4 us -> 0 us
  other arithmetic: 18.4 us -> 9.98 us
    all_to_all x8 -> x0, starting transfers between devices: 38.3 us -> none  [swap(): return lax.all_to_all(values, 'head', 0, 0, tiled=True)]
    pallas_call x1, Pallas kernels: 103 us -> 74.5 us  [reduce_grads(): pl.pallas_call(functools.partial(reduce_kernel, dp, ranks, widths, len(re...]
    pallas_call x12 -> x4, Pallas kernels: 138 us -> 165 us  [the longest x1 63.4 us: word_fwd(): pl.pallas_call(functools.partial(word_fwd_kernel, dp, ranks), in_specs=[v...]
    unnamed x103 -> x18, local copies, waits for them, and re-layouts: 28.8 us -> 1.99 us
    all_to_all x8 -> x0, waiting for transfers between devices: 25.4 us -> none  [swap(): return lax.all_to_all(values, 'head', 0, 0, tiled=True)]
    transpose x9 -> x2, local copies, waits for them, and re-layouts: 18.5 us -> 1.86 us  [joined(): return block.transpose(1, 2, 0, 3).reshape(ranks * cols, dp * rows)]
    convert_element_type x9 -> x1, other arithmetic: 10.8 us -> 0.68 us  [body(): count_col = char_counts.astype(f32)[:, :, None]]
    slice x5 -> x0, local copies, waits for them, and re-layouts: 6.71 us -> none  [the longest x1 3.41 us: body(): up = word_in_low[:, 4 * D:]]
  transfers between devices with their start and end apart: 8 -> 0, of which waited for: 4 -> 0; matrix products, arithmetic and copies ran while one was open for 5% -> 0% of each run, Pallas kernels for 17% -> 0%
where the time goes in v3:
time: 410 us; the launch traced here: 406 us
  Pallas kernels  366 us (89%)
  local copies, waits for them, and re-layouts  27.2 us (7%)
  other arithmetic  9.98 us (2%)
    pallas_call x1, Pallas kernels, reduce_grads(): pl.pallas_call(functools.partial(reduce_kernel, dp, ranks, widths, len(re...  74.5 us
    pallas_call x2, Pallas kernels, char_bwd(): pl.pallas_call(char_bwd_kernel, grid_spec=pltpu.PrefetchScalarGridSpec(nu...  64.2 us
    pallas_call x1, Pallas kernels, word_fwd(): pl.pallas_call(functools.partial(word_fwd_kernel, dp, ranks), in_specs=[v...  63.4 us
    pallas_call x1, Pallas kernels, word_bwd(): pl.pallas_call(functools.partial(word_bwd_kernel, dp, ranks), in_specs=[v...  60.7 us
    pallas_call x2, Pallas kernels, char_fwd(): pl.pallas_call(char_fwd_kernel, grid_spec=pltpu.PrefetchScalarGridSpec(nu...  58.8 us
    pallas_call x1, Pallas kernels, gather(): pl.pallas_call(functools.partial(gather_kernel, dp, ranks), in_specs=[vme...  38.4 us

profile of v3, /device:TPU:0, one launch (start us, length us, event | category | flops | bytes accessed | tf_op | source)
XLA Modules:
  0.0 405.8 jit_solution(595462876299610557)
XLA Ops:
  0.7 1.3 fusion.6
  3.3 1.3 iota_compare_fusion
  4.6 0.8 fusion.4
  5.4 0.7 fusion.5
  6.1 0.6 broadcast_in_dim.73.refs_6_
  6.6 0.7 fusion.3
  7.3 2.8 pack.1
  10.1 1.3 fusion.7
  11.4 1.5 slice_bitcast_fusion.3
  13.0 0.9 copy.77.refs_1_
  13.8 0.9 broadcast_in_dim.74.refs_12_
  14.8 0.9 broadcast_in_dim.70.refs_7_.refs_8_
  15.7 0.9 broadcast_in_dim.69.refs_6_.refs_7_
  16.6 1.0 broadcast_in_dim.72.refs_5_.refs_11_
  17.6 38.4 %gather.1 = (bf16[8,4,64,128]{3,2,1,0:T(8,128)(2,1)}, bf16[8,32,2560]{2,1,0:T(8,128)(2,1)}, bf16[8,4,64,128]{3,2,1,0:T(8,128)(2,1)}, bf16[8,64,2048]{2,1,0:T(8,1...) custom-call(f32[64,128]{1,0:T(8,128)} %bitcast.104, f32[32,640]{1,0:T(8,128)} %refs_1_.3, ...), custom_call_target="tpu_custom_call" | custom-call | tf_op jit(solution)/shard_map/gather/pallas_call | solution.py:941
  56.0 1.5 copy.69
  57.5 0.1 copy.86
  57.6 0.8 constant_dynamic-slice_fusion.1
  58.4 0.8 copy.72.refs_3_
  59.1 0.7 slice.81.refs_3_.refs_7_
  59.9 0.3 copy.70
  60.2 0.1 copy.85
  60.3 1.0 copy.78
  61.3 0.8 fusion.2
  62.1 0.9 fusion
  63.1 1.0 copy.73.refs_4_
  64.1 0.9 copy.71.refs_2_
  65.0 29.6 %char_fwd.3 = (f32[256,256]{1,0:T(8,128)}, bf16[4096,256]{1,0:T(8,128)(2,1)}, f32[16,16384]{1,0:T(8,128)}, bf16[768,4096]{1,0:T(8,128)(2,1)}, bf16[256,4096]{1,0...) custom-call(s32[1]{0:T(128)} %get-tuple-element.240.tiles_ref, ...), custom_call_target="tpu_custom_call" | custom-call | tf_op jit(solution)/shard_map/char_fwd/pallas_call | solution.py:286
  94.6 29.2 %char_fwd.2 = (f32[256,256]{1,0:T(8,128)}, bf16[4096,256]{1,0:T(8,128)(2,1)}, f32[16,16384]{1,0:T(8,128)}, bf16[768,4096]{1,0:T(8,128)(2,1)}, bf16[256,4096]{1,0...) custom-call(s32[1]{0:T(128)} %get-tuple-element.239.tiles_ref, ...), custom_call_target="tpu_custom_call" | custom-call | tf_op jit(solution)/shard_map/char_fwd/pallas_call | solution.py:286
  123.8 1.8 pad_maximum_fusion.refs_0_
  125.6 63.4 %word_fwd.1 = (f32[2,512,256]{2,1,0:T(8,128)}, bf16[2,256,256]{2,1,0:T(8,128)(2,1)}, bf16[2,4,384,256]{3,2,1,0:T(8,128)(2,1)}, f32[2,2,4,8,256]{4,3,2,1,0:T(8,12...) custom-call(f32[2,256,256]{2,1,0:T(8,128)} %pad_maximum_fusion.refs_0_, ...), custom_call_target="tpu_custom_call" | custom-call | tf_op jit(solution)/shard_map/word_fwd/pallas_call | solution.py:647
  189.0 60.7 %word_bwd.1 = (bf16[2,256,512]{2,1,0:T(8,128)(2,1)}, f32[2,256,512]{2,1,0:T(8,128)}, bf16[2,512,256]{2,1,0:T(8,128)(2,1)}, bf16[512,1536]{1,0:T(8,128)(2,1)}, bf...) custom-call(f32[2,512,256]{2,1,0:T(8,128)} %get-tuple-element.136.re, ...), custom_call_target="tpu_custom_call" | custom-call | tf_op jit(solution)/shard_map/word_bwd/pallas_call | solution.py:818
  249.7 1.1 reduce_sum.38
  250.8 1.1 reduce_sum.39
  251.9 1.9 slice_bitcast_fusion.1
  253.7 31.9 %char_bwd.2 = (f32[256,256]{1,0:T(8,128)}, f32[256,768]{1,0:T(8,128)}, f32[256,256]{1,0:T(8,128)}, f32[256,1024]{1,0:T(8,128)}, f32[1024,256]{1,0:T(8,128)}, /*index=5*/f32[256,128]{1,0:T(8,128)}, f32[256,128]{1,0:T(8,128)}) custom-call(s32[1]{0:T(128)} %get-tuple-element.239.tiles_ref, s32[4,32,128]{2,1,0:T(8,128)} %get-tuple-element.229.refs_0_, ...), custom_call_target="tpu_custom_call" | custom-call | tf_op jit(solution)/shard_map/char_bwd/pallas_call | solution.py:413
  285.7 0.0 copy-start.5
  285.7 32.3 %char_bwd.3 = (f32[256,256]{1,0:T(8,128)}, bf16[256,768]{1,0:T(8,128)(2,1)}, bf16[256,256]{1,0:T(8,128)(2,1)}, bf16[256,1024]{1,0:T(8,128)(2,1)}, bf16[1024,256]...) custom-call(s32[1]{0:T(128)} %get-tuple-element.240.tiles_ref, s32[4,32,128]{2,1,0:T(8,128)} %get-tuple-element.230.refs_0_, ...), custom_call_target="tpu_custom_call" | custom-call | tf_op jit(solution)/shard_map/char_bwd/pallas_call | solution.py:413
  318.0 2.0 add_convert_fusion.refs_0_
  319.9 1.0 reduce_sum.36
  321.0 1.0 reduce_sum.37
  322.0 0.6 pad.4.refs_7_
  322.6 74.5 %reduce_grads.1 = (f32[128,64]{1,0:T(8,128)}, f32[32,640]{1,0:T(8,128)}, f32[128,64]{1,0:T(8,128)}, f32[64,1024]{1,0:T(8,128)}, f32[256,128]{1,0:T(8,128)}, /*index=5*/f32[16,128]{1,0:T(8,128)}, f32[8,128]{1,0:T(8,128)}) custom-call(bf16[4,2,128,256]{3,2,1,0:T(8,128)(2,1)} %add_convert_fusion.refs_0_, bf16[4,2,32,768]{3,2,1,0:T(8,128)(2,1)} %bitcast.98, ...), custom_call_target="tpu_custom_call" | custom-call | tf_op jit(solution)/shard_map/reduce_grads/pallas_call | solution.py:1112
  397.1 1.7 copy.79
  398.8 1.5 copy.80
  400.3 3.3 update.1
  403.6 0.8 copy.89
  404.4 1.0 copy.90
  (14 shorter events, 0.0 us)
Async XLA Ops:
  56.0 1.6 copy-start.1
  56.0 3.9 copy-start.4
  60.3 3.8 copy-start
  94.6 29.2 %copy-start.6 = (f32[256,256]{1,0:T(8,128)S(1)}, f32[256,256]{1,0:T(8,128)}, u32[]{:S(2)}) copy-start(f32[256,256]{1,0:T(8,128)} %get-tuple-element.132) | copy-start | bytes 786436
  285.7 32.3 %copy-start.5 = (f32[256,256]{1,0:T(8,128)S(1)}, f32[256,256]{1,0:T(8,128)}, u32[]{:S(2)}) copy-start(f32[256,256]{1,0:T(8,128)} %get-tuple-element.153) | copy-start | bytes 786436
  397.1 6.5 %copy-start.3 = (bf16[2,256,512]{2,1,0:T(8,128)(2,1)S(1)}, bf16[2,256,512]{2,1,0:T(8,128)(2,1)}, u32[]{:S(2)}) copy-start(bf16[2,256,512]{2,1,0:T(8,128)(2,1)} %get-tuple-element.278) | copy-start | bytes 1572868
  397.1 7.3 %copy-start.2 = (f32[2,256,512]{2,1,0:T(8,128)S(1)}, f32[2,256,512]{2,1,0:T(8,128)}, u32[]{:S(2)}) copy-start(f32[2,256,512]{2,1,0:T(8,128)} %get-tuple-element.279) | copy-start | bytes 3145732

commit v4 on v3

--- a/solution.py
+++ b/solution.py
@@ -31,10 +31,9 @@
 
 ROWS = 512
 SLOTS = 16
+CHAINS = 1
 GROUP = 128
 VMEM_BYTES = 56 * 1024 * 1024
-ERFC_P = 0.39
-ERFC = (0.235325887, 0.091384224, 0.649569841, -0.635413203, 0.886672317, -0.227539068)
 
 
 def dot_nn(left_side, right_side):
@@ -56,14 +55,8 @@
 
 
 def gelu_pair(upper):
-    size = jnp.abs(upper)
-    t = 1.0 / (1.0 + (ERFC_P * SQRT_HALF) * size)
-    poly = ERFC[5]
-    for c in ERFC[4::-1]:
-        poly = poly * t + c
+    phi = 0.5 + 0.5 * lax.erf(upper * SQRT_HALF)
     bell = jnp.exp(upper * upper * -0.5)
-    half = 0.5 * (poly * t * bell)
-    phi = jnp.where(upper > 0, 1.0 - half, half)
     return upper * phi, phi + upper * (bell * INV_ROOT_TWO_PI)
 
 
@@ -102,6 +95,7 @@
         return jnp.where(mask, values, 0).astype(jnp.float32).astype(jnp.bfloat16)
 
     groups = n * SLOTS // GROUP
+    spare = out_ref.shape[2] - groups
     per = GROUP // SLOTS
     own = iota((groups, per, GROUP), 1) == lax.div(iota((groups, per, GROUP), 2), SLOTS)
     back = jnp.concatenate([ids[SLOTS - 1 - j : SLOTS - j] for j in range(SLOTS)] * per, axis=0)
@@ -112,49 +106,68 @@
     ):
         full = dot_nt(first_map, kept(in_first, one)) + dot_nt(second_map, kept(in_second, two))
         full = jnp.where(own, full.reshape(groups, per, GROUP), 0.0)
-        out_ref[seq, k] = jnp.sum(full, axis=1).astype(jnp.int32)
+        full = jnp.sum(full, axis=1).astype(jnp.int32)
+        if spare:
+            full = jnp.concatenate([full, jnp.zeros((spare, GROUP), jnp.int32)], axis=0)
+        out_ref[seq, k] = full
     used = alone + lax.div(n - alone + 1, 2)
     tiles_ref[seq] = lax.div(used * SLOTS + ROWS - 1, ROWS)
 
 
-def pack_kernel(counts_ref, ids_ref, out_ref, tiles_ref):
-    for seq in range(ids_ref.shape[0]):
-        pack_words(counts_ref[seq : seq + 1, :], ids_ref[seq], out_ref, tiles_ref, seq)
-
-
-def pack_rows(char_ids, char_counts):
-    seqs, words, slots = char_ids.shape
-    vmem = pl.BlockSpec(memory_space=pltpu.VMEM)
-    return pl.pallas_call(
-        pack_kernel,
-        in_specs=[vmem, vmem],
-        out_specs=[vmem, pl.BlockSpec(memory_space=pltpu.SMEM)],
-        out_shape=[
-            jax.ShapeDtypeStruct((seqs, 4, words * slots // GROUP, GROUP), jnp.int32),
-            jax.ShapeDtypeStruct((seqs,), jnp.int32),
-        ],
-        name="pack",
-    )(char_counts, char_ids.transpose(0, 2, 1))
-
-
-def tile_maps(pack_ref, step, words):
-    per = ROWS // GROUP
-    id_rows = pack_ref[0, pl.ds(step * per, per), :]
-    word_rows = pack_ref[1, pl.ds(step * per, per), :]
-    letters = iota((CV, GROUP), 0) + 1
-    spots = iota((words, GROUP), 0) + 1
-    one_hot = [
-        (letters == id_rows[g : g + 1]).astype(jnp.float32).astype(jnp.bfloat16) for g in range(per)
+def lane_map(rows, size):
+    spots = iota((size, GROUP), 0) + 1
+    maps = [
+        (spots == rows[g : g + 1]).astype(jnp.float32).astype(jnp.bfloat16)
+        for g in range(rows.shape[0])
     ]
-    word_map = [
-        (spots == word_rows[g : g + 1]).astype(jnp.float32).astype(jnp.bfloat16) for g in range(per)
-    ]
-    return jnp.concatenate(one_hot, axis=1), jnp.concatenate(word_map, axis=1)
+    return jnp.concatenate(maps, axis=1)
+
+
+def in_step(chains):
+    results = [None] * len(chains)
+    waiting = list(enumerate(chains))
+    running = []
+    while waiting or running:
+        if waiting:
+            running.append(waiting.pop(0))
+        for item in list(running):
+            try:
+                next(item[1])
+            except StopIteration as stop:
+                results[item[0]] = stop.value
+                running.remove(item)
+    return results
+
+
+def lane_copies(ref, width):
+    return jnp.concatenate([ref[...]] * (width // GROUP), axis=1)
 
 
 def column_rms(values):
     inverse = lax.rsqrt(jnp.mean(values * values, axis=0, keepdims=True) + EPS)
     return values * inverse, inverse
+
+
+def tile_count(words):
+    return -(-words * SLOTS // ROWS)
+
+
+def tile_at(step, tiles_ref, seqs):
+    seq, start, total = 0, 0, tiles_ref[0]
+    for s in range(1, seqs):
+        past = step >= total
+        seq, start = jnp.where(past, s, seq), jnp.where(past, total, start)
+        total = total + tiles_ref[s]
+    return seq, step - start, total
+
+
+def placed(seqs, index):
+    def place(step, tiles_ref, language_ref):
+        total = tile_at(step, tiles_ref, seqs)[2]
+        seq, tile, _ = tile_at(jnp.minimum(step, total - 1), tiles_ref, seqs)
+        return index(seq, tile, language_ref)
+
+    return place
 
 
 def own_block():
@@ -182,18 +195,20 @@
     return jnp.concatenate(rows, axis=0)
 
 
-def char_fwd_kernel(tiles_ref, *refs):
-    @pl.when(pl.program_id(0) < tiles_ref[0])
+def char_fwd_kernel(seqs, tiles_ref, language_ref, *refs):
+    step = pl.program_id(0)
+    _, tile, total = tile_at(step, tiles_ref, seqs)
+
+    @pl.when(step < total)
     def _():
-        char_fwd_tile(*refs)
+        char_fwd_tile(tile, *refs)
 
 
 def char_fwd_tile(
-    pack_ref, table_ref, qkv_ref, out_ref, up_ref, down_ref, g1_ref, g2_ref,
-    pooled_ref, keep_values, keep_probs, keep_qkv, keep_mixed, keep_first, keep_hidden, keep_slope,
+    step, pack_ref, table_ref, in_ref, down_ref, g1_ref, g2_ref, pooled_ref,
+    keep_values, keep_probs, keep_qkv, keep_mixed, keep_first, keep_hidden, keep_slope,
 ):
-    step = pl.program_id(0)
-    words = pooled_ref.shape[0]
+    words = pooled_ref.shape[1]
     per = ROWS // GROUP
     head = CD // CHEADS
 
@@ -201,51 +216,71 @@
     def _():
         pooled_ref[...] = jnp.zeros_like(pooled_ref)
 
-    one_hot, word_map = tile_maps(pack_ref, step, words)
-    embedded = dot_nn(table_ref[...], one_hot)
-    act_one = (column_rms(embedded)[0] * g1_ref[...]).astype(jnp.bfloat16)
-    triple = dot_nn(qkv_ref[...], act_one).astype(jnp.bfloat16)
-    keep_qkv[...] = triple
-    low_rows = pack_ref[2, pl.ds(step * per, per), :]
-    high_rows = pack_ref[3, pl.ds(step * per, per), :]
     own = own_block()
     key_pos = iota((SLOTS, GROUP), 0)
-    key_rows = triple[CD : 2 * CD].T
-    keep_values[...] = triple[2 * CD :].T
-    mixed = []
-    for g in range(per):
-        valid = (key_pos >= low_rows[g : g + 1]) & (key_pos < high_rows[g : g + 1])
-        valid = jnp.concatenate([valid.astype(jnp.float32)] * CHEADS, axis=1) > 0
-        lanes = slice(g * GROUP, (g + 1) * GROUP)
-        scores = to_compact(dot_nn(key_rows[lanes], spread_heads(triple[:CD, lanes])), own)
-        scores = jnp.where(valid, scores * head**-0.5, NEG_FILL)
-        powers = jnp.exp(scores - jnp.max(scores, axis=0, keepdims=True))
-        powers = jnp.where(valid, powers, 0.0)
-        total = jnp.sum(powers, axis=0, keepdims=True)
-        probs = powers / jnp.where(total > 0, total, 1.0)
-        keep_probs[:, g * CHEADS * GROUP : (g + 1) * CHEADS * GROUP] = probs
-        probs = from_compact(probs, own)
-        parts = []
-        for h in range(CHEADS):
-            v = triple[2 * CD + h * head : 2 * CD + (h + 1) * head, lanes]
-            parts.append(dot_nn(v, probs[:, h * GROUP : (h + 1) * GROUP]).astype(jnp.bfloat16))
-        mixed.append(jnp.concatenate(parts, axis=0))
-    mixed = jnp.concatenate(mixed, axis=1)
-    keep_mixed[...] = mixed
-    first = embedded + dot_nn(out_ref[...], mixed)
-    keep_first[...] = first
-    act_two = (column_rms(first)[0] * g2_ref[...]).astype(jnp.bfloat16)
-    branch = None
-    for c in range(CFF // CD):
-        rows = slice(c * CD, (c + 1) * CD)
-        hidden, slope = gelu_pair(dot_nn(up_ref[rows, :], act_two))
-        hidden = hidden.astype(jnp.bfloat16)
-        keep_hidden[rows, :] = hidden
-        keep_slope[rows, :] = slope.astype(jnp.bfloat16)
-        part = dot_nn(down_ref[:, rows], hidden)
-        branch = part if branch is None else branch + part
-    high, low = split_two(first + branch)
-    pooled_ref[...] += dot_nt(word_map, high) + dot_nt(word_map, low)
+    packs = [pack_ref[0, k, pl.ds(step * per, per), :] for k in range(4)]
+
+    def chain(part):
+        groups = per // CHAINS
+        cols = slice(part * groups * GROUP, (part + 1) * groups * GROUP)
+        size = groups * GROUP
+        ids, spots, low_rows, high_rows = (p[part * groups : (part + 1) * groups] for p in packs)
+        embedded = dot_nn(table_ref[...], lane_map(ids, CV))
+        yield
+        act_one = (column_rms(embedded)[0] * lane_copies(g1_ref, size)).astype(jnp.bfloat16)
+        triple = dot_tn(in_ref[:, : 3 * CD], act_one).astype(jnp.bfloat16)
+        keep_qkv[:, cols] = triple
+        yield
+        key_rows = triple[CD : 2 * CD].T
+        keep_values[cols, :] = triple[2 * CD :].T
+        all_probs = []
+        for g in range(groups):
+            valid = (key_pos >= low_rows[g : g + 1]) & (key_pos < high_rows[g : g + 1])
+            valid = jnp.concatenate([valid.astype(jnp.float32)] * CHEADS, axis=1) > 0
+            lanes = slice(g * GROUP, (g + 1) * GROUP)
+            scores = to_compact(dot_nn(key_rows[lanes], spread_heads(triple[:CD, lanes])), own)
+            scores = jnp.where(valid, scores * head**-0.5, NEG_FILL)
+            powers = jnp.exp(scores - jnp.max(scores, axis=0, keepdims=True))
+            powers = jnp.where(valid, powers, 0.0)
+            total = jnp.sum(powers, axis=0, keepdims=True)
+            probs = powers / jnp.where(total > 0, total, 1.0)
+            wide = (part * groups + g) * CHEADS * GROUP
+            keep_probs[:, wide : wide + CHEADS * GROUP] = probs
+            all_probs.append(from_compact(probs, own))
+        yield
+        mixed = []
+        for g in range(groups):
+            lanes = slice(g * GROUP, (g + 1) * GROUP)
+            heads = []
+            for h in range(CHEADS):
+                v = triple[2 * CD + h * head : 2 * CD + (h + 1) * head, lanes]
+                probs = all_probs[g][:, h * GROUP : (h + 1) * GROUP]
+                heads.append(dot_nn(v, probs).astype(jnp.bfloat16))
+            mixed.append(jnp.concatenate(heads, axis=0))
+        mixed = jnp.concatenate(mixed, axis=1)
+        keep_mixed[:, cols] = mixed
+        yield
+        first = embedded + dot_tn(in_ref[:, 3 * CD : 4 * CD], mixed)
+        keep_first[:, cols] = first
+        act_two = (column_rms(first)[0] * lane_copies(g2_ref, size)).astype(jnp.bfloat16)
+        second = first
+        for c in range(CFF // CD):
+            yield
+            rows = slice(c * CD, (c + 1) * CD)
+            up = in_ref[:, 4 * CD + c * CD : 4 * CD + (c + 1) * CD]
+            hidden, slope = gelu_pair(dot_tn(up, act_two))
+            hidden = hidden.astype(jnp.bfloat16)
+            keep_hidden[rows, cols] = hidden
+            keep_slope[rows, cols] = slope.astype(jnp.bfloat16)
+            second = second + dot_nn(down_ref[:, rows], hidden)
+        yield
+        return lane_map(spots, words), split_two(second)
+
+    ends = in_step([chain(part) for part in range(CHAINS)])
+    word_map = jnp.concatenate([end[0] for end in ends], axis=1)
+    high = jnp.concatenate([end[1][0] for end in ends], axis=1)
+    low = jnp.concatenate([end[1][1] for end in ends], axis=1)
+    pooled_ref[0] += dot_nt(word_map, high) + dot_nt(word_map, low)
 
 
 KEPT = (
@@ -257,11 +292,12 @@
 )
 
 
-def kept_specs():
+def kept_specs(seqs, count):
+    place = placed(seqs, lambda seq, tile, _: (0, seq * count + tile))
     return [
-        pl.BlockSpec((ROWS, CD), lambda t, n: (kept_place(t, n)[1], 0)),
-        pl.BlockSpec((SLOTS, CHEADS * ROWS), kept_place),
-    ] + [pl.BlockSpec((depth, ROWS), kept_place) for depth, _ in KEPT]
+        pl.BlockSpec((ROWS, CD), lambda *at: place(*at)[::-1]),
+        pl.BlockSpec((SLOTS, CHEADS * ROWS), place),
+    ] + [pl.BlockSpec((depth, ROWS), place) for depth, _ in KEPT]
 
 
 def kept_shapes(rows):
@@ -276,26 +312,31 @@
     return pl.BlockSpec(array.shape, lambda *_: zeros)
 
 
-def kept_place(step, tiles):
-    return 0, jnp.minimum(step, tiles[0] - 1)
-
-
-def char_fwd(tiles, pack, weights, words):
-    rows = words * SLOTS
-    operands = (pack,) + weights
+def char_specs(seqs, pack, others):
+    one = (1,) + pack.shape[1:]
+    return [
+        pl.BlockSpec(one, placed(seqs, lambda seq, tile, _: (seq, 0, 0, 0))),
+        pl.BlockSpec((CD, CV), placed(seqs, lambda seq, tile, language: (0, language[seq]))),
+    ] + [whole(a) for a in others]
+
+
+def char_fwd(tiles, language, pack, table, others, words):
+    seqs = pack.shape[0]
+    count = tile_count(words)
+    one = placed(seqs, lambda seq, tile, _: (seq, 0, 0))
     return pl.pallas_call(
-        char_fwd_kernel,
+        functools.partial(char_fwd_kernel, seqs),
         grid_spec=pltpu.PrefetchScalarGridSpec(
-            num_scalar_prefetch=1,
-            grid=(rows // ROWS,),
-            in_specs=[whole(a) for a in operands],
-            out_specs=[pl.BlockSpec((words, CD), lambda t, n: (0, 0))]
-            + kept_specs(),
+            num_scalar_prefetch=2,
+            grid=(seqs * count,),
+            in_specs=char_specs(seqs, pack, others),
+            out_specs=[pl.BlockSpec((1, words, CD), one)] + kept_specs(seqs, count),
         ),
-        out_shape=[jax.ShapeDtypeStruct((words, CD), jnp.float32)] + kept_shapes(rows),
+        out_shape=[jax.ShapeDtypeStruct((seqs, words, CD), jnp.float32)]
+        + kept_shapes(seqs * count * ROWS),
         compiler_params=pltpu.CompilerParams(vmem_limit_bytes=VMEM_BYTES),
         name="char_fwd",
-    )(tiles, *operands)
+    )(tiles, language, pack, table, *others)
 
 
 def fold_lanes(values):
@@ -310,119 +351,159 @@
     return inverse * (scaled - normed * jnp.mean(scaled * normed, axis=0, keepdims=True))
 
 
-def char_bwd_kernel(tiles_ref, *refs):
-    @pl.when(pl.program_id(0) < tiles_ref[0])
+def char_bwd_kernel(seqs, tiles_ref, language_ref, *refs):
+    step = pl.program_id(0)
+    seq, tile, total = tile_at(step, tiles_ref, seqs)
+
+    @pl.when(step < total)
     def _():
-        char_bwd_tile(tiles_ref[0] - 1, *refs)
+        char_bwd_tile(tile, step == 0, step == total - 1, language_ref[seq] * CV, *refs)
 
 
 def char_bwd_tile(
-    last, pack_ref, spread_ref, table_ref, qkv_ref, out_ref, up_ref, down_ref, g1_ref, g2_ref,
+    step, at_start, at_end, letter, pack_ref, table_ref, in_ref, down_ref, g1_ref, g2_ref, spread_ref,
     keep_values, keep_probs, keep_qkv, keep_mixed, keep_first, keep_hidden, keep_slope,
     *refs,
 ):
-    sums = 7
-    earlier, results, totals = (), refs[-2 * sums : -sums], refs[-sums:]
-    if len(refs) == 3 * sums - 1:
-        earlier = refs[: sums - 1]
+    results, totals = refs[:7], refs[7:]
     d_table, d_qkv, d_out, d_up, d_down, d_g1, d_g2 = totals
-    step = pl.program_id(0)
-    words = spread_ref.shape[1]
+    words = spread_ref.shape[2]
     per = ROWS // GROUP
     head = CD // CHEADS
 
-    @pl.when(step == 0)
+    @pl.when(at_start)
     def _():
-        d_table[...] = jnp.zeros_like(d_table)
-        for i, ref in enumerate(totals[1:]):
-            ref[...] = earlier[i][...] if earlier else jnp.zeros_like(ref)
-
-    one_hot, word_map = tile_maps(pack_ref, step, words)
-    halves = dot_nn(spread_ref[...], word_map)
-    grad_second = halves[:CD] + halves[CD:]
-    grad_branch = grad_second.astype(jnp.bfloat16)
-    first = keep_first[...]
-    normed_two, inverse_two = column_rms(first)
-    act_two = (normed_two * g2_ref[...]).astype(jnp.bfloat16)
-    grad_act_two = None
-    for c in range(CFF // CD):
-        rows = slice(c * CD, (c + 1) * CD)
-        d_down[rows, :] += dot_nt(keep_hidden[rows, :], grad_branch)
-        grad_upper = dot_nn(down_ref[rows, :], grad_branch) * keep_slope[rows, :].astype(
-            jnp.float32
+        for ref in totals:
+            ref[...] = jnp.zeros_like(ref)
+
+    own = own_block()
+    packs = [pack_ref[0, k, pl.ds(step * per, per), :] for k in range(2)]
+
+    def chain(part):
+        groups = per // CHAINS
+        cols = slice(part * groups * GROUP, (part + 1) * groups * GROUP)
+        size = groups * GROUP
+        ids, spots = (p[part * groups : (part + 1) * groups] for p in packs)
+        halves = dot_nn(spread_ref[0], lane_map(spots, words))
+        grad_second = halves[:CD] + halves[CD:]
+        grad_branch = grad_second.astype(jnp.bfloat16)
+        normed_two, inverse_two = column_rms(keep_first[:, cols])
+        gain_two = lane_copies(g2_ref, size)
+        act_two = (normed_two * gain_two).astype(jnp.bfloat16)
+        grad_uppers = []
+        grad_act_two = None
+        for c in range(CFF // CD):
+            yield
+            rows = slice(c * CD, (c + 1) * CD)
+            slope = keep_slope[rows, cols].astype(jnp.float32)
+            grad_upper = dot_tn(down_ref[:, rows], grad_branch) * slope
+            grad_upper = grad_upper.astype(jnp.bfloat16)
+            grad_uppers.append(grad_upper)
+            piece = dot_nn(in_ref[:, 4 * CD + c * CD : 4 * CD + (c + 1) * CD], grad_upper)
+            grad_act_two = piece if grad_act_two is None else grad_act_two + piece
+        yield
+        gain_sum_two = fold_lanes(grad_act_two * normed_two)
+        grad_first = grad_second + column_rms_back(
+            grad_act_two, gain_two, normed_two, inverse_two
         )
-        grad_upper = grad_upper.astype(jnp.bfloat16)
-        d_up[:, rows] += dot_nt(act_two, grad_upper)
-        part = dot_nn(up_ref[:, rows], grad_upper)
-        grad_act_two = part if grad_act_two is None else grad_act_two + part
-    d_g2[...] += fold_lanes(grad_act_two * normed_two)
-    grad_first = grad_second + column_rms_back(
-        grad_act_two, g2_ref[...], normed_two, inverse_two
+        grad_attn = grad_first.astype(jnp.bfloat16)
+        grad_mixed = dot_nn(in_ref[:, 3 * CD : 4 * CD], grad_attn).astype(jnp.bfloat16)
+        yield
+        triple = keep_qkv[:, cols]
+        raws, lows = [], []
+        for g in range(groups):
+            lanes = slice(g * GROUP, (g + 1) * GROUP)
+            at = part * groups + g
+            wide = slice(at * CHEADS * GROUP, (at + 1) * CHEADS * GROUP)
+            probs = keep_probs[:, wide]
+            values = keep_values[at * GROUP : (at + 1) * GROUP, :]
+            grad_probs = to_compact(dot_nn(values, spread_heads(grad_mixed[:, lanes])), own)
+            grad_scores = probs * (
+                grad_probs - jnp.sum(probs * grad_probs, axis=0, keepdims=True)
+            )
+            raws.append(from_compact(grad_scores * head**-0.5, own))
+            lows.append(from_compact(probs, own))
+        yield
+        columns = []
+        for g in range(groups):
+            lanes = slice(g * GROUP, (g + 1) * GROUP)
+            gq, gk, gv = [], [], []
+            for h in range(CHEADS):
+                q = triple[h * head : (h + 1) * head, lanes]
+                k = triple[CD + h * head : CD + (h + 1) * head, lanes]
+                grad_o = grad_mixed[h * head : (h + 1) * head, lanes]
+                piece = slice(h * GROUP, (h + 1) * GROUP)
+                gq.append(dot_nn(k, raws[g][:, piece]).astype(jnp.bfloat16))
+                gk.append(dot_nt(q, raws[g][:, piece]).astype(jnp.bfloat16))
+                gv.append(dot_nt(grad_o, lows[g][:, piece]).astype(jnp.bfloat16))
+            columns.append(jnp.concatenate(gq + gk + gv, axis=0))
+        grad_triple = jnp.concatenate(columns, axis=1)
+        yield
+        one_hot = lane_map(ids, CV)
+        embedded = dot_nn(table_ref[...], one_hot)
+        normed_one, inverse_one = column_rms(embedded)
+        gain_one = lane_copies(g1_ref, size)
+        act_one = (normed_one * gain_one).astype(jnp.bfloat16)
+        grad_act_one = dot_nn(in_ref[:, : 3 * CD], grad_triple)
+        yield
+        gain_sum_one = fold_lanes(grad_act_one * normed_one)
+        back_one = column_rms_back(grad_act_one, gain_one, normed_one, inverse_one)
+        grad_embedded = (grad_first + back_one).astype(jnp.bfloat16)
+        grad_upper = jnp.concatenate(grad_uppers, axis=0)
+        return (
+            gain_sum_one, gain_sum_two, grad_branch, act_two, grad_upper, grad_attn,
+            act_one, grad_triple, one_hot, grad_embedded,
+        )
+
+    ends = in_step([chain(part) for part in range(CHAINS)])
+    for end in ends:
+        d_g1[...] += end[0]
+        d_g2[...] += end[1]
+    grad_branch, act_two, grad_upper, grad_attn, act_one, grad_triple, one_hot, grad_embedded = (
+        jnp.concatenate(parts, axis=1) for parts in list(zip(*ends))[2:]
     )
-    grad_attn = grad_first.astype(jnp.bfloat16)
+    d_down[...] += dot_nt(keep_hidden[...], grad_branch)
+    d_up[...] += dot_nt(act_two, grad_upper)
     d_out[...] += dot_nt(keep_mixed[...], grad_attn)
-    grad_mixed = dot_nn(out_ref[...], grad_attn).astype(jnp.bfloat16)
-    own = own_block()
-    triple = keep_qkv[...]
-    columns = []
-    for g in range(per):
-        lanes = slice(g * GROUP, (g + 1) * GROUP)
-        wide = slice(g * CHEADS * GROUP, (g + 1) * CHEADS * GROUP)
-        probs = keep_probs[:, wide]
-        grad_probs = to_compact(
-            dot_nn(keep_values[lanes, :], spread_heads(grad_mixed[:, lanes])), own
-        )
-        grad_scores = probs * (
-            grad_probs - jnp.sum(probs * grad_probs, axis=0, keepdims=True)
-        )
-        grad_raw = from_compact(grad_scores * head**-0.5, own)
-        probs = from_compact(probs, own)
-        gq, gk, gv = [], [], []
-        for h in range(CHEADS):
-            q = triple[h * head : (h + 1) * head, lanes]
-            k = triple[CD + h * head : CD + (h + 1) * head, lanes]
-            grad_o = grad_mixed[h * head : (h + 1) * head, lanes]
-            part = slice(h * GROUP, (h + 1) * GROUP)
-            gq.append(dot_nn(k, grad_raw[:, part]).astype(jnp.bfloat16))
-            gk.append(dot_nt(q, grad_raw[:, part]).astype(jnp.bfloat16))
-            gv.append(dot_nt(grad_o, probs[:, part]).astype(jnp.bfloat16))
-        columns.append(jnp.concatenate(gq + gk + gv, axis=0))
-    grad_triple = jnp.concatenate(columns, axis=1)
-    embedded = dot_nn(table_ref[...], one_hot)
-    normed_one, inverse_one = column_rms(embedded)
-    act_one = (normed_one * g1_ref[...]).astype(jnp.bfloat16)
     d_qkv[...] += dot_nt(act_one, grad_triple)
-    grad_act_one = dot_nn(qkv_ref[...], grad_triple)
-    d_g1[...] += fold_lanes(grad_act_one * normed_one)
-    back_one = column_rms_back(grad_act_one, g1_ref[...], normed_one, inverse_one)
-    grad_embedded = (grad_first + back_one).astype(jnp.bfloat16)
-    d_table[...] += dot_nt(one_hot, grad_embedded)
-
-    @pl.when(step == last)
+    d_table[pl.ds(pl.multiple_of(letter, CV), CV), :] += dot_nt(one_hot, grad_embedded)
+
+    @pl.when(at_end)
     def _():
         for ref, total in zip(results, totals):
             ref[...] = total[...].astype(ref.dtype)
 
 
-def char_bwd(tiles, pack, spread, weights, kept, earlier):
-    operands = (pack, spread) + weights
-    shapes = ((CV, CD), (CD, 3 * CD), (CD, CD), (CD, CFF), (CFF, CD), (CD, GROUP), (CD, GROUP))
+def char_bwd(tiles, language, pack, table, others, spread, kept):
+    shapes = (
+        table.shape[::-1],
+        (CD, 3 * CD),
+        (CD, CD),
+        (CD, CFF),
+        (CFF, CD),
+        (CD, GROUP),
+        (CD, GROUP),
+    )
     f32, bf16 = jnp.float32, jnp.bfloat16
-    kinds = [f32] * 7 if earlier is None else [f32] + [bf16] * 4 + [f32] * 2
-    earlier = () if earlier is None else tuple(earlier)
+    kinds = [bf16] * 5 + [f32] * 2
+    seqs = pack.shape[0]
+    count = tile_count(spread.shape[2])
+    one = (1,) + spread.shape[1:]
     return pl.pallas_call(
-        char_bwd_kernel,
+        functools.partial(char_bwd_kernel, seqs),
         grid_spec=pltpu.PrefetchScalarGridSpec(
-            num_scalar_prefetch=1,
-            grid=(kept[0].shape[0] // ROWS,),
-            in_specs=[whole(a) for a in operands] + kept_specs() + [whole(a) for a in earlier],
-            out_specs=[pl.BlockSpec(s, lambda t, n: (0, 0)) for s in shapes],
+            num_scalar_prefetch=2,
+            grid=(seqs * count,),
+            in_specs=char_specs(seqs, pack, others)
+            + [pl.BlockSpec(one, placed(seqs, lambda seq, tile, _: (seq, 0, 0)))]
+            + kept_specs(seqs, count),
+            out_specs=[pl.BlockSpec(s, lambda *_: (0, 0)) for s in shapes],
             scratch_shapes=[pltpu.VMEM(s, f32) for s in shapes],
         ),
         out_shape=[jax.ShapeDtypeStruct(s, kind) for s, kind in zip(shapes, kinds)],
         compiler_params=pltpu.CompilerParams(vmem_limit_bytes=VMEM_BYTES),
         name="char_bwd",
-    )(tiles, *operands, *kept, *earlier)
+    )(tiles, language, pack, table, *others, spread, *kept)
 
 
 def adam_step(weight, grad, first_old, second_old, clip_factor, rate, decay):
@@ -582,7 +663,7 @@
 
 
 def word_fwd_kernel(dp, ranks, *refs):
-    (sum_ref, count_ref, words_ref, pool_ref, early_ref, g3_ref, up_rows, down_rows) = refs[:8]
+    (sum_ref, count_ref, words_ref, in_ref, early_ref, g3_ref, up_rows, down_rows) = refs[:8]
     (start_ref, pooled_ref, triple_in, lse_ref, mixed_in, up_ref, down_ref) = refs[8:15]
     triple_ref, mixed_ref, own_sem, late_sem, pair_sem, triple_sem, mixed_sem = refs[15:]
     ring = Ring(dp, ranks)
@@ -604,11 +685,12 @@
     part = D // ranks
     moving = []
     for s in range(seqs):
-        pooled = (sum_ref[s] / count_ref[s]).T.astype(jnp.bfloat16)
+        count = count_ref[s : s + 1, :].astype(jnp.float32)
+        pooled = (sum_ref[s].T / count).astype(jnp.bfloat16)
         pooled_ref[s] = pooled
-        start = words_ref[s].astype(jnp.float32).T + dot_tn(pool_ref[...], pooled)
+        start = words_ref[s].astype(jnp.float32).T + dot_tn(in_ref[:, 4 * CD + CFF :], pooled)
         start_ref[s] = start
-        act = (column_rms(start)[0] * g3_ref[...]).astype(jnp.bfloat16)
+        act = (column_rms(start)[0] * lane_copies(g3_ref, start.shape[1])).astype(jnp.bfloat16)
         for t in range(3):
             triple = dot_tn(early_ref[:, t * D : (t + 1) * D], act).astype(jnp.bfloat16)
             for r in range(ranks):
@@ -633,7 +715,7 @@
         wait_all(copies)
 
 
-def word_fwd(sums, counts, words, pool, early, g3, up_rows, down_rows, collective):
+def word_fwd(sums, counts, words, char_in, early, g3, up_rows, down_rows, collective):
     dp, ranks = lax.axis_size("dp"), lax.axis_size("head")
     seqs, width, _ = words.shape
     part = D // ranks
@@ -670,12 +752,12 @@
             collective_id=collective, has_side_effects=True, vmem_limit_bytes=VMEM_BYTES
         ),
         name="word_fwd",
-    )(sums, counts, words, pool, early, g3, up_rows, down_rows)
+    )(sums, counts, words, char_in, early, g3, up_rows, down_rows)
 
 
 def word_bwd_kernel(dp, ranks, *refs):
     (start_ref, pooled_ref, triple_in, lse_ref, mixed_in, cot_ref, count_ref) = refs[:7]
-    (pool_ref, early_ref, up_ref, down_ref, g3_ref, g4_ref) = refs[7:13]
+    (in_ref, early_ref, up_ref, down_ref, g3_ref, g4_ref) = refs[7:13]
     (output_ref, input_grad_ref, spread_ref, d_qkv, d_pool, d_g3, d_g4) = refs[13:20]
     sums = refs[20:23]
     (acts, hiddens, grad_ups, cots, lows, mixes, triples) = refs[23:30]
@@ -715,13 +797,14 @@
 
     moving = []
     gain = None
+    g3, g4 = lane_copies(g3_ref, width), lane_copies(g4_ref, width)
     for s in range(seqs):
         lanes = slice(s * width, (s + 1) * width)
         mixed = mixed_in[s].reshape(D, width)
         mixes[:, lanes] = mixed
         after = start_ref[s] + dot_tn(early_ref[:, 3 * D :], mixed)
         normed, inverse = column_rms(after)
-        act = (normed * g4_ref[...]).astype(bf16)
+        act = (normed * g4).astype(bf16)
         acts[:, lanes] = act
         cot = cot_ref[s].astype(f32).T
         cot_low = cot.astype(bf16)
@@ -740,7 +823,7 @@
         output_ref[s] = result.T.astype(bf16)
         piece = fold_lanes(grad * normed)
         gain = piece if gain is None else gain + piece
-        total = cot + column_rms_back(grad, g4_ref[...], normed, inverse)
+        total = cot + column_rms_back(grad, g4, normed, inverse)
         afters[s] = total
         low = total.astype(bf16)
         lows[:, lanes] = low
@@ -769,15 +852,16 @@
                     s, r, t * part : (t + 1) * part, :
                 ]
         normed, inverse = column_rms(start_ref[s])
-        acts[:, lanes] = (normed * g3_ref[...]).astype(bf16)
+        acts[:, lanes] = (normed * g3).astype(bf16)
         grad = dot_nn(early_ref[:, : 3 * D], triples[:, lanes])
         piece = fold_lanes(grad * normed)
         gain = piece if gain is None else gain + piece
-        total = afters[s] + column_rms_back(grad, g3_ref[...], normed, inverse)
+        total = afters[s] + column_rms_back(grad, g3, normed, inverse)
         input_grad_ref[s] = total.T
         low = total.astype(bf16)
         lows[:, lanes] = low
-        high, rest = split_two(dot_nn(pool_ref[...], low) / count_ref[s])
+        count = count_ref[s : s + 1, :].astype(f32)
+        high, rest = split_two(dot_nn(in_ref[:, 4 * CD + CFF :], low) / count)
         spread_ref[s, :CD, :] = high
         spread_ref[s, CD:, :] = rest
     d_g3[...] = gain
@@ -796,7 +880,7 @@
 def word_bwd(saved, cot, counts, weights, gains, collective):
     dp, ranks = lax.axis_size("dp"), lax.axis_size("head")
     start, pooled, triple, lse, mixed = saved
-    pool, early, up, down = weights
+    char_in, early, up, down = weights
     seqs, _, width = start.shape
     hidden = up.shape[1]
     chips = dp // 2
@@ -805,7 +889,7 @@
     rows = ((hidden // dp, D), (D // dp, hidden), (D // dp, D))
     columns = seqs * width
     dma = pltpu.SemaphoreType.DMA
-    operands = (*saved, cot, counts, pool, early, up, down, *gains)
+    operands = (*saved, cot, counts, char_in, early, up, down, *gains)
     shapes = [
         ((seqs, width, D), bf16),
         ((seqs, width, D), f32),
@@ -851,9 +935,27 @@
     )(*operands)
 
 
+def block_of(ref, d, h, shard):
+    if len(ref.shape) == 4:
+        return ref.at[d, h]
+    rows, cols = shard.shape
+    return ref.at[
+        pl.ds(pl.multiple_of(h * rows, rows), rows), pl.ds(pl.multiple_of(d * cols, cols), cols)
+    ]
+
+
+def rows_of(ref, d, shard):
+    if len(ref.shape) > 2:
+        return ref.at[d]
+    cols = shard.shape[1]
+    return ref.at[:, pl.ds(pl.multiple_of(d * cols, cols), cols)]
+
+
 def gather_kernel(dp, ranks, *refs):
-    shards, outs, low = refs[:5], refs[5:11], refs[11:16]
-    own_sem, line_sem, plane_sem, pair_sem, copy_sem = refs[16:]
+    shards, (counts_ref, ids_ref, gains_ref) = refs[:5], refs[5:8]
+    outs, (pack_ref, tiles_ref), gain_refs = refs[8:14], refs[14:16], refs[16:20]
+    low = refs[20:25]
+    own_sem, line_sem, plane_sem, pair_sem, copy_sem = refs[25:]
     table, char_in, down, early, word_rows, down_rows = outs
     ring = Ring(dp, ranks)
     for shard, ref in zip(shards, low):
@@ -865,9 +967,9 @@
         return ref.at[:, pl.ds(pl.multiple_of(ring.h * wide, GROUP), wide)]
 
     places = (
-        table.at[ring.d, ring.h],
+        block_of(table, ring.d, ring.h, low[0]),
         column(char_in.at[ring.d], low[1]),
-        down.at[ring.d, ring.h],
+        block_of(down, ring.d, ring.h, low[2]),
         column(word_rows, low[3]),
         column(down_rows, low[4]),
     )
@@ -889,7 +991,7 @@
     second, sent = [], []
 
     def onward(m, block):
-        place = blocks[m].at[ring.d]
+        place = rows_of(blocks[m], ring.d, low[m])
         second.append(
             [send(block, place, plane_sem, (m, k), ring.plane(k)) for k in range(1, ring.chips)]
         )
@@ -897,9 +999,17 @@
 
     for m in range(3):
         along_line(m)
+    for seq in range(ids_ref.shape[0]):
+        pack_words(counts_ref[seq : seq + 1, :], ids_ref[seq], pack_ref, tiles_ref, seq)
+    row = 0
+    for ref in gain_refs:
+        for at in range(0, ref.shape[0], GROUP):
+            gain = jnp.broadcast_to(gains_ref[row : row + 1, :], (GROUP, GROUP))
+            ref[at : at + GROUP, :] = gain.T
+            row += 1
     for m in range(3):
         arrived(m)
-        onward(m, blocks[m].at[ring.d])
+        onward(m, rows_of(blocks[m], ring.d, low[m]))
     along_line(3)
     along_line(4)
     arrived(3)
@@ -910,7 +1020,8 @@
     for m in range(4):
         for k in range(1, ring.chips):
             second[m][k - 1].wait_recv()
-            block = blocks[m].at[2 * ring.chip_at(ring.chips - k) + ring.core]
+            place = 2 * ring.chip_at(ring.chips - k) + ring.core
+            block = rows_of(blocks[m], place, low[m])
             sent.append(send(block, block, pair_sem, (m, k), ring.sibling()))
     arrived(4)
     copy.wait()
@@ -923,26 +1034,38 @@
             copy.wait_send()
 
 
-def gather(shards, collective):
+def gather(shards, counts, ids, gains, collective):
     dp, ranks = lax.axis_size("dp"), lax.axis_size("head")
     bf16 = jnp.bfloat16
     vmem = pl.BlockSpec(memory_space=pltpu.VMEM)
     anywhere = pl.BlockSpec(memory_space=pl.ANY)
     table, char_in, down, word_in, word_down = (s.shape for s in shards)
     dma = pltpu.SemaphoreType.DMA
+
+    def narrow(shape):
+        if shape[1] % GROUP == 0:
+            return (ranks * shape[0], dp * shape[1])
+        return (dp, ranks) + shape
+
+    seqs, slots, words = ids.shape
     outs = [
-        (dp, ranks) + table,
+        narrow(table),
         (dp, char_in[0], ranks * char_in[1]),
-        (dp, ranks) + down,
+        narrow(down),
         (dp, word_in[0], 4 * D),
         (word_in[0], ranks * word_in[1]),
         (word_down[0], ranks * word_down[1]),
     ]
     return pl.pallas_call(
         functools.partial(gather_kernel, dp, ranks),
-        in_specs=[vmem] * 5,
-        out_specs=[anywhere] * 6,
-        out_shape=[jax.ShapeDtypeStruct(s, bf16) for s in outs],
+        in_specs=[vmem] * 8,
+        out_specs=[anywhere] * 6 + [vmem, pl.BlockSpec(memory_space=pltpu.SMEM)] + [vmem] * 4,
+        out_shape=[jax.ShapeDtypeStruct(s, bf16) for s in outs]
+        + [
+            jax.ShapeDtypeStruct((seqs, 4, tile_count(words) * (ROWS // GROUP), GROUP), jnp.int32),
+            jax.ShapeDtypeStruct((seqs,), jnp.int32),
+        ]
+        + [jax.ShapeDtypeStruct((n, GROUP), jnp.float32) for n in (CD, CD, D, D)],
         scratch_shapes=[pltpu.VMEM(s.shape, bf16) for s in shards]
         + [
             dma((5,)),
@@ -955,7 +1078,7 @@
             collective_id=collective, has_side_effects=True, vmem_limit_bytes=VMEM_BYTES
         ),
         name="gather",
-    )(*shards)
+    )(*shards, counts, ids, gains)
 
 
 def column_cuts(widths, ranks):
@@ -977,9 +1100,9 @@
     pieces = sum(len(g) - done for g, done in groups)
     mats = len(groups)
     parts = refs[:pieces]
-    gain_ref = refs[pieces]
-    ready = refs[pieces + 1 : pieces + 1 + extra]
-    place = pieces + 1 + extra
+    gain_refs = refs[pieces : pieces + 4]
+    ready = refs[pieces + 4 : pieces + 4 + extra]
+    place = pieces + 4 + extra
     outs = refs[place : place + mats]
     gain_out, square_out = refs[place + mats : place + mats + 2]
     place += mats + 2
@@ -1023,11 +1146,56 @@
             value = shared(slot, share(slot, value, stage), stage)
         return value
 
+    def line_copy(m, k):
+        return pltpu.make_async_remote_copy(
+            src_ref=line_sum[m].at[ring.rank_at(k)],
+            dst_ref=line_in[m].at[k],
+            send_sem=line_sem.at[0, m, k],
+            recv_sem=line_sem.at[1, m, k],
+            device_id=ring.line(k),
+            device_id_type=pl.DeviceIdType.MESH,
+        )
+
+    def put_columns(m, cuts, total):
+        for rank, first, last, inside in cuts:
+            line_sum[m][rank, :, inside : inside + last - first] = total[:, first:last]
+
+    def early_rank(m):
+        widths, done = groups[m]
+        own = sum(widths[: len(widths) - done])
+        ready_from = sum(
+            w for at, w in enumerate(widths) if at < len(widths) - done
+        ) if done else sum(widths)
+        block = sum(widths) // ranks
+        return -(-max(own, ready_from) // block)
+
+    def begin(copy, now, first):
+        if first == 0:
+            copy.start()
+        elif first < ranks:
+            pl.when(now)(copy.start)
+
     pairs = [
         send(parts[i].at[:, 1 - ring.core], pair_in[i], pair_sem, (i,), ring.sibling())
         for i in range(pieces)
     ]
-    gain = shared(0, share(0, gain_ref[...], 0), 0)
+    starts = []
+    j = 0
+    for m, (widths, done) in enumerate(groups):
+        lines = [line_copy(m, k) for k in range(1, ranks)]
+        starts.append(lines)
+        cuts = column_cuts(widths, ranks)
+        for at in range(len(widths) - done, len(widths)):
+            put_columns(m, cuts[at], ready[j][...])
+            j += 1
+        for k in range(1, ranks):
+            begin(lines[k - 1], early_rank(m) <= ring.rank_at(k), early_rank(m))
+    rows = []
+    for ref in gain_refs:
+        for at in range(0, ref.shape[0], GROUP):
+            rows.append(jnp.sum(ref[at : at + GROUP, :].T, axis=0, keepdims=True))
+    rows.append(jnp.zeros((small.shape[3] - len(rows), GROUP), f32))
+    gain = shared(0, share(0, jnp.concatenate(rows, axis=0), 0), 0)
     planes = []
     for i in range(pieces):
         pairs[i].wait()
@@ -1051,30 +1219,22 @@
             ]
         )
     gain = shared(0, share(0, gain, 1), 1)
-    gain_out[...] = shared(0, share(0, gain, 2), 2)
-    lines, i, j = [], 0, 0
+    gain_out[...] = shared(0, share(0, gain, 2), 2)[: gain_out.shape[0]]
+    i = 0
     for m, (widths, done) in enumerate(groups):
-        for at, cuts in enumerate(column_cuts(widths, ranks)):
-            if at < len(widths) - done:
-                total = pair_sum[i][ring.chip].astype(f32)
-                for k in range(1, chips):
-                    planes[i][k - 1].wait()
-                    total = total + plane_in[i][k].astype(f32)
-                total = total.astype(bf16)
-                i += 1
-            else:
-                total = ready[j][...]
-                j += 1
-            for rank, first, last, inside in cuts:
-                line_sum[m][rank, :, inside : inside + last - first] = total[:, first:last]
-        lines.append(
-            [
-                send(
-                    line_sum[m].at[ring.rank_at(k)], line_in[m].at[k], line_sem, (m, k), ring.line(k)
-                )
-                for k in range(1, ranks)
-            ]
-        )
+        for cuts in column_cuts(widths, ranks)[: len(widths) - done]:
+            total = pair_sum[i][ring.chip].astype(f32)
+            for k in range(1, chips):
+                planes[i][k - 1].wait()
+                total = total + plane_in[i][k].astype(f32)
+            put_columns(m, cuts, total.astype(bf16))
+            i += 1
+        first = early_rank(m)
+        for k in range(1, ranks):
+            if first >= ranks:
+                starts[m][k - 1].start()
+            elif first > 0:
+                pl.when(ring.rank_at(k) < first)(starts[m][k - 1].start)
     square = jnp.zeros(square_out.shape, f32)
 
     def squares(value):
@@ -1087,9 +1247,9 @@
     for m in range(mats):
         total = line_sum[m][ring.h].astype(f32)
         for k in range(1, ranks):
-            lines[m][k - 1].wait()
+            starts[m][k - 1].wait()
             total = total + line_in[m][k].astype(f32)
-        outs[m][...] = total
+        outs[m][...] = total if outs[m].shape == total.shape else total.T
         square = square + squares(total)
     small_square = jnp.concatenate([square, jnp.zeros_like(square)], axis=0)
     square_out[...] = total_of(1, small_square)[:8]
@@ -1109,16 +1269,17 @@
     blocks = [p.shape[2:] for p in pieces]
     vmem = pl.BlockSpec(memory_space=pltpu.VMEM)
     n, mats = len(pieces), len(groups)
+    gain_rows = sum(g.shape[0] for g in gains) // GROUP
     return pl.pallas_call(
         functools.partial(reduce_kernel, dp, ranks, widths, len(ready)),
-        in_specs=[vmem] * (n + 1 + len(ready)),
+        in_specs=[vmem] * (n + 4 + len(ready)),
         out_specs=[vmem] * (mats + 2),
-        out_shape=[jax.ShapeDtypeStruct(s, f32) for s in shards]
-        + [jax.ShapeDtypeStruct(gains.shape, f32), jax.ShapeDtypeStruct((8, GROUP), f32)],
+        out_shape=[jax.ShapeDtypeStruct(s if s[1] % GROUP == 0 else s[::-1], f32) for s in shards]
+        + [jax.ShapeDtypeStruct((gain_rows, GROUP), f32), jax.ShapeDtypeStruct((8, GROUP), f32)],
         scratch_shapes=[pltpu.VMEM((chips,) + b, bf16) for b in blocks] * 3
         + [pltpu.VMEM((ranks,) + s, bf16) for s in shards] * 2
         + [
-            pltpu.VMEM((2, 3, max(2, chips, ranks)) + gains.shape, f32),
+            pltpu.VMEM((2, 3, max(2, chips, ranks), 16, GROUP), f32),
             pltpu.SemaphoreType.DMA((2, n)),
             pltpu.SemaphoreType.DMA((2, n, chips)),
             pltpu.SemaphoreType.DMA((2, mats, ranks)),
@@ -1128,7 +1289,7 @@
             collective_id=collective, has_side_effects=True, vmem_limit_bytes=VMEM_BYTES
         ),
         name="reduce_grads",
-    )(*pieces, gains, *ready)
+    )(*pieces, *gains, *ready)
 
 
 def update_kernel(count, *refs):
@@ -1195,54 +1356,30 @@
     old_gains_first,
     old_gains_second,
 ):
-    bf16, f32 = jnp.bfloat16, jnp.float32
-    packed, tiles = pack_rows(char_ids, char_counts)
-    table_t_low, char_in_low, char_down_t, early, up_rows, down_rows = gather(
-        (char_table.T, char_in, char_down.T, word_in, word_down), 0
+    narrow = (norm_gains.shape[0] // GROUP, GROUP)
+    table_t, char_in_low, char_down_t, early, up_rows, down_rows, packed, tiles, *gains = gather(
+        (char_table.T, char_in, char_down.T, word_in, word_down),
+        char_counts,
+        char_ids.transpose(0, 2, 1),
+        norm_gains.reshape(narrow),
+        0,
     )
 
     def joined(block):
+        if block.ndim == 2:
+            return block
         dp, ranks, cols, rows = block.shape
         return block.transpose(1, 2, 0, 3).reshape(ranks * cols, dp * rows)
 
     def stacked(block):
         return block.reshape(-1, block.shape[2])
 
-    table_t_low, char_down_t = joined(table_t_low), joined(char_down_t)
+    table_t = joined(table_t)
     char_in_low, early = stacked(char_in_low), stacked(early)
-    seq_count, local_words = (words_in.shape[0], words_in.shape[1])
-    languages = table_t_low.shape[1] // CV
-
-    def lanes(gain, width):
-        return jnp.broadcast_to(gain[:, None], (gain.shape[0], width))
-
-    gains = (lanes(norm_gains[:CD], ROWS), lanes(norm_gains[CD : 2 * CD], ROWS))
-    g3 = lanes(norm_gains[2 * CD : 2 * CD + D], local_words)
-    g4 = lanes(norm_gains[2 * CD + D :], local_words)
-    table_t = [
-        lax.dynamic_slice_in_dim(table_t_low, language[i] * CV, CV, axis=1)
-        for i in range(seq_count)
-    ]
-    char_parts = (
-        char_in_low[:, : 3 * CD],
-        char_in_low[:, 3 * CD : 4 * CD],
-        char_in_low[:, 4 * CD : 4 * CD + CFF],
-        char_down_t.T,
-    )
-    flipped = tuple(part.T for part in char_parts[:3]) + (char_down_t,)
-    pool = char_in_low[:, 4 * CD + CFF :]
-    count_row = char_counts.astype(f32)[:, None, :]
-    count_col = char_counts.astype(f32)[:, :, None]
-    seqs = range(seq_count)
-    kept, sums = [], []
-    for i in seqs:
-        total, *saved = char_fwd(
-            tiles[i : i + 1], packed[i], (table_t[i],) + flipped + gains, local_words
-        )
-        kept.append(saved)
-        sums.append(total)
+    char_others = (char_in_low, joined(char_down_t), gains[0], gains[1])
+    sums, *kept = char_fwd(tiles, language, packed, table_t, char_others, words_in.shape[1])
     *saved, up, down = word_fwd(
-        jnp.stack(sums), count_col, words_in, pool, early, g3, up_rows, down_rows, 1
+        sums, char_counts, words_in, char_in_low, early, gains[2], up_rows, down_rows, 1
     )
     (
         output,
@@ -1258,55 +1395,35 @@
     ) = word_bwd(
         tuple(saved),
         out_cotangent,
-        count_row,
-        (pool, early, stacked(up), stacked(down)),
-        (g3, g4),
+        char_counts,
+        (char_in_low, early, stacked(up), stacked(down)),
+        gains[2:],
         2,
     )
-    last, tables_out = None, []
-    for i in seqs:
-        one_table, *last = char_bwd(
-            tiles[i : i + 1],
-            packed[i],
-            spread[i],
-            (table_t[i],) + char_parts + gains,
-            kept[i],
-            last,
-        )
-        tables_out.append(one_table)
-    grad_table = sum(
-        jnp.where(
-            (jnp.arange(languages) == language[i])[:, None, None], tables_out[i][None], 0.0
-        )
-        for i in seqs
-    ).reshape(-1, CD)
-    c_qkv, c_out, c_up, c_down, gain_one, gain_two = last
-    gain_grads = jnp.concatenate(
-        [jnp.sum(g, axis=1) for g in (gain_one, gain_two, gain_three, gain_four)]
+    grad_table, c_qkv, c_out, c_up, c_down, gain_one, gain_two = char_bwd(
+        tiles, language, packed, table_t, char_others, spread, kept
     )
-    flat = (gain_grads.shape[0] // GROUP, GROUP)
-    rest = 16 - flat[0]
     *shards, gains_sum, square = reduce_grads(
         [
-            ([grad_table.astype(bf16)], []),
-            ([c_qkv.astype(bf16), c_out.astype(bf16), c_up.astype(bf16), grad_pool], []),
-            ([c_down.astype(bf16)], []),
+            ([grad_table], []),
+            ([c_qkv, c_out, c_up, grad_pool], []),
+            ([c_down], []),
             ([grad_qkv], [out_sum, up_sum]),
             ([], [down_sum]),
         ],
-        jnp.pad(gain_grads.reshape(flat), ((0, rest), (0, 0))),
+        (gain_one, gain_two, gain_three, gain_four),
         3,
     )
 
     def turned(parts):
         parts = list(parts)
         parts[0], parts[2] = parts[0].T, parts[2].T
-        parts[5] = parts[5].reshape(flat)
+        parts[5] = parts[5].reshape(narrow)
         return parts
 
     norm, *updated = update(
         turned((char_table, char_in, char_down, word_in, word_down, norm_gains)),
-        turned((*shards, gains_sum[: flat[0]])),
+        (*shards, gains_sum),
         turned(
             (
                 old_table_first,

time: 410 us -> 325 us (0.79)
  Pallas kernels: 366 us -> 322 us
  local copies, waits for them, and re-layouts: 27.2 us -> 1.77 us
  other arithmetic: 9.98 us -> 0 us
    pallas_call x5 -> x2, Pallas kernels: 126 us -> 86.7 us  [the longest x1 48 us: char_bwd(): pl.pallas_call(functools.partial(char_bwd_kernel, seqs), grid_spec=pltpu....]
    slice x7 -> x0, local copies, waits for them, and re-layouts: 6.55 us -> none  [the longest x1 1.31 us: body(): tiles[i:i + 1]]
    broadcast_in_dim x6 -> x0, local copies, waits for them, and re-layouts: 5.18 us -> none  [the longest x4 3.74 us: lanes(): return jnp.broadcast_to(gain[:, None], (gain.shape[0], width))]
    transpose x5 -> x0, local copies, waits for them, and re-layouts: 4.58 us -> none  [the longest x3 2.71 us: body(): flipped = tuple((part.T for part in char_parts[:3])) + (char_down_t,)]
    reduce_sum x4 -> x0, other arithmetic: 4.22 us -> none  [body(): jnp.sum(g, axis=1)]
where the time goes in v4:
time: 325 us
  Pallas kernels  322 us (99%)
    pallas_call x1, Pallas kernels, reduce_grads(): pl.pallas_call(functools.partial(reduce_kernel, dp, ranks, widths, len(re...  70.8 us
    pallas_call x1, Pallas kernels, word_fwd(): pl.pallas_call(functools.partial(word_fwd_kernel, dp, ranks), in_specs=[v...  63.8 us
    pallas_call x1, Pallas kernels, word_bwd(): pl.pallas_call(functools.partial(word_bwd_kernel, dp, ranks), in_specs=[v...  58.2 us
    pallas_call x1, Pallas kernels, char_bwd(): pl.pallas_call(functools.partial(char_bwd_kernel, seqs), grid_spec=pltpu....  48 us
    pallas_call x1, Pallas kernels, gather(): pl.pallas_call(functools.partial(gather_kernel, dp, ranks), in_specs=[vme...  39.4 us
    pallas_call x1, Pallas kernels, char_fwd(): pl.pallas_call(functools.partial(char_fwd_kernel, seqs), grid_spec=pltpu....  38.6 us

profile of v4, /device:TPU:0, one launch (start us, length us, event | category | flops | bytes accessed | tf_op | source)
XLA Modules:
  0.0 324.9 jit_solution(12044342395249529453)
XLA Ops:
  0.7 39.4 %gather.1 = (bf16[256,1024]{1,0:T(8,128)(2,1)}, bf16[8,32,2560]{2,1,0:T(8,128)(2,1)}, bf16[256,1024]{1,0:T(8,128)(2,1)}, bf16[8,64,2048]{2,1,0:T(8,128)(2,1)}, b...) custom-call(f32[64,128]{1,0:T(8,128)} %bitcast.52, ...), custom_call_target="tpu_custom_call" | custom-call | tf_op jit(solution)/shard_map/gather/pallas_call | solution.py:1059
  40.1 38.6 %char_fwd.1 = (f32[2,256,256]{2,1,0:T(8,128)}, bf16[8192,256]{1,0:T(8,128)(2,1)}, f32[16,32768]{1,0:T(8,128)}, bf16[768,8192]{1,0:T(8,128)(2,1)}, bf16[256,8192]...) custom-call(s32[2]{0:T(128)} %get-tuple-element.115.tiles_ref, ...), custom_call_target="tpu_custom_call" | custom-call | tf_op jit(solution)/shard_map/char_fwd/pallas_call | solution.py:327
  78.7 63.8 %word_fwd.1 = (f32[2,512,256]{2,1,0:T(8,128)}, bf16[2,256,256]{2,1,0:T(8,128)(2,1)}, bf16[2,4,384,256]{3,2,1,0:T(8,128)(2,1)}, f32[2,2,4,8,256]{4,3,2,1,0:T(8,12...) custom-call(f32[2,256,256]{2,1,0:T(8,128)} %get-tuple-element.122.refs_0_, ...), custom_call_target="tpu_custom_call" | custom-call | tf_op jit(solution)/shard_map/word_fwd/pallas_call | solution.py:729
  142.5 58.2 %word_bwd.1 = (bf16[2,256,512]{2,1,0:T(8,128)(2,1)}, f32[2,256,512]{2,1,0:T(8,128)}, bf16[2,512,256]{2,1,0:T(8,128)(2,1)}, bf16[512,1536]{1,0:T(8,128)(2,1)}, bf...) custom-call(f32[2,512,256]{2,1,0:T(8,128)} %get-tuple-element.127.re, ...), custom_call_target="tpu_custom_call" | custom-call | tf_op jit(solution)/shard_map/word_bwd/pallas_call | solution.py:902
  200.7 48.0 %char_bwd.1 = (bf16[1024,256]{1,0:T(8,128)(2,1)}, bf16[256,768]{1,0:T(8,128)(2,1)}, bf16[256,256]{1,0:T(8,128)(2,1)}, bf16[256,1024]{1,0:T(8,128)(2,1)}, bf16[10...) custom-call(s32[2]{0:T(128)} %get-tuple-element.115.tiles_ref, s32[2]{0:T(128)} %language_ref.3, ...), custom_call_target="tpu_custom_call" | custom-call | tf_op jit(solution)/shard_map/char_bwd/pallas_call | solution.py:492
  248.8 70.8 %reduce_grads.1 = (f32[64,128]{1,0:T(8,128)}, f32[32,640]{1,0:T(8,128)}, f32[64,128]{1,0:T(8,128)}, f32[64,1024]{1,0:T(8,128)}, f32[256,128]{1,0:T(8,128)}, /*index=5*/f32[12,128]{1,0:T(8,128)}, f32[8,128]{1,0:T(8,128)}) custom-call(bf16[4,2,128,256]{3,2,1,0:T(8,128)(2,1)} %bitcast.47, bf16[4,2,32,768]{3,2,1,0:T(8,128)(2,1)} %bitcast.50, ...), custom_call_target="tpu_custom_call" | custom-call | tf_op jit(solution)/shard_map/reduce_grads/pallas_call | solution.py:1273
  319.6 0.0 copy-start.1
  319.6 0.0 copy-start
  319.6 3.5 %update.1 = (f32[1,128]{1,0:T(1,128)}, f32[64,128]{1,0:T(8,128)}, f32[64,128]{1,0:T(8,128)}, f32[64,128]{1,0:T(8,128)}, f32[64,128]{1,0:T(8,128)}, /*index=5*/bf...) custom-call(f32[64,128]{1,0:T(8,128)} %bitcast.53, ...), custom_call_target="tpu_custom_call" | custom-call | tf_op jit(solution)/shard_map/update/pallas_call | solution.py:1326
  323.1 0.0 copy-done.1
  323.1 0.8 copy.58
  323.9 0.0 copy-done
  323.9 1.0 copy.59
Async XLA Ops:
  319.6 3.5 %copy-start.1 = (bf16[2,256,512]{2,1,0:T(8,128)(2,1)S(1)}, bf16[2,256,512]{2,1,0:T(8,128)(2,1)}, u32[]{:S(2)}) copy-start(bf16[2,256,512]{2,1,0:T(8,128)(2,1)} %get-tuple-element.230) | copy-start | bytes 1572868
  319.6 4.3 %copy-start = (f32[2,256,512]{2,1,0:T(8,128)S(1)}, f32[2,256,512]{2,1,0:T(8,128)}, u32[]{:S(2)}) copy-start(f32[2,256,512]{2,1,0:T(8,128)} %get-tuple-element.231) | copy-start | bytes 3145732
